TPU v7x, 32 devices: a whole 2x2x4 slice. The times are simulated.
32 devices in a mesh: tile: 8 (over y, x, core), sample: 4 (over z).
Axes of the slice: x: 2, y: 2, z: 4, core: 2. Of those that a mesh axis runs over, the one named last changes fastest.
Arguments:
- features: bfloat16 [8, 9, 224, 10752], P('sample', None, 'tile'), may hold values from -6 to 6
- norm_gain: float32 [96], replicated, may hold values from 0.4 to 2.5
- conv_weight: bfloat16 [3, 3, 3, 3, 96], replicated, may hold values from -0.125 to 0.125
- patch_embed: bfloat16 [588, 1280], P(None, 'tile'), may hold values from -0.25 to 0.25
- position: bfloat16 [128, 1280], P('sample', 'tile'), may hold values from -6 to 6
- attend_in: bfloat16 [1280, 1920], P('sample', 'tile'), may hold values from -0.15625 to 0.15625
- attend_out: bfloat16 [640, 1280], P('sample', 'tile'), may hold values from -0.25 to 0.25
- reward_head: float32 [1280], replicated, may hold values from -0.24 to 0.24
- group_index: int32 [8], P('sample'), may hold values from 0 to 1, as said below
- frame_pick: int32 [8, 8], P('sample'), may hold values from 0 to 8, as said below
Outputs:
- feature_grad: bfloat16 [8, 9, 224, 10752], P('sample', None, 'tile')
Inputs may be any that keep to these rules, and one draw needn't show every extreme that they name: `group_index`: each prompt number is the prompt of exactly 4 samples. `frame_pick`: the 8 frames of one sample are all different.
All inputs are finite; a program needn't handle non-finite values.
Results may differ from a plain program's by a relative error of at most 0.02.
Values may be sent and summed in bfloat16 or wider, within the bound.
No kernel may reach another device: no remote copies, remote signals or barrier semaphores. Data moves between devices by JAX's collectives and lax.ppermute only.
A program may use at most 192 MiB of HBM per device.

v0:
```python
import jax
import jax.numpy as jnp
from jax import lax
from jax.sharding import PartitionSpec as P

SCORED = 8
PATCH = 14
HEADS = 8
HD = 80
GROUP = 4


LOSS_SCALE = 16384.0
SMOOTH = 0.01


def padded_2(block, sides, width):
    for axis, dim in sides:
        count = lax.axis_size(axis)
        forward = [(i, i + 1) for i in range(count - 1)]
        backward = [(target, source) for source, target in forward]
        low = lax.ppermute(
            lax.slice_in_dim(block, block.shape[dim] - width, None, axis=dim), axis, forward
        )
        high = lax.ppermute(lax.slice_in_dim(block, 0, width, axis=dim), axis, backward)
        block = jnp.concatenate([low, block, high], axis=dim)
    return block


def normed_silu(inputs, norm_gain):
    second = jnp.mean(inputs * inputs, axis=-4, keepdims=True)
    scaled = inputs * lax.rsqrt(second + 1e-06) * norm_gain[:, None, None, None]
    return jax.nn.silu(scaled)


def conv_rows(padded, tap_weights, frame_count, row_count, column_count):
    sample_count = padded.shape[0]
    spread = jnp.einsum(
        "koc,sctrw->skotrw", tap_weights, padded, preferred_element_type=jnp.float32
    )
    summed = jnp.zeros((sample_count, 3, frame_count, row_count, column_count), jnp.float32)
    for step_time in range(3):
        for step_row in range(3):
            for step_column in range(3):
                tap_index = step_time * 9 + step_row * 3 + step_column
                summed = (
                    summed
                    + spread[
                        :,
                        tap_index,
                        :,
                        step_time : step_time + frame_count,
                        step_row : step_row + row_count,
                        step_column : step_column + column_count,
                    ]
                )
    return summed


def frame_score(frame_one, patch_embed, position, attend_in, attend_out, reward_head):
    row_count = frame_one.shape[1] // PATCH
    column_count = frame_one.shape[2] // PATCH
    patches = (
        frame_one.reshape(3, row_count, PATCH, column_count, PATCH)
        .transpose(1, 3, 0, 2, 4)
        .reshape(row_count * column_count, 3 * PATCH * PATCH)
    )
    tokens = jnp.dot(patches, patch_embed, preferred_element_type=jnp.float32) + position.astype(
        jnp.float32
    )
    centered = tokens - jnp.mean(tokens, axis=-1, keepdims=True)
    normed = (
        centered * lax.rsqrt(jnp.mean(centered * centered, axis=-1, keepdims=True) + 1e-05)
    ).astype(jnp.bfloat16)
    mixed_rows = jnp.dot(normed, attend_in, preferred_element_type=jnp.float32).astype(jnp.bfloat16)
    inner_width = HEADS * HD
    query_rows = mixed_rows[:, :inner_width].reshape(-1, HEADS, HD)
    key_rows = mixed_rows[:, inner_width : 2 * inner_width].reshape(-1, HEADS, HD)
    values = mixed_rows[:, 2 * inner_width :].reshape(-1, HEADS, HD)
    scores = jnp.einsum(
        "qhd,khd->hqk", query_rows, key_rows, preferred_element_type=jnp.float32
    ) * HD ** (-0.5)
    weights = jax.nn.softmax(scores, axis=-1).astype(jnp.bfloat16)
    attended = jnp.einsum("hqk,khd->qhd", weights, values, preferred_element_type=jnp.float32)
    attended = attended.reshape(-1, inner_width).astype(jnp.bfloat16)
    residual = tokens + jnp.dot(attended, attend_out, preferred_element_type=jnp.float32)
    pooled = jnp.mean(residual, axis=0)
    pooled_centered = pooled - jnp.mean(pooled)
    pooled_normed = pooled_centered * lax.rsqrt(jnp.mean(pooled_centered * pooled_centered) + 1e-05)
    return jnp.sum(pooled_normed * reward_head)


def local(
    features,
    norm_gain,
    conv_weight,
    patch_embed,
    position,
    attend_in,
    attend_out,
    reward_head,
    group_index,
    frame_pick,
):
    row_parts = (
        lax.all_gather(position, "sample", axis=0, tiled=True),
        lax.all_gather(attend_in, "sample", axis=0, tiled=True),
        lax.all_gather(attend_out, "sample", axis=0, tiled=True),
    )
    position_full, in_full, out_full, embed_full = (
        lax.all_gather(row_parts[0], "tile", axis=1, tiled=True),
        lax.all_gather(row_parts[1], "tile", axis=1, tiled=True),
        lax.all_gather(row_parts[2], "tile", axis=1, tiled=True),
        lax.all_gather(patch_embed, "tile", axis=1, tiled=True),
    )
    sample_count, frame_count, row_count, merged = features.shape
    channels = norm_gain.shape[0]
    column_count = merged // channels
    owners = lax.axis_size("tile")
    layered = features.reshape(
        sample_count, frame_count, row_count, channels, column_count
    ).transpose(0, 3, 1, 2, 4)
    inputs = layered.astype(jnp.float32)
    activation = normed_silu(inputs, norm_gain).astype(jnp.bfloat16)
    tap_weights = conv_weight.reshape(27, 3, channels)
    rimmed = padded_2(activation, (("tile", 3),), 1)
    padded = jnp.pad(rimmed, ((0, 0), (0, 0), (2, 0), (0, 0), (1, 1)))
    summed = conv_rows(padded, tap_weights, frame_count, row_count, column_count)
    decoded = summed.astype(jnp.bfloat16)
    entry_range = jnp.arange(owners, dtype=jnp.int32)
    pick_padded = jnp.concatenate(
        [frame_pick, jnp.zeros((sample_count, owners - SCORED), jnp.int32)], axis=1
    )
    entry_live = entry_range < SCORED
    picked = jax.vmap(lambda clip_one, pick_one: jnp.take(clip_one, pick_one, axis=1))(
        decoded, pick_padded
    )
    picked = picked * entry_live.astype(jnp.bfloat16)[None, None, :, None, None]
    owned = lax.all_to_all(picked, "tile", split_axis=2, concat_axis=3, tiled=True)
    owned_frames = owned[:, :, 0]
    owner_live = (lax.axis_index("tile") < SCORED).astype(jnp.float32)

    def score_all(frames_in):
        return jax.vmap(
            lambda frame_one: frame_score(
                frame_one, embed_full, position_full, in_full, out_full, reward_head
            )
        )(frames_in)

    raw_scores, pull_scores = jax.vjp(score_all, owned_frames)
    scores = raw_scores * owner_live
    prompts = sample_count * lax.axis_size("sample") // GROUP
    prompt_range = jnp.arange(prompts, dtype=jnp.int32)
    member = (group_index[:, None] == prompt_range[None, :]).astype(jnp.float32)
    score_total = lax.psum(scores, "tile")
    rewards = score_total / SCORED
    group_sum, group_square = lax.psum(
        (
            jnp.sum(member * rewards[:, None], axis=0),
            jnp.sum(member * (rewards * rewards)[:, None], axis=0),
        ),
        "sample",
    )
    mean_group = group_sum / GROUP
    second_group = group_square / GROUP - mean_group * mean_group
    sample_mean = jnp.sum(member * mean_group[None, :], axis=1)
    sample_second = jnp.sum(member * second_group[None, :], axis=1)
    advantage = (rewards - sample_mean) * lax.rsqrt(sample_second + SMOOTH)
    cotangent = -LOSS_SCALE * advantage / SCORED * owner_live
    pixel_grad = pull_scores(cotangent)[0]
    returned = lax.all_to_all(
        pixel_grad[:, :, None], "tile", split_axis=3, concat_axis=2, tiled=True
    )
    chosen = (
        (pick_padded[:, :, None] == jnp.arange(frame_count, dtype=jnp.int32)[None, None, :])
        & entry_live[None, :, None]
    ).astype(jnp.bfloat16)
    frame_grad = jnp.einsum(
        "sjf,scjrw->scfrw", chosen, returned, preferred_element_type=jnp.float32
    ).astype(jnp.bfloat16)
    grad_rimmed = padded_2(frame_grad, (("tile", 3),), 1)
    grad_pad = jnp.pad(grad_rimmed, ((0, 0), (0, 0), (0, 2), (0, 0), (1, 1)))
    pieces = []
    for step_time in range(3):
        for step_row in range(3):
            for step_column in range(3):
                pieces.append(
                    grad_pad[
                        :,
                        :,
                        2 - step_time : 2 - step_time + frame_count,
                        2 - step_row : 2 - step_row + row_count,
                        2 - step_column : 2 - step_column + column_count,
                    ]
                )
    stacked = jnp.stack(pieces, axis=1)
    activation_grad = jnp.einsum(
        "koc,skotrw->sctrw", tap_weights, stacked, preferred_element_type=jnp.float32
    )
    unused, pull_norm = jax.vjp(lambda values_in: normed_silu(values_in, norm_gain), inputs)
    result = pull_norm(activation_grad)[0].astype(jnp.bfloat16)
    return result.transpose(0, 2, 3, 1, 4).reshape(sample_count, frame_count, row_count, merged)


def solution(mesh):
    in_specs = (
        P("sample", None, "tile", None),
        P(),
        P(),
        P(None, "tile"),
        P("sample", "tile"),
        P("sample", "tile"),
        P("sample", "tile"),
        P(),
        P("sample"),
        P("sample", None),
    )
    out_specs = P("sample", None, "tile", None)
    return jax.shard_map(local, mesh=mesh, in_specs=in_specs, out_specs=out_specs, check_vma=False)
```

profile of v0, /device:TPU:0, one launch (start us, length us, event | category | flops | bytes accessed | tf_op | source)
XLA Modules:
  0.0 480.3 jit_solution(15964166979684310372)
XLA Ops:
  7.3 19.8 %all_gather.24 = bf16[1280,240]{1,0:T(8,128)(2,1)S(1)} all-gather(bf16[320,240]{1,0:T(8,128)(2,1)} %param.15), channel_id=1, replica_groups=mesh['tile'=8,'sample'=4] {'sample'}, dimensions={0}, use_global_device_ids=true | all-gather | bytes 768000 | tf_op jit(solution)/shard_map/all_gather | solution.py:107
  28.3 28.0 %reshape.158 = f32[2,9,28,96,112]{4,3,0,2,1:T(8,128)} reshape(bf16[2,9,28,10752]{3,0,2,1:T(2,128)(2,1)} %param.10) | data formatting | bytes 32514048 | tf_op jit(solution)/shard_map/convert_element_type | solution.py:123
  56.2 12.6 %fusion.16 = f32[2,9,28,112]{3,2,1,0:T(8,128)S(1)} fusion(f32[2,9,28,96,112]{4,3,0,2,1:T(8,128)} %reshape.158), kind=kLoop, calls=%fused_computation.29 | loop fusion | flops 10781568 | bytes 21901824 | tf_op jit(solution)/shard_map/reduce_sum | solution.py:31
  69.6 2.8 copy-done.1
  72.5 7.2 %fusion.23 = bf16[2,96,9,28,112]{4,1,3,2,0:T(8,128)(2,1)S(1)} fusion(f32[2,9,28,96,112]{4,3,0,2,1:T(8,128)S(1)} %copy-done.1, f32[96]{0:T(128)S(1)} %copy-done.13, f32[2,9,28,112]{3,2,1,0:T(8,128)S(1)} %fusion.139), kind=kLoop, calls=%fused_computation.36 | loop fusion | flops 37933056 | bytes 32740224 | tf_op jit(solution)/shard_map/convert_element_type | solution.py:124
  79.7 4.4 copy-done.2
  84.1 1.3 collective-permute-start
  85.5 1.3 collective-permute-start.1
  86.8 14.9 %all_gather.26 = bf16[640,160]{1,0:T(8,128)(2,1)S(1)} all-gather(bf16[160,160]{1,0:T(8,128)(2,1)S(1)} %copy-done.9), channel_id=1, replica_groups=mesh['tile'=8,'sample'=4] {'sample'}, dimensions={0}, use_global_device_ids=true | all-gather | bytes 256000 | tf_op jit(solution)/shard_map/all_gather | solution.py:108
  102.7 20.2 %fusion.41 = f32[2,27,3,11,30,114]{5,1,2,4,3,0:T(8,128)} fusion(bf16[2,96,9,1,112]{4,1,3,2,0:T(8,128)(2,1)S(1)} %collective-permute-done.1, bf16[2,96,9,28,112]{4,1,3,2,0:T(8,128)(2,1)} %copy-done.2, bf16[2,96,9,1,112]{4,1,3,2,0:T(8,128)(2,1)S(1)} %collective-permute-done, bf16[27,3,96,1,1,1]{2,1,0,5,4,3:T(4,128)(2,1)S(1)} %bitcast.272), kind=kOutput, calls=%fused_computation.50 | convolution fusion | flops 1292924160 | bytes 36005472 | tf_op jit(solution)/shard_map/koc,sctrw->skotrw/dot_general | solution.py:38
  123.0 22.7 %fusion.163 = (f32[2,1,3,9,28,112]{5,1,2,4,3,0:T(1,128)}, f32[2,1,3,9,28,112]{5,1,2,4,3,0:T(1,128)}, f32[2,1,3,9,28,112]{5,1,2,4,3,0:T(1,128)}, f32[2,1,3,9,28,1...) fusion(f32[2,27,3,11,30,114]{5,1,2,4,3,0:T(8,128)} %fusion.41), kind=kLoop, calls=%fused_computation.271 | loop fusion | bytes 10838016 | tf_op jit(solution)/shard_map/slice | solution.py:48
  145.7 48.2 %slice_add_fusion = (f32[2,1,3,9,28,112]{5,1,2,4,3,0:T(1,128)}, f32[2,1,3,9,28,112]{5,1,2,4,3,0:T(1,128)}, f32[2,1,3,9,28,112]{5,1,2,4,3,0:T(1,128)}) fusion(f32[2,27,3,11,30,114]{5,1,2,4,3,0:T(8,128)} %fusion.41), kind=kLoop, calls=%fused_computation.119 | loop fusion | flops 2709504 | bytes 14902272 | tf_op jit(solution)/shard_map/add | solution.py:47
  193.9 1.5 copy.984
  195.5 2.2 copy_bitcast_fusion.8
  197.6 2.2 copy_bitcast_fusion.4
  201.4 2.2 copy_bitcast_fusion.5
  204.9 1.2 fusion.136
  206.1 6.3 %all-to-all-start = ((bf16[2,3,8,28,112]{4,0,3,1,2:T(2,128)(2,1)}), bf16[2,3,8,28,112]{4,0,3,1,2:T(2,128)(2,1)S(1)}, u32[]{:S(2)}, u32[]{:S(2)}) async-start(bf16[2,3,8,28,112]{4,0,3,1,2:T(2,128)(2,1)} %fusion.136), calls=%async_computation | async-start | bytes 688128 | tf_op jit(solution)/shard_map/all_to_all | solution.py:139
  212.4 13.1 %all_gather.22 = bf16[128,160]{1,0:T(8,128)(2,1)S(1)} all-gather(bf16[32,160]{1,0:T(8,128)(2,1)S(1)} %copy-done.11), channel_id=1, replica_groups=mesh['tile'=8,'sample'=4] {'sample'}, dimensions={0}, use_global_device_ids=true | all-gather | bytes 51200 | tf_op jit(solution)/shard_map/all_gather | solution.py:106
  225.7 10.5 %all_gather.23 = bf16[128,1280]{0,1:T(8,128)(2,1)S(1)} all-gather(bf16[128,160]{0,1:T(8,128)(2,1)S(1)} %copy.879), channel_id=1, replica_groups=mesh['tile'=8,'sample'=4] {'tile'}, dimensions={1}, use_global_device_ids=true | all-gather | bytes 368640 | tf_op jit(solution)/shard_map/all_gather | solution.py:111
  237.4 2.8 reshape_squeeze.3
  240.2 2.6 copy.877
  242.8 3.4 reshape.144
  246.2 2.5 fusion.167
  249.0 4.0 fusion.51
  254.6 1.6 fusion.168
  257.3 2.3 fusion.75
  260.2 13.2 %psum.21 = f32[2]{0:T(128)S(1)} all-reduce(f32[2]{0:T(128)S(1)} %broadcast_multiply_fusion.3), channel_id=1, replica_groups=mesh['tile'=8,'sample'=4] {'tile'}, use_global_device_ids=true, to_apply=%region_9.10 | all-reduce | flops 2 | bytes 16 | tf_op jit(solution)/shard_map/psum | solution.py:155
  273.5 11.6 %all-reduce.5 = (f32[2]{0:T(128)S(1)}, f32[2]{0:T(128)S(1)}) all-reduce(f32[2]{0:T(128)S(1)} %get-tuple-element.7, f32[2]{0:T(128)S(1)} %get-tuple-element.8), channel_id=1, replica_groups=mesh['tile'=8,'sample'=4] {'sample'}, use_global_device_ids=true, to_apply=%region_11.12 | all-reduce | flops 4 | bytes 32 | tf_op jit(solution)/shard_map/psum | solution.py:157
  285.8 2.9 fusion.78
  288.6 1.9 copy.888
  290.5 2.6 convolution_convert_fusion.4
  293.0 1.8 fusion.90
  294.9 2.5 convolution_convert_fusion.3
  297.4 2.4 convolution_convert_fusion.2
  299.8 1.9 copy.890
  301.6 1.9 copy.892
  303.5 1.9 copy.894
  305.4 4.3 multiply_reduce_fusion
  310.2 1.8 fusion.81
  312.0 1.9 copy.895
  313.9 4.5 reshape.152
  318.4 2.2 copy.918
  320.6 4.9 %reshape.188 = bf16[2,3,1,224,112]{4,0,2,1,3:T(2,128)(2,1)} reshape(bf16[2,3,16,14,8,14]{5,4,0,1,3,2:T(8,128)(2,1)} %copy.918) | data formatting | bytes 602112 | tf_op jit(solution)/shard_map/broadcast_in_dim;transpose(jvp(vmap()))/reshape | solution.py:172
  325.5 3.4 all-to-all-start.1
  329.0 7.7 %all-to-all-done.1 = bf16[2,3,1,224,112]{4,0,2,1,3:T(2,128)(2,1)S(1)} async-done(((bf16[2,3,1,224,112]{4,0,2,1,3:T(2,128)(2,1)}), bf16[2,3,1,224,112]{4,0,2,1,3:T(2,128)(2,1)S(1)}, u32[]{:S(2)}, u32[]{:S(2)}) %all-to-all-start.1) | async-done | bytes 301088 | tf_op jit(solution)/shard_map/all_to_all | solution.py:171
  337.2 1.3 collective-permute-start.2
  338.5 1.5 collective-permute-start.3
  340.0 2.4 collective-permute-done.3
  344.0 1.2 fusion.128
  346.4 1.2 fusion.126
  347.6 1.3 fusion.125
  350.0 1.2 fusion.123
  351.2 1.2 fusion.122
  353.6 1.2 fusion.120
  354.9 1.2 fusion.119
  357.3 1.2 fusion.117
  358.5 1.3 fusion.116
  360.9 1.2 fusion.114
  362.2 1.3 fusion.113
  373.9 29.5 %fusion.14 = (f32[2,9,28,112]{3,2,1,0:T(8,128)S(1)}, f32[2,9,28,112,96,1]{3,4,5,2,1,0:T(8,128)}) fusion(f32[2,9,28,96,112]{4,3,0,2,1:T(8,128)} %reshape.158, f32[96]{0:T(128)S(1)} %copy-done.13, f32[2,9,28,112]{3,2,1,0:T(8,128)S(1)} %fusion.139, bf16[27,3,96,1,1,1]{2,1,0,5,4,3:T(4,128)(2,1)S(1)} %bitcast.273, bf16[2,27,3,9,28,112]{5,3,4,2,0,1:T(8,128)(2,1)} %fusion.102), kind=kOutput, calls=%fused_computation.21 | convolution fusion | flops 953688960 | bytes 52964160 | tf_op jit(solution)/shard_map/koc,skotrw->sctrw/dot_general | solution.py:197
  403.5 24.9 %fusion.15 = bf16[2,9,28,96,112]{4,3,2,1,0:T(8,128)(2,1)} fusion(f32[2,9,28,112,96,1]{3,4,5,2,1,0:T(8,128)} %get-tuple-element.46, f32[2,9,28,96,112]{4,3,0,2,1:T(8,128)} %reshape.158, f32[2,9,28,112]{3,2,1,0:T(8,128)S(1)} %multiply_multiply_fusion, f32[96]{0:T(128)S(1)} %copy-done.13, f32[2,9,28,112]{3,2,1,0:T(8,128)S(1)} %fusion.139), kind=kLoop, calls=%fused_computation.22 | loop fusion | flops 92123136 | bytes 54642048 | tf_op jit(solution)/shard_map/convert_element_type | solution.py:201
  428.4 25.7 %reshape.189 = bf16[2,9,28,10752]{3,2,1,0:T(8,128)(2,1)} reshape(bf16[2,9,28,96,112]{4,3,2,1,0:T(8,128)(2,1)} %fusion.15) | data formatting | bytes 21676032 | tf_op jit(solution)/shard_map/reshape | solution.py:202
  454.1 19.4 %copy.923 = bf16[2,9,28,10752]{3,0,2,1:T(2,128)(2,1)} copy(bf16[2,9,28,10752]{3,2,1,0:T(8,128)(2,1)} %reshape.189) | data formatting | bytes 21676032 | tf_op jit(solution)/shard_map/reshape | solution.py:202
  (107 shorter events, 31.2 us)
Async XLA Ops:
  6.5 96.2 %copy-start = (bf16[3,3,3,3,96]{4,3,2,1,0:T(4,128)(2,1)S(1)}, bf16[3,3,3,3,96]{4,3,2,1,0:T(4,128)(2,1)}, u32[]{:S(2)}) copy-start(bf16[3,3,3,3,96]{4,3,2,1,0:T(4,128)(2,1)} %param.12) | copy-start | bytes 46660
  6.5 239.7 %all-gather.4.cloned.1.call-start = ((), (), s32[]{:S(2)}) async-start(), calls=%async_computation.2 | async-start | bytes 1843200 | tf_op jit(solution)/shard_map/all_gather | solution.py:114
  7.3 241.8 %all-gather.6.cloned.1.call-start = ((), (), s32[]{:S(2)}) async-start(), calls=%async_computation.3 | async-start | bytes 5529600 | tf_op jit(solution)/shard_map/all_gather | solution.py:112
  28.2 229.1 %all-gather.8.cloned.1.call-start = ((), (), s32[]{:S(2)}) async-start(), calls=%async_computation.4 | async-start | bytes 1843200 | tf_op jit(solution)/shard_map/all_gather | solution.py:113
  56.2 16.2 %copy-start.1 = (f32[2,9,28,96,112]{4,3,0,2,1:T(8,128)S(1)}, f32[2,9,28,96,112]{4,3,0,2,1:T(8,128)}, u32[]{:S(2)}) copy-start(f32[2,9,28,96,112]{4,3,0,2,1:T(8,128)} %reshape.158) | copy-start | bytes 65028100
  56.2 16.2 %copy-start.13 = (f32[96]{0:T(128)S(1)}, f32[96]{0:T(128)}, u32[]{:S(2)}) copy-start(f32[96]{0:T(128)} %param.11) | copy-start | bytes 1156
  68.9 0.7 copy-start.3
  72.5 14.3 %copy-start.9 = (bf16[160,160]{1,0:T(8,128)(2,1)S(1)}, bf16[160,160]{1,0:T(8,128)(2,1)}, u32[]{:S(2)}) copy-start(bf16[160,160]{1,0:T(8,128)(2,1)} %param.16) | copy-start | bytes 153604
  72.5 30.0 %copy-start.12 = (s32[2,8]{1,0:T(2,128)S(1)}, s32[2,8]{1,0:T(2,128)}, u32[]{:S(2)}) copy-start(s32[2,8]{1,0:T(2,128)} %param.19) | copy-start | bytes 196
  79.7 4.4 copy-start.2
  84.1 18.6 %collective-permute-start = (bf16[2,96,9,1,112]{4,1,3,2,0:T(8,128)(2,1)S(1)}, bf16[2,96,9,1,112]{4,1,3,2,0:T(8,128)(2,1)S(1)}, u32[]{:S(2)}, u32[]{:S(2)}) collective-permute-start(bf16[2,96,9,1,112]{4,1,3,2,0:T(8,128)(2,1)S(1)} %get-tuple-element.26), channel_id=1, source_target_pairs={{0,4},{4,8},{8,12},{12,16},{16,20},{20,24},{24,28},{1,5},{5,9},{9,... | collective-permute-start | bytes 1161224 | tf_op jit(solution)/shard_map/ppermute | solution.py:22
  85.5 17.3 %collective-permute-start.1 = (bf16[2,96,9,1,112]{4,1,3,2,0:T(8,128)(2,1)S(1)}, bf16[2,96,9,1,112]{4,1,3,2,0:T(8,128)(2,1)S(1)}, u32[]{:S(2)}, u32[]{:S(2)}) collective-permute-start(bf16[2,96,9,1,112]{4,1,3,2,0:T(8,128)(2,1)S(1)} %get-tuple-element.27), channel_id=1, source_target_pairs={{4,0},{8,4},{12,8},{16,12},{20,16},{24,20},{28,24},{5,1},{9,5},{13... | collective-permute-start | bytes 1161224 | tf_op jit(solution)/shard_map/ppermute | solution.py:25
  145.7 66.7 %copy-start.11 = (bf16[32,160]{1,0:T(8,128)(2,1)S(1)}, bf16[32,160]{1,0:T(8,128)(2,1)}, u32[]{:S(2)}) copy-start(bf16[32,160]{1,0:T(8,128)(2,1)} %param.14) | copy-start | bytes 30724
  206.1 31.0 %all-to-all-start = ((bf16[2,3,8,28,112]{4,0,3,1,2:T(2,128)(2,1)}), bf16[2,3,8,28,112]{4,0,3,1,2:T(2,128)(2,1)S(1)}, u32[]{:S(2)}, u32[]{:S(2)}) async-start(bf16[2,3,8,28,112]{4,0,3,1,2:T(2,128)(2,1)} %fusion.136), calls=%async_computation | async-start | bytes 688128 | tf_op jit(solution)/shard_map/all_to_all | solution.py:139
  240.2 19.7 %copy-start.10 = (f32[1280]{0:T(1024)S(1)}, f32[1280]{0:T(1024)}, u32[]{:S(2)}) copy-start(f32[1280]{0:T(1024)} %param.17) | copy-start | bytes 15364
  240.2 33.2 %copy-start.14 = (s32[2]{0:T(128)S(1)}, s32[2]{0:T(128)}, u32[]{:S(2)}) copy-start(s32[2]{0:T(128)} %param.18) | copy-start | bytes 28
  253.4 3.9 copy-start.8
  254.5 2.8 copy-start.6
  256.2 1.1 copy-start.7
  259.6 50.6 %copy-start.5 = (bf16[588,1280]{0,1:T(8,128)(2,1)S(1)}, bf16[588,1280]{0,1:T(8,128)(2,1)}, u32[]{:S(2)}) copy-start(bf16[588,1280]{0,1:T(8,128)(2,1)} %all-gather.4.cloned.1.call-done) | copy-start | bytes 4515844
  325.5 11.2 %all-to-all-start.1 = ((bf16[2,3,1,224,112]{4,0,2,1,3:T(2,128)(2,1)}), bf16[2,3,1,224,112]{4,0,2,1,3:T(2,128)(2,1)S(1)}, u32[]{:S(2)}, u32[]{:S(2)}) async-start(bf16[2,3,1,224,112]{4,0,2,1,3:T(2,128)(2,1)} %reshape.188), calls=%async_computation.1 | async-start | bytes 688128 | tf_op jit(solution)/shard_map/all_to_all | solution.py:171
  337.2 2.8 collective-permute-start.2
  338.5 3.9 collective-permute-start.3
  373.9 29.5 %copy-start.4 = (f32[2,9,28,112]{3,2,1,0:T(8,128)S(1)}, f32[2,9,28,112]{3,2,1,0:T(8,128)}, u32[]{:S(2)}) copy-start(f32[2,9,28,112]{3,2,1,0:T(8,128)} %copy-done.3) | copy-start | bytes 677380
Sparse Core Ops, SparseCore 0:
  9.2 28.6 all-gather.3
  39.8 39.7 all-gather.5
  102.6 29.4 all-gather.7
where the time goes:
time: 489 us; the launch traced here: 480 us
  local copies, waits for them, and re-layouts  178 us (36%)
  other arithmetic  99.5 us (20%)
  blocking collectives  83.1 us (17%)
  matrix products  80 us (16%)
  starting transfers between devices  15.2 us (3%)
  between operations  13.8 us (3%)
  waiting for transfers between devices  10.9 us (2%)
    add x1, other arithmetic, conv_rows(): summed + spread[:, tap_index, :, step_time:step_time + frame_count, step_...  48.2 us
    reshape x2, local copies, waits for them, and re-layouts, local(): result.transpose(0, 2, 3, 1, 4)  45.1 us
    unnamed x54, local copies, waits for them, and re-layouts  36.1 us
    dot_general x1, matrix products, local(): jnp.einsum('koc,skotrw->sctrw', tap_weights, stacked, preferred_element_t...  29.5 us
    convert_element_type x1, local copies, waits for them, and re-layouts, local(): inputs = layered.astype(jnp.float32)  28 us
    convert_element_type x1, other arithmetic, local(): result = pull_norm(activation_grad)[0].astype(jnp.bfloat16)  24.9 us
    slice x1, local copies, waits for them, and re-layouts, conv_rows(): spread[:, tap_index, :, step_time:step_time + frame_count, step_row:step_...  22.7 us
    dot_general x1, matrix products, conv_rows(): jnp.einsum('koc,sctrw->skotrw', tap_weights, padded, preferred_element_ty...  20.2 us
  transfers between devices with their start and end apart: 9, of which 2 were waited for; matrix products, arithmetic and copies ran while one was open for 36% of the time, Pallas kernels for 0%

commit v1 on v0

v1 whole, which is shorter than its diff:
```python
import functools

import jax
import jax.numpy as jnp
from jax import lax
from jax.experimental import pallas as pl
from jax.experimental.pallas import tpu as pltpu
from jax.sharding import PartitionSpec as P

SCORED = 8
PATCH = 14
HEADS = 8
HD = 80
GROUP = 4
LOSS_SCALE = 16384.0
SMOOTH = 0.01

CH = 96
COLS = 112
SPAN = 8 * COLS
SPANS = CH // 8
OUT_ROWS = 27 * 16
IN_ROWS = CH * 8
NT = 8
NZ = 4
PACK = 1120
KIN = 896
D = 1280
NTOK = 128
F32 = jnp.float32
BF16 = jnp.bfloat16


def lane_iota(rows):
    return lax.broadcasted_iota(jnp.int32, (rows, 128), 1)


def left(value, amount):
    amount = amount % 128
    return value if amount == 0 else pltpu.roll(value, 128 - amount, 1)


def to_channels(tiles, lane):
    found = []
    for k in range(8):
        start = COLS * k
        q, off = divmod(start, 128)
        head = left(tiles[q], off)
        if 128 - off < COLS:
            head = jnp.where(lane < 128 - off, head, left(tiles[q + 1], off))
        found.append(head)
    return found


def to_tiles(channels, lane):
    found = []
    for q in range(7):
        cut = COLS - 16 * q
        found.append(
            jnp.where(lane < cut, left(channels[q], 16 * q), left(channels[q + 1], 128 - cut))
        )
    return found


def spread_all(value, lane):
    return to_tiles([value] * 8, lane)


def fold_all(tiles, lane):
    parts = to_channels(tiles, lane)
    while len(parts) > 1:
        parts = [parts[i] + parts[i + 1] for i in range(0, len(parts), 2)]
    return parts[0]


def load_rows(ref, row, count, lane):
    value = ref[0, 0, row : row + count, lane : lane + SPAN].astype(F32)
    if count < 16:
        value = jnp.concatenate([value, jnp.zeros((16 - count, SPAN), F32)], axis=0)
    return value


def lane_tiles(value):
    return [value[:, 128 * q : 128 * q + 128] for q in range(7)]


def banded(weight_ref, transposed):
    pick = (
        lax.broadcasted_iota(jnp.int32, (OUT_ROWS, 32), 0) // 16
        == lax.broadcasted_iota(jnp.int32, (OUT_ROWS, 32), 1)
    ).astype(BF16)
    if transposed:
        shape, p_dim, r_dim = (IN_ROWS, OUT_ROWS), 1, 0
        grow = (
            lax.broadcasted_iota(jnp.int32, (IN_ROWS, CH), 0) // 8
            == lax.broadcasted_iota(jnp.int32, (IN_ROWS, CH), 1)
        ).astype(BF16)
    else:
        shape, p_dim, r_dim = (OUT_ROWS, IN_ROWS), 0, 1
        grow = (
            lax.broadcasted_iota(jnp.int32, (CH, IN_ROWS), 1) // 8
            == lax.broadcasted_iota(jnp.int32, (CH, IN_ROWS), 0)
        ).astype(BF16)
    p_at = lax.broadcasted_iota(jnp.int32, shape, p_dim) % 16
    r_at = lax.broadcasted_iota(jnp.int32, shape, r_dim) % 8
    total = jnp.zeros(shape, F32)
    for b in range(3):
        rows = jnp.dot(pick, weight_ref[b], preferred_element_type=F32).astype(BF16)
        if transposed:
            full = lax.dot_general(
                grow, rows, (((1,), (1,)), ((), ())), preferred_element_type=F32
            )
        else:
            full = jnp.dot(rows, grow, preferred_element_type=F32)
        total = jnp.where(p_at == r_at + 2 - b, full, total)
    return total.astype(BF16)


def decode_kernel(row_count, slot_ref, live_ref, x_ref, gain_ref, weight_ref, out_ref, inv_ref, band, operand, acc):
    s, t = pl.program_id(0), pl.program_id(1)
    frames = pl.num_programs(1)
    slabs = -(-row_count // 16)
    lane = lane_iota(16)

    @pl.when((s == 0) & (t == 0))
    def _():
        band[...] = banded(weight_ref, False)

    @pl.when(t == 0)
    def _():
        acc[...] = jnp.zeros(acc.shape, F32)

    for slab in range(slabs):
        row = 16 * slab
        count = min(16, row_count - row)
        square = jnp.zeros((16, SPAN), F32)
        for g in range(SPANS):
            value = load_rows(x_ref, row, count, g * SPAN)
            square = square + value * value
        second = fold_all(lane_tiles(square), lane) * (1.0 / CH)
        inv = jnp.concatenate(spread_all(lax.rsqrt(second + 1e-06), lane), axis=1)
        inv_ref[0, 0, row : row + 16, :] = inv
        for g in range(SPANS):
            value = load_rows(x_ref, row, count, g * SPAN)
            half = value * inv * gain_ref[:, g * SPAN : g * SPAN + SPAN]
            act = half + half * jnp.tanh(half)
            found = to_channels(lane_tiles(act), lane)
            for m in range(4):
                at = (g * 8 + 2 * m) * 8
                one, two = found[2 * m], found[2 * m + 1]
                operand[slab, at : at + 16, 0:128] = jnp.concatenate(
                    [one[:8], two[:8]], axis=0
                ).astype(BF16)
                operand[slab, at : at + 16, 128:256] = jnp.concatenate(
                    [one[8:], two[8:]], axis=0
                ).astype(BF16)
        spread = jnp.dot(band[...], operand[slab], preferred_element_type=F32)
        lane_out = lane_iota(144)
        for half_at in range(2):
            k = 2 * slab + half_at
            part = spread[:, 128 * half_at : 128 * half_at + 128]
            low, mid, high = part[0:144], part[144:288], part[288:432]
            low = jnp.where(lane_out == 0, 0.0, pltpu.roll(low, 1, 1))
            high = jnp.where(lane_out == COLS - 1, 0.0, pltpu.roll(high, 127, 1))
            total = low + mid + high
            for a in range(3):
                for o in range(3):
                    at = (a * 3 + o) * 16
                    acc[2 - a, o, 8 * k : 8 * k + 16, :] += total[at : at + 16]

    @pl.when(live_ref[s * frames + t] > 0)
    def _():
        rows = out_ref.shape[3]
        keep = lane_iota(rows) < COLS
        for o in range(3):
            out_ref[0, 0, o] = jnp.where(keep, acc[0, o, 0:rows, :], 0.0).astype(BF16)

    acc[0] = acc[1]
    acc[1] = acc[2]
    acc[2] = jnp.zeros(acc.shape[1:], F32)


def restore_kernel(row_count, entry_ref, x_ref, inv_ref, gain_ref, weight_ref, grad_ref, scale_ref, out_ref, band, shifted, operand, coming, inner):
    s, t = pl.program_id(0), pl.program_id(1)
    frames = pl.num_programs(1)
    slabs = -(-row_count // 16)
    lane = lane_iota(16)
    lane8 = lane_iota(8)
    rows = grad_ref.shape[3]

    @pl.when((s == 0) & (t == 0))
    def _():
        band[...] = banded(weight_ref, True)
        shifted[...] = jnp.zeros(shifted.shape, F32)

    @pl.when(t == 0)
    def _():
        lane_rows = lane_iota(rows)

        def one_frame(frame, carry):
            entry = entry_ref[s * frames + frame]
            scale = jnp.where(entry >= 0, scale_ref[s], 0.0)
            source = jnp.maximum(entry, 0)
            for o in range(3):
                value = grad_ref[source, s, o].astype(F32) * scale
                value = jnp.where(lane_rows < COLS, value, 0.0).astype(BF16).astype(F32)
                shifted[frame, 0, o, 0:rows, :] = pltpu.roll(value, 127, 1)
                shifted[frame, 1, o, 0:rows, :] = value
                shifted[frame, 2, o, 0:rows, :] = pltpu.roll(value, 1, 1)
            return carry

        lax.fori_loop(0, frames, one_frame, 0)

    for slab in range(slabs):
        row = 16 * slab
        count = min(16, row_count - row)
        for e in range(3):
            for a in range(3):
                for o in range(3):
                    at = ((e * 3 + a) * 3 + o) * 16
                    for half_at in range(2):
                        k = 2 * slab + half_at
                        operand[slab, at : at + 16, 128 * half_at : 128 * half_at + 128] = shifted[
                            t + 2 - a, e, o, 8 * k : 8 * k + 16, :
                        ].astype(BF16)
        coming[slab] = jnp.dot(band[...], operand[slab], preferred_element_type=F32)
        inv = inv_ref[0, 0, row : row + 16, :]
        total = jnp.zeros((16, SPAN), F32)
        for g in range(SPANS):
            halves = []
            for half_at in range(2):
                channels = [
                    coming[slab, (g * 8 + k) * 8 : (g * 8 + k) * 8 + 8, 128 * half_at : 128 * half_at + 128]
                    for k in range(8)
                ]
                halves.append(jnp.concatenate(to_tiles(channels, lane8), axis=1))
            cot = jnp.concatenate(halves, axis=0)
            value = load_rows(x_ref, row, count, g * SPAN)
            gain = gain_ref[:, g * SPAN : g * SPAN + SPAN]
            half = value * inv * gain
            th = jnp.tanh(half)
            out = cot * gain * (1.0 + th) * (1.0 + half * (1.0 - th))
            total = total + out * value
            inner[slab, :, g * SPAN : g * SPAN + SPAN] = out
        folded = fold_all(lane_tiles(total), lane) * (1.0 / CH)
        factor = jnp.concatenate(spread_all(folded, lane), axis=1) * inv * inv * inv
        for g in range(SPANS):
            value = load_rows(x_ref, row, count, g * SPAN)
            result = inner[slab, :, g * SPAN : g * SPAN + SPAN] * inv - value * factor
            out_ref[0, 0, row : row + count, g * SPAN : g * SPAN + SPAN] = result[:count].astype(BF16)


def nt_dot(one, two):
    return lax.dot_general(one, two, (((1,), (1,)), ((), ())), preferred_element_type=F32)


def tn_dot(one, two):
    return lax.dot_general(one, two, (((0,), (0,)), ((), ())), preferred_element_type=F32)


def nn_dot(one, two):
    return jnp.dot(one, two, preferred_element_type=F32)


def split_two(value):
    high = value.astype(BF16)
    low = (value - high.astype(F32)).astype(BF16)
    return jnp.concatenate([high, low], axis=0)


def reward_kernel(
    row_count, tiles, samples,
    part_ref, pack_ref, head_ref,
    out_ref, score_ref,
    frame, flip, embed, outw, place, patches, tokens, normed, normed16, slots, weights, dslots, dnormed, rows8, abar,
):
    height = row_count * tiles
    patch_rows = height // PATCH
    lane64 = lane_iota(8) < 64
    lane = lane_iota(NTOK)
    count = samples * NTOK

    embed[...] = jnp.zeros(embed.shape, BF16)
    lane96 = lane_iota(96)
    for z in range(NZ):
        for i in range(NT):
            source = pack_ref.at[i * NZ + z]
            for xx in range(4):
                x = 4 * z + xx
                if x < PATCH:
                    embed[64 * x : 64 * x + 48, 128 * i : 128 * i + 128] = source[640 + 48 * xx : 688 + 48 * xx, :]
            outw[160 * z : 160 * z + 160, 128 * i : 128 * i + 128] = source[832:992, :]
            place[32 * z : 32 * z + 32, 128 * i : 128 * i + 128] = source[992:1024, :]
        for ib in range(2):
            sources = [pack_ref[(4 * ib + j) * NZ + z, 1024:1120, :].astype(F32) for j in range(4)]
            rolled = [[sources[j] if d == 0 else pltpu.roll(sources[j], 32 * d, 1) for d in range(4)] for j in range(4)]
            at = 1024 + 128 * ib
            for q in range(4):
                found = rolled[0][(0 - q) % 4]
                for j in range(1, 4):
                    found = jnp.where(lane96 >= 32 * j, rolled[j][(j - q) % 4], found)
                found = found.astype(BF16)
                if q < 2:
                    for xx in range(2):
                        x = 4 * z + 2 * q + xx
                        if x < PATCH:
                            embed[64 * x : 64 * x + 48, at : at + 128] = found[48 * xx : 48 * xx + 48]
                elif q == 2:
                    outw[160 * z : 160 * z + 96, at : at + 128] = found
                else:
                    outw[160 * z + 96 : 160 * z + 160, at : at + 128] = found[:64]
                    place[32 * z : 32 * z + 32, at : at + 128] = found[64:96]

    flip[...] = jnp.zeros(flip.shape, F32)
    for f in range(samples):
        frame[...] = jnp.zeros(frame.shape, F32)
        for i in range(tiles):
            at = row_count * i + 7
            for o in range(3):
                frame[o, at : at + row_count + 2, :] += part_ref[i, f, o, 0 : row_count + 2, :].astype(F32)
        for pair in range(patch_rows // 2):
            for local in range(2):
                at = 8 + PATCH * (2 * pair + local)
                for o in range(3):
                    flip[0, 64 * local + PATCH * o : 64 * local + PATCH * o + PATCH, :] = (
                        frame[o, at : at + PATCH, :].astype(BF16).astype(F32)
                    )
            flip[1] = flip[0].T
            token = f * NTOK + pair * 16
            for y in range(PATCH // 2):
                even = flip[1, pl.ds(2 * y, 8, stride=PATCH), :]
                odd = flip[1, pl.ds(2 * y + 1, 8, stride=PATCH), :]
                patches[token : token + 8, 128 * y : 128 * y + 128] = jnp.where(lane64, even, pltpu.roll(odd, 64, 1))
                patches[token + 8 : token + 16, 128 * y : 128 * y + 128] = jnp.where(lane64, pltpu.roll(even, 64, 1), odd)

    token_value = nn_dot(patches[...].astype(BF16), embed[...])
    rows8[...] = jnp.zeros(rows8.shape, F32)
    abar[...] = jnp.zeros(abar.shape, F32)
    place_value = place[...].astype(F32)
    for f in range(samples):
        value = token_value[f * NTOK : f * NTOK + NTOK] + place_value
        rows8[0, f : f + 1, :] = jnp.mean(value, axis=0, keepdims=True)
        centered = value - jnp.mean(value, axis=-1, keepdims=True)
        scale = lax.rsqrt(jnp.mean(centered * centered, axis=-1, keepdims=True) + 1e-05)
        value = centered * scale
        normed[f * NTOK : f * NTOK + NTOK, :] = value
        normed16[f * NTOK : f * NTOK + NTOK, :] = value.astype(BF16)
        tokens[f * NTOK : f * NTOK + NTOK, :] = jnp.broadcast_to(scale, (NTOK, 128))

    def weight_part(i, z):
        source = pack_ref.at[i * NZ + z]
        return jnp.concatenate([source[0:256, :], source[320:576, :]], axis=1)

    def weight_rest(i):
        return jnp.concatenate(
            [
                jnp.concatenate([pack_ref[i * NZ + z, 256:320, :], pack_ref[i * NZ + z, 576:640, :]], axis=1)
                for z in range(NZ)
            ],
            axis=0,
        )

    lane_all = lane_iota(count)
    for i in range(NT):
        mixed = nn_dot(normed16[:, 1024:1280], weight_rest(i))
        for z in range(NZ):
            mixed = mixed + nn_dot(normed16[:, 256 * z : 256 * z + 256], weight_part(i, z))
        first, second = mixed[:, 0:128], mixed[:, 128:256]
        found = (
            first,
            jnp.where(lane_all < 48, pltpu.roll(first, 48, 1), pltpu.roll(second, 48, 1)),
            pltpu.roll(second, 96, 1),
        )
        for m in range(3):
            slots[3 * i + m] = jnp.where(lane_all < HD, found[m], 0.0).astype(BF16)

    for h in range(HEADS):
        for f in range(samples):
            span = slice(f * NTOK, f * NTOK + NTOK)
            logits = nt_dot(slots[h, span, :], slots[HEADS + h, span, :]) * HD ** (-0.5)
            logits = jnp.exp(logits - jnp.max(logits, axis=-1, keepdims=True))
            prob = logits / jnp.sum(logits, axis=-1, keepdims=True)
            weights[h * samples + f] = prob
            attended = nn_dot(prob.astype(BF16), slots[2 * HEADS + h, span, :]).astype(BF16)
            abar[h, f : f + 1, :] = jnp.mean(attended.astype(F32), axis=0, keepdims=True)

    pooled = rows8[0]
    for h in range(HEADS):
        part = nn_dot(split_two(abar[h])[:, 0:HD], outw[HD * h : HD * h + HD, :])
        pooled = pooled + part[0:8] + part[8:16]
    pooled = pooled - jnp.mean(pooled, axis=-1, keepdims=True)
    scale = lax.rsqrt(jnp.mean(pooled * pooled, axis=-1, keepdims=True) + 1e-05)
    pooled = pooled * scale
    head = head_ref[...]
    score_ref[...] = jnp.broadcast_to(jnp.sum(pooled * head, axis=-1, keepdims=True), (8, 128))
    dpooled = scale * (
        head - jnp.mean(head, axis=-1, keepdims=True) - pooled * jnp.mean(pooled * head, axis=-1, keepdims=True)
    )
    dres = dpooled * (1.0 / NTOK)
    rows8[1] = dres
    dres_two = split_two(dres)

    for h in range(HEADS):
        datt = nt_dot(dres_two, outw[HD * h : HD * h + HD, :])
        datt = (datt[0:8] + datt[8:16]).astype(BF16)
        datt = jnp.concatenate([datt, jnp.zeros((8, 128 - HD), BF16)], axis=1)
        for f in range(samples):
            span = slice(f * NTOK, f * NTOK + NTOK)
            prob = weights[h * samples + f]
            row = datt[f : f + 1, :]
            dweight = nt_dot(datt, slots[2 * HEADS + h, span, :])[f : f + 1, :].astype(BF16).astype(F32)
            inner = jnp.sum(prob * dweight, axis=-1, keepdims=True)
            dlogit = (prob * (dweight - inner) * HD ** (-0.5)).astype(BF16)
            dslots[h, span, :] = nn_dot(dlogit, slots[HEADS + h, span, :])
            dslots[HEADS + h, span, :] = tn_dot(dlogit, slots[h, span, :])
            dslots[2 * HEADS + h, span, :] = tn_dot(
                prob.astype(BF16), jnp.broadcast_to(row.astype(F32), (NTOK, 128)).astype(BF16)
            )

    dnormed[...] = jnp.zeros(dnormed.shape, F32)
    for i in range(NT):
        one, two, three = dslots[3 * i], dslots[3 * i + 1], dslots[3 * i + 2]
        two = pltpu.roll(two, 80, 1)
        three = pltpu.roll(three, 32, 1)
        first = jnp.where(lane_all < HD, one, two)
        second = jnp.where(lane_all < 32, two, jnp.where(lane_all < COLS, three, 0.0))
        dmixed = jnp.concatenate([first, second], axis=1).astype(BF16)
        for z in range(NZ):
            dnormed[:, 256 * z : 256 * z + 256] += nt_dot(dmixed, weight_part(i, z))
        dnormed[:, 1024:1280] += nt_dot(dmixed, weight_rest(i))

    for f in range(samples):
        span = slice(f * NTOK, f * NTOK + NTOK)
        value, dvalue = normed[span, :], dnormed[span, :]
        scale = tokens[span, 0:1]
        dvalue = scale * (
            dvalue
            - jnp.mean(dvalue, axis=-1, keepdims=True)
            - value * jnp.mean(dvalue * value, axis=-1, keepdims=True)
        )
        normed16[span, :] = (dvalue + rows8[1, f : f + 1, :]).astype(BF16)
    patches[...] = nt_dot(normed16[...], embed[...])

    frame[...] = jnp.zeros(frame.shape, F32)
    rows = out_ref.shape[3]
    flip[...] = jnp.zeros(flip.shape, F32)
    for f in range(samples):
        for pair in range(patch_rows // 2):
            token = f * NTOK + pair * 16
            for y in range(PATCH // 2):
                one = patches[token : token + 8, 128 * y : 128 * y + 128]
                two = patches[token + 8 : token + 16, 128 * y : 128 * y + 128]
                flip[1, pl.ds(2 * y, 8, stride=PATCH), :] = jnp.where(lane64, one, pltpu.roll(two, 64, 1))
                flip[1, pl.ds(2 * y + 1, 8, stride=PATCH), :] = jnp.where(lane64, pltpu.roll(one, 64, 1), two)
            flip[0] = flip[1].T
            for local in range(2):
                at = 8 + PATCH * (2 * pair + local)
                for o in range(3):
                    frame[o, at : at + PATCH, :] = flip[0, 64 * local + PATCH * o : 64 * local + PATCH * o + PATCH, :]
        for i in range(tiles):
            at = row_count * i + 7
            for o in range(3):
                out_ref[i, f, o] = frame[o, at : at + rows, :].astype(BF16)


def pack_part(rows_in, embed_part, out_part, place_part):
    ordered = jnp.concatenate([rows_in[0:128], rows_in[160:288], rows_in[128:160], rows_in[288:320]], axis=0)
    upper = jnp.pad(ordered[:, 128:240], ((0, 0), (0, 16)))
    other = jnp.concatenate([embed_part, out_part, place_part], axis=0)
    rest = other[:, 128:160].reshape(4, 96, 32)
    rest = jnp.concatenate([rest[q] for q in range(4)], axis=1)
    return jnp.concatenate([ordered[:, 0:128], upper, other[:, 0:128], rest], axis=0)


def embed_rows(patch_embed):
    columns = patch_embed.shape[1]
    ordered = patch_embed.reshape(3 * PATCH, PATCH, columns).transpose(1, 0, 2)
    ordered = jnp.pad(ordered, ((0, 16 - PATCH), (0, 48 - 3 * PATCH), (0, 0)))
    return ordered.reshape(16 * 48, columns)


def packed_weights(patch_embed, position, attend_in, attend_out):
    tiles, parts = lax.axis_size("tile"), lax.axis_size("sample")
    if tiles == NT and parts == NZ:
        z = lax.axis_index("sample")
        embed_part = lax.dynamic_slice_in_dim(embed_rows(patch_embed), z * 192, 192, axis=0)
        mine = pack_part(attend_in, embed_part, attend_out, position)
        return lax.all_gather(mine, ("tile", "sample"), axis=0)

    def whole(value):
        value = lax.all_gather(value, "sample", axis=0, tiled=True)
        return lax.all_gather(value, "tile", axis=1, tiled=True)

    embed_full = embed_rows(lax.all_gather(patch_embed, "tile", axis=1, tiled=True))
    split = [
        value.reshape(NZ, value.shape[0] // NZ, NT, value.shape[1] // NT).transpose(2, 0, 1, 3)
        for value in (whole(attend_in), embed_full, whole(attend_out), whole(position))
    ]
    split = [value.reshape((NT * NZ,) + value.shape[2:]) for value in split]
    return jax.vmap(pack_part)(*split)


def params(mib=48):
    return pltpu.CompilerParams(vmem_limit_bytes=mib * 1024 * 1024)


def local(
    features,
    norm_gain,
    conv_weight,
    patch_embed,
    position,
    attend_in,
    attend_out,
    reward_head,
    group_index,
    frame_pick,
):
    samples, frames, row_count, merged = features.shape
    tiles, parts = lax.axis_size("tile"), lax.axis_size("sample")
    slabs = -(-row_count // 16)
    sent_rows = -(-(row_count + 2) // 16) * 16
    acc_rows = max(16 * slabs + 8, sent_rows)
    packed = packed_weights(patch_embed, position, attend_in, attend_out)
    half_gain = jnp.repeat(0.5 * norm_gain, COLS)[None, :]
    taps = jnp.pad(
        conv_weight.transpose(1, 2, 0, 3, 4).reshape(3, 27, CH), ((0, 0), (0, 5), (0, 0))
    )

    is_entry = frame_pick[:, None, :] == jnp.arange(frames, dtype=jnp.int32)[None, :, None]
    entry_at = jnp.arange(SCORED, dtype=jnp.int32)[None, None, :]
    live = jnp.any(is_entry, axis=2).astype(jnp.int32)
    entry = jnp.sum(jnp.where(is_entry, entry_at, 0), axis=2) - (1 - live)
    following = jnp.concatenate([entry[:, 1:], entry[:, -2:-1]], axis=1)
    slot = jnp.where(entry >= 0, entry, following).reshape(-1)
    live = live.reshape(-1)

    x_spec = pl.BlockSpec((1, 1, row_count, merged), lambda s, t, *_: (s, t, 0, 0))
    inv_spec = pl.BlockSpec((1, 1, 16 * slabs, SPAN), lambda s, t, *_: (s, t, 0, 0))
    gain_spec = pl.BlockSpec((1, merged), lambda s, t, *_: (0, 0))
    taps_spec = pl.BlockSpec((3, 32, CH), lambda s, t, *_: (0, 0, 0))
    decoded, inverse = pl.pallas_call(
        functools.partial(decode_kernel, row_count),
        grid_spec=pltpu.PrefetchScalarGridSpec(
            num_scalar_prefetch=2,
            grid=(samples, frames),
            in_specs=[x_spec, gain_spec, taps_spec],
            out_specs=[
                pl.BlockSpec(
                    (1, 1, 3, sent_rows, 128),
                    lambda s, t, slot_ref, live_ref: (slot_ref[s * frames + t], s, 0, 0, 0),
                ),
                inv_spec,
            ],
            scratch_shapes=[
                pltpu.VMEM((OUT_ROWS, IN_ROWS), BF16),
                pltpu.VMEM((slabs, IN_ROWS, 256), BF16),
                pltpu.VMEM((3, 3, acc_rows, 128), F32),
            ],
        ),
        out_shape=[
            jax.ShapeDtypeStruct((SCORED, samples, 3, sent_rows, 128), BF16),
            jax.ShapeDtypeStruct((samples, frames, 16 * slabs, SPAN), F32),
        ],
        compiler_params=params(),
        name="decode",
    )(slot, live, features, half_gain, taps)

    if tiles > SCORED:
        decoded = jnp.pad(decoded, ((0, tiles - SCORED),) + ((0, 0),) * 4)
    owned = lax.all_to_all(decoded, "tile", split_axis=0, concat_axis=0, tiled=True)

    head = reward_head.reshape(NT, D // NT)
    head = jnp.concatenate([head[:, :128].reshape(-1), head[:, 128:].reshape(-1)])[None, :]
    height = row_count * tiles
    count = samples * NTOK
    grads, scores = pl.pallas_call(
        functools.partial(reward_kernel, row_count, tiles, samples),
        out_shape=[
            jax.ShapeDtypeStruct((tiles, samples, 3, sent_rows, 128), BF16),
            jax.ShapeDtypeStruct((8, 128), F32),
        ],
        scratch_shapes=[
            pltpu.VMEM((3, height + 48, 128), F32),
            pltpu.VMEM((2, 128, 128), F32),
            pltpu.VMEM((KIN, D), BF16),
            pltpu.VMEM((HEADS * HD, D), BF16),
            pltpu.VMEM((NTOK, D), BF16),
            pltpu.VMEM((count, KIN), F32),
            pltpu.VMEM((count, 128), F32),
            pltpu.VMEM((count, D), F32),
            pltpu.VMEM((count, D), BF16),
            pltpu.VMEM((3 * HEADS, count, 128), BF16),
            pltpu.VMEM((HEADS * samples, NTOK, NTOK), F32),
            pltpu.VMEM((3 * HEADS, count, 128), F32),
            pltpu.VMEM((count, D), F32),
            pltpu.VMEM((2, 8, D), F32),
            pltpu.VMEM((HEADS, 8, 128), F32),
        ],
        compiler_params=params(),
        name="reward",
    )(owned, packed, head)

    mine = jnp.concatenate([scores[:samples, 0], group_index.astype(F32)])
    gathered = [mine]
    for shift in range(1, parts):
        ring = [(z, (z + shift) % parts) for z in range(parts)]
        gathered.append(lax.ppermute(mine, "sample", ring))
    gathered = jnp.stack(gathered)
    groups = gathered[:, samples:].reshape(-1)
    score_row = gathered[:, :samples].reshape(-1)
    high = score_row.astype(BF16)
    low = score_row - high.astype(F32)
    mid = low.astype(BF16)
    low = (low - mid.astype(F32)).astype(BF16)
    total = parts * samples
    carried = jnp.concatenate([high, mid, low])
    grads = grads.at[:, 0, 0, sent_rows - 1, 0 : 3 * total].set(
        jnp.broadcast_to(carried, (tiles, 3 * total))
    )
    returned = lax.all_to_all(grads, "tile", split_axis=0, concat_axis=0, tiled=True)
    returned = returned[:SCORED]

    got = returned[:, 0, 0, sent_rows - 1, 0 : 3 * total].astype(F32).reshape(SCORED, 3, total)
    entry_scores = got[:, 0] + (got[:, 1] + got[:, 2])
    rewards = jnp.sum(entry_scores, axis=0) / SCORED
    member = (groups[:samples, None] == groups[None, :]).astype(F32)
    mean_group = jnp.sum(member * rewards[None, :], axis=1) / GROUP
    second_group = jnp.sum(member * (rewards * rewards)[None, :], axis=1) / GROUP - mean_group * mean_group
    advantage = (rewards[:samples] - mean_group) * lax.rsqrt(second_group + SMOOTH)
    cotangent = -LOSS_SCALE * advantage / SCORED

    return pl.pallas_call(
        functools.partial(restore_kernel, row_count),
        grid_spec=pltpu.PrefetchScalarGridSpec(
            num_scalar_prefetch=1,
            grid=(samples, frames),
            in_specs=[
                x_spec,
                inv_spec,
                gain_spec,
                taps_spec,
                pl.BlockSpec((SCORED, samples, 3, sent_rows, 128), lambda s, t, *_: (0, 0, 0, 0, 0)),
                pl.BlockSpec(memory_space=pltpu.SMEM),
            ],
            out_specs=x_spec,
            scratch_shapes=[
                pltpu.VMEM((IN_ROWS, OUT_ROWS), BF16),
                pltpu.VMEM((frames + 2, 3, 3, acc_rows, 128), F32),
                pltpu.VMEM((slabs, OUT_ROWS, 256), BF16),
                pltpu.VMEM((slabs, IN_ROWS, 256), F32),
                pltpu.VMEM((slabs, 16, merged), F32),
            ],
        ),
        out_shape=jax.ShapeDtypeStruct(features.shape, BF16),
        compiler_params=params(),
        name="restore",
    )(entry.reshape(-1), features, inverse, half_gain, taps, returned, cotangent)


def solution(mesh):
    in_specs = (
        P("sample", None, "tile", None),
        P(),
        P(),
        P(None, "tile"),
        P("sample", "tile"),
        P("sample", "tile"),
        P("sample", "tile"),
        P(),
        P("sample"),
        P("sample", None),
    )
    out_specs = P("sample", None, "tile", None)
    return jax.shard_map(local, mesh=mesh, in_specs=in_specs, out_specs=out_specs, check_vma=False)
```

time: 489 us -> 204 us (0.42); the launches traced: 480 us -> 203 us
  local copies, waits for them, and re-layouts: 178 us -> 37.7 us
  other arithmetic: 99.5 us -> 4.55 us
  Pallas kernels: 0 us -> 83.5 us
  blocking collectives: 83.1 us -> 0 us
  matrix products: 80 us -> 0 us
  waiting for transfers between devices: 10.9 us -> 50.9 us
    pallas_call x0 -> x3, Pallas kernels: none -> 83.5 us  [the longest x1 35.2 us: local(): pl.pallas_call(functools.partial(restore_kernel, row_count), grid_spec=pl...]
    dot_general x14 -> x0, matrix products: 78.3 us -> none  [the longest x1 29.5 us: local(): jnp.einsum('koc,skotrw->sctrw', tap_weights, stacked, preferred_element_t...]
    reshape x9 -> x6, local copies, waits for them, and re-layouts: 65.7 us -> 0.38 us  [the longest x1 0.12 us: embed_rows(): ordered = patch_embed.reshape(3 * PATCH, PATCH, columns).transpose(1, 0, 2)]
    all_gather x4 -> x0, blocking collectives: 58.3 us -> none  [the longest x1 19.8 us: local(): lax.all_gather(attend_in, 'sample', axis=0, tiled=True)]
    add x1 -> x0, other arithmetic: 48.2 us -> none  [conv_rows(): summed + spread[:, tap_index, :, step_time:step_time + frame_count, step_...]
    convert_element_type x4, other arithmetic: 32.8 us -> 0.04 us  [the longest x1 0.02 us: local(): returned[:, 0, 0, sent_rows - 1, 0:3 * total].astype(F32)]
    convert_element_type x4 -> x2, local copies, waits for them, and re-layouts: 32.7 us -> 0.16 us  [the longest x1 0.08 us: local(): live = jnp.any(is_entry, axis=2).astype(jnp.int32)]
    all_gather x3 -> x1, waiting for transfers between devices: 0.02 us -> 30.5 us  [packed_weights(): return lax.all_gather(mine, ('tile', 'sample'), axis=0)]
  transfers between devices with their start and end apart: 9 -> 6, of which waited for: 2 -> 5; matrix products, arithmetic and copies ran while one was open for 36% -> 7% of each run, Pallas kernels for 0% -> 12%
where the time goes in v1:
time: 204 us; the launch traced here: 203 us
  Pallas kernels  83.5 us (41%)
  waiting for transfers between devices  50.9 us (25%)
  local copies, waits for them, and re-layouts  37.7 us (18%)
  between operations  13.6 us (7%)
  starting transfers between devices  12.8 us (6%)
  other arithmetic  4.55 us (2%)
    pallas_call x1, Pallas kernels, local(): pl.pallas_call(functools.partial(restore_kernel, row_count), grid_spec=pl...  35.2 us
    all_gather x1, waiting for transfers between devices, packed_weights(): return lax.all_gather(mine, ('tile', 'sample'), axis=0)  30.5 us
    pallas_call x1, Pallas kernels, local(): pl.pallas_call(functools.partial(decode_kernel, row_count), grid_spec=plt...  24.8 us
    pallas_call x1, Pallas kernels, local(): pl.pallas_call(functools.partial(reward_kernel, row_count, tiles, samples...  23.4 us
    pallas_call x1, local copies, waits for them, and re-layouts, local(): pl.pallas_call(functools.partial(restore_kernel, row_count), grid_spec=pl...  19.4 us
    unnamed x7, local copies, waits for them, and re-layouts  12.2 us
    all_to_all x1, waiting for transfers between devices, local(): lax.all_to_all(decoded, 'tile', split_axis=0, concat_axis=0, tiled=True)  8.14 us
    all_to_all x1, waiting for transfers between devices, local(): lax.all_to_all(grads, 'tile', split_axis=0, concat_axis=0, tiled=True)  7.9 us
  transfers between devices with their start and end apart: 6, of which 5 were waited for; matrix products, arithmetic and copies ran while one was open for 7% of the time, Pallas kernels for 12%

profile of v1, /device:TPU:0, one launch (start us, length us, event | category | flops | bytes accessed | tf_op | source)
XLA Modules:
  0.0 203.0 jit_solution(5587147600375227816)
XLA Ops:
  6.5 0.0 all-gather.3.cloned.1.call-start
  6.5 0.7 fusion.22
  7.3 0.9 fusion.21
  8.2 0.7 slice.140
  9.0 1.1 copy.29
  10.1 0.1 reshape.99
  10.2 0.1 copy.33
  10.3 0.1 pad.18.clone
  10.4 1.8 fusion.9
  12.2 0.0 all-gather.3.cloned.1.call-update
  12.2 0.8 select_reduce_fusion
  13.0 0.1 reduce_sum.39
  13.1 0.8 fusion.12
  13.9 0.1 slice.130
  13.9 0.1 slice.129
  14.0 0.1 reshape.105.live_ref
  14.1 0.1 pad_add_fusion
  14.2 0.1 concatenate.34
  14.3 0.8 copy.27
  15.1 0.7 broadcast_multiply_fusion.1
  15.7 0.1 broadcast_in_dim.27
  15.8 0.1 broadcast_in_dim_reshape.4.gain_ref
  15.9 11.0 %copy.31.x_ref = bf16[2,9,28,10752]{3,2,1,0:T(8,128)(2,1)} copy(bf16[2,9,28,10752]{3,0,2,1:T(2,128)(2,1)} %param.12) | data formatting | bytes 21676032 | tf_op args[0]
  27.0 0.0 copy-start.1
  27.0 0.0 copy-start
  27.0 24.8 %decode.1 = (bf16[8,2,3,32,128]{4,3,2,1,0:T(8,128)(2,1)}, f32[2,9,32,896]{3,2,1,0:T(8,128)S(1)}) custom-call(s32[18]{0:T(128)S(1)} %get-tuple-element.27.slot_ref, s32[18]{0:T(128)S(1)} %reshape.105.live_ref, bf16[2,9,28,10752]{3,2,1,0:T(8,128)(2,1)} %copy.31.x_ref, f32[1,10752]{1,0:T(1,128)S(1)} %broadcast_in_dim_reshape.4.gain_ref, ...), custom_call_target="tpu_custom_call" | custom-call | tf_op jit(solution)/shard_map/decode/pallas_call | solution.py:542
  51.8 5.1 %all-to-all-start = ((bf16[8,2,3,32,128]{4,3,2,1,0:T(8,128)(2,1)}), bf16[8,2,3,32,128]{4,3,2,1,0:T(8,128)(2,1)S(1)}, u32[]{:S(2)}, u32[]{:S(2)}) async-start(bf16[8,2,3,32,128]{4,3,2,1,0:T(8,128)(2,1)} %get-tuple-element.22), calls=%async_computation | async-start | bytes 786432 | tf_op jit(solution)/shard_map/all_to_all | solution.py:571
  57.0 0.0 copy-done.1
  57.0 0.0 copy-done
  57.0 0.1 reshape.101
  57.1 0.1 reshape.103
  57.2 8.1 %all-to-all-done.part_ref = bf16[8,2,3,32,128]{4,3,2,1,0:T(8,128)(2,1)S(1)} async-done(((bf16[8,2,3,32,128]{4,3,2,1,0:T(8,128)(2,1)}), bf16[8,2,3,32,128]{4,3,2,1,0:T(8,128)(2,1)S(1)}, u32[]{:S(2)}, u32[]{:S(2)}) %all-to-all-start) | async-done | bytes 393248 | tf_op jit(solution)/shard_map/all_to_all | solution.py:571
  65.3 30.5 %all-gather.3.cloned.1.call-done = bf16[35840,128]{1,0:T(8,128)(2,1)} async-done(((bf16[1120,128]{1,0:T(8,128)(2,1)}), bf16[35840,128]{1,0:T(8,128)(2,1)}) %all-gather.3.cloned.1.call-update) | async-done | bytes 9175056 | tf_op jit(solution)/shard_map/all_gather | solution.py:488
  95.8 23.4 %reward.1 = (bf16[8,2,3,32,128]{4,3,2,1,0:T(8,128)(2,1)}, f32[8,128]{1,0:T(8,128)S(1)}) custom-call(bf16[8,2,3,32,128]{4,3,2,1,0:T(8,128)(2,1)S(1)} %all-to-all-done.part_ref, bf16[32,1120,128]{2,1,0:T(8,128)(2,1)} %bitcast.12, f32[1,1280]{1,0:T(1,128)S(1)} %broadcast_in_dim.28.head_ref), custom_call_target="tpu_custom_call" | custom-call | tf_op jit(solution)/shard_map/reward/pallas_call | solution.py:577
  119.3 0.1 slice_reduce_fusion
  119.4 0.1 pad_maximum_fusion.5
  119.5 1.9 collective-permute-start.2
  121.4 1.0 collective-permute-start.1
  122.4 1.0 collective-permute-start
  123.5 0.0 collective-permute-done.2
  123.5 2.4 %collective-permute-done.1 = f32[4]{0:T(128)S(1)} collective-permute-done((f32[4]{0:T(128)S(1)}, f32[4]{0:T(128)S(1)}, u32[]{:S(2)}, u32[]{:S(2)}) %collective-permute-start.1) | collective-permute-done | bytes 48 | tf_op jit(solution)/shard_map/ppermute | solution.py:608
  125.8 1.9 collective-permute-done
  127.8 0.1 fusion.23
  127.9 0.1 reshape.104
  128.0 0.1 pad_maximum_fusion.6
  128.1 1.4 scatter.4
  129.4 3.7 %all-to-all-start.1 = ((bf16[8,2,3,32,128]{4,3,2,1,0:T(8,128)(2,1)}), bf16[8,2,3,32,128]{4,3,2,1,0:T(8,128)(2,1)S(1)}, u32[]{:S(2)}, u32[]{:S(2)}) async-start(bf16[8,2,3,32,128]{4,3,2,1,0:T(8,128)(2,1)} %scatter.4), calls=%async_computation.1 | async-start | bytes 786432 | tf_op jit(solution)/shard_map/all_to_all | solution.py:621
  133.1 0.1 slice_bitcast_fusion.1
  133.2 0.1 eq.35
  133.3 7.9 %all-to-all-done.1.grad_ref = bf16[8,2,3,32,128]{4,3,2,1,0:T(8,128)(2,1)S(1)} async-done(((bf16[8,2,3,32,128]{4,3,2,1,0:T(8,128)(2,1)}), bf16[8,2,3,32,128]{4,3,2,1,0:T(8,128)(2,1)S(1)}, u32[]{:S(2)}, u32[]{:S(2)}) %all-to-all-start.1) | async-done | bytes 393248 | tf_op jit(solution)/shard_map/all_to_all | solution.py:621
  141.2 0.1 reshape.106
  141.3 0.2 fusion.16
  141.5 35.2 %restore.1 = bf16[2,9,28,10752]{3,2,1,0:T(8,128)(2,1)} custom-call(s32[18]{0:T(128)S(1)} %get-tuple-element.28.entry_ref, bf16[2,9,28,10752]{3,2,1,0:T(8,128)(2,1)} %copy.31.x_ref, f32[2,9,32,896]{3,2,1,0:T(8,128)S(1)} %get-tuple-element.21.inv_ref, f32[1,10752]{1,0:T(1,128)S(1)} %broadcast_in_dim_reshape.4.gain_ref, bf16[3,32,96]{2,1,0:T(8,128)(2,1)S(1)} %pad.16.weight_ref, ...), custom_call_target="tpu_custom_call" | custom-call | tf_op jit(solution)/shard_map/restore/pallas_call | solution.py:633
  176.7 19.4 %copy.32 = bf16[2,9,28,10752]{3,0,2,1:T(2,128)(2,1)} copy(bf16[2,9,28,10752]{3,2,1,0:T(8,128)(2,1)} %restore.1) | data formatting | bytes 21676032 | tf_op jit(solution)/shard_map/restore/pallas_call | solution.py:633
  (22 shorter events, 0.2 us)
Async XLA Ops:
  6.5 89.3 %all-gather.3.cloned.1.call-start = ((), (), s32[]{:S(2)}) async-start(), calls=%async_computation.2 | async-start | bytes 9461760 | tf_op jit(solution)/shard_map/all_gather | solution.py:488
  27.0 30.0 %copy-start.1 = (s32[2]{0:T(128)S(1)}, s32[2]{0:T(128)}, u32[]{:S(2)}) copy-start(s32[2]{0:T(128)} %param.20) | copy-start | bytes 28
  27.0 30.0 %copy-start = (f32[1280]{0:T(1024)S(1)}, f32[1280]{0:T(1024)}, u32[]{:S(2)}) copy-start(f32[1280]{0:T(1024)} %param.19) | copy-start | bytes 15364
  51.8 13.5 %all-to-all-start = ((bf16[8,2,3,32,128]{4,3,2,1,0:T(8,128)(2,1)}), bf16[8,2,3,32,128]{4,3,2,1,0:T(8,128)(2,1)S(1)}, u32[]{:S(2)}, u32[]{:S(2)}) async-start(bf16[8,2,3,32,128]{4,3,2,1,0:T(8,128)(2,1)} %get-tuple-element.22), calls=%async_computation | async-start | bytes 786432 | tf_op jit(solution)/shard_map/all_to_all | solution.py:571
  119.5 4.0 %collective-permute-start.2 = (f32[4]{0:T(128)S(1)}, f32[4]{0:T(128)S(1)}, u32[]{:S(2)}, u32[]{:S(2)}) collective-permute-start(f32[4]{0:T(128)S(1)} %pad_maximum_fusion.5), channel_id=1, source_target_pairs={{0,3},{1,0},{2,1},{3,2},{4,7},{5,4},{6,5},{7,6},{8,11},{9,8},{10,9... | collective-permute-start | bytes 56 | tf_op jit(solution)/shard_map/ppermute | solution.py:608
  121.4 4.4 %collective-permute-start.1 = (f32[4]{0:T(128)S(1)}, f32[4]{0:T(128)S(1)}, u32[]{:S(2)}, u32[]{:S(2)}) collective-permute-start(f32[4]{0:T(128)S(1)} %pad_maximum_fusion.5), channel_id=1, source_target_pairs={{0,2},{1,3},{2,0},{3,1},{4,6},{5,7},{6,4},{7,5},{8,10},{9,11},{10,... | collective-permute-start | bytes 56 | tf_op jit(solution)/shard_map/ppermute | solution.py:608
  122.4 5.3 %collective-permute-start = (f32[4]{0:T(128)S(1)}, f32[4]{0:T(128)S(1)}, u32[]{:S(2)}, u32[]{:S(2)}) collective-permute-start(f32[4]{0:T(128)S(1)} %pad_maximum_fusion.5), channel_id=1, source_target_pairs={{0,1},{1,2},{2,3},{3,0},{4,5},{5,6},{6,7},{7,4},{8,9},{9,10},{10,1... | collective-permute-start | bytes 56 | tf_op jit(solution)/shard_map/ppermute | solution.py:608
  129.4 11.7 %all-to-all-start.1 = ((bf16[8,2,3,32,128]{4,3,2,1,0:T(8,128)(2,1)}), bf16[8,2,3,32,128]{4,3,2,1,0:T(8,128)(2,1)S(1)}, u32[]{:S(2)}, u32[]{:S(2)}) async-start(bf16[8,2,3,32,128]{4,3,2,1,0:T(8,128)(2,1)} %scatter.4), calls=%async_computation.1 | async-start | bytes 786432 | tf_op jit(solution)/shard_map/all_to_all | solution.py:621
Sparse Core Ops, SparseCore 0:
  12.4 83.4 all-gather.2

commit v2 on v1

v2 whole, which is shorter than its diff:
```python
import functools

import jax
import jax.numpy as jnp
from jax import lax
from jax.experimental import pallas as pl
from jax.experimental.pallas import tpu as pltpu
from jax.experimental.layout import Layout, with_layout_constraint
from jax.sharding import Mesh, PartitionSpec as P

SCORED = 8
PATCH = 14
HEADS = 8
HD = 80
GROUP = 4
LOSS_SCALE = 16384.0
SMOOTH = 0.01

TILE = ("chip", "core")
CH = 96
COLS = 112
SPANS = CH // 8
OUT_ROWS = 27 * 16
NT = 8
NZ = 4
PACK = 1120
CYCLE = [
    (2 * chip + core) * NZ + z
    for chip, heights in ((0, (0, 1, 2, 3)), (1, (3, 2, 1, 0)), (3, (0, 1, 2, 3)), (2, (3, 2, 1, 0)))
    for z in heights
    for core in range(2)
]
PLACES = [[CYCLE.index(i * NZ + z) for z in range(NZ)] for i in range(NT)]
KIN = 896
D = 1280
NTOK = 128
F32 = jnp.float32
BF16 = jnp.bfloat16


def lane_iota(rows):
    return lax.broadcasted_iota(jnp.int32, (rows, 128), 1)


def sub_iota(rows):
    return lax.broadcasted_iota(jnp.int32, (rows, 128), 0)


def channels_of(raw, at, group, sample):
    start = 8 + 14 * group + sample
    here = raw[at, pl.ds(start, 8, stride=2), :]
    before = raw[at, pl.ds(start - 2, 8, stride=2), :]
    joined = jnp.where(lane_iota(8) < 128 - 16 * sub_iota(8), here, before)
    return pltpu.roll(joined, 0, 1, stride=16, stride_axis=0)


def tiles_of(value):
    turned = jnp.take_along_axis(value, (lane_iota(8) + 16 * sub_iota(8)) % 128, axis=1)
    return jnp.where(lane_iota(8) < COLS - 16 * sub_iota(8), turned, pltpu.roll(turned, 7, 0))


def banded(weight_ref, taps, row_block, transposed):
    taps[...] = jnp.zeros(taps.shape, F32)
    for a in range(3):
        for b in range(3):
            for e in range(3):
                for o in range(3):
                    at = (a * 3 + e) * 3 + o
                    taps[b, at : at + 1, :] = weight_ref[a, b, e, o : o + 1, :].astype(F32)
    inner = row_block * CH
    pick = (
        lax.broadcasted_iota(jnp.int32, (OUT_ROWS, 32), 0) // 16
        == lax.broadcasted_iota(jnp.int32, (OUT_ROWS, 32), 1)
    ).astype(BF16)
    if transposed:
        shape, p_dim, r_dim = (inner, OUT_ROWS), 1, 0
        grow_shape, grow_dim = (inner, CH), 0
    else:
        shape, p_dim, r_dim = (OUT_ROWS, inner), 0, 1
        grow_shape, grow_dim = (CH, inner), 1
    at = lax.broadcasted_iota(jnp.int32, grow_shape, grow_dim)
    at = at - CH * ((at.astype(F32) + 0.5) * (1.0 / CH)).astype(jnp.int32)
    grow = (at == lax.broadcasted_iota(jnp.int32, grow_shape, 1 - grow_dim)).astype(BF16)
    p_at = lax.broadcasted_iota(jnp.int32, shape, p_dim) % 16
    r_at = lax.broadcasted_iota(jnp.int32, shape, r_dim)
    r_at = ((r_at.astype(F32) + 0.5) * (1.0 / CH)).astype(jnp.int32)
    total = jnp.zeros(shape, F32)
    for b in range(3):
        rows = jnp.dot(pick, taps[b].astype(BF16), preferred_element_type=F32).astype(BF16)
        if transposed:
            full = lax.dot_general(
                grow, rows, (((1,), (1,)), ((), ())), preferred_element_type=F32
            )
        else:
            full = jnp.dot(rows, grow, preferred_element_type=F32)
        total = jnp.where(p_at == r_at + 2 - b, full, total)
    return total.astype(BF16)


def half_gains(gain_ref):
    rows = jnp.concatenate([gain_ref[0:1, :], jnp.zeros((1, 128 - CH), F32)], axis=1)
    return 0.5 * jnp.broadcast_to(rows, (128, 128)).T


def entry_of(pick_ref, sample, frame):
    found = jnp.int32(-1)
    for j in range(SCORED):
        found = jnp.where(pick_ref[sample, j] == frame, jnp.int32(j), found)
    return found


def decode_kernel(row_block, pick_ref, x_ref, gain_ref, weight_ref, out_ref, band, taps, gains, raw, operand, acc, final):
    t = pl.program_id(0)
    blocks = x_ref.shape[1] // row_block
    rows = out_ref.shape[3]

    @pl.when(t == 0)
    def _():
        band[...] = banded(weight_ref, taps, row_block, False)
        gains[...] = half_gains(gain_ref)
        acc[...] = jnp.zeros(acc.shape, F32)
        raw[...] = jnp.zeros(raw.shape, F32)

    for k in range(blocks):

        def one_row(row, at):
            raw[at, 8:176, :] = x_ref[0, k * row_block + row].astype(F32)
            for s in range(2):
                found = [channels_of(raw, at, g, s) for g in range(SPANS)]
                square = found[0] * found[0]
                for g in range(1, SPANS):
                    square = square + found[g] * found[g]
                second = jnp.sum(square, axis=0, keepdims=True) * (1.0 / CH)
                inv = lax.rsqrt(second + 1e-06)
                for m in range(SPANS // 2):
                    acts = []
                    for g in (2 * m, 2 * m + 1):
                        half = found[g] * inv * gains[8 * g : 8 * g + 8, :]
                        acts.append(half + half * jnp.tanh(half))
                    start = row * CH + 16 * m
                    operand[k, start : start + 16, 128 * s : 128 * s + 128] = jnp.concatenate(
                        acts, axis=0
                    ).astype(BF16)

        for row in range(row_block):
            one_row(row, row)
        spread = jnp.dot(band[...], operand[k], preferred_element_type=F32)
        lane = lane_iota(48)
        for s in range(2):
            part = spread[:, 128 * s : 128 * s + 128]
            for a in range(3):
                low, mid, high = (part[144 * a + 48 * e : 144 * a + 48 * e + 48] for e in range(3))
                low = jnp.where(lane == 0, 0.0, pltpu.roll(low, 1, 1))
                high = jnp.where(lane == COLS - 1, 0.0, pltpu.roll(high, 127, 1))
                acc[k, 2 - a, s] += low + mid + high

    keep = lane_iota(rows) < COLS
    for s in range(2):
        entry = entry_of(pick_ref, s, t)

        @pl.when(entry >= 0)
        def _():
            for o in range(3):
                final[...] = jnp.zeros(final.shape, F32)
                for k in range(blocks):
                    start = k * row_block
                    final[start : start + 16, :] += acc[k, 0, s, 16 * o : 16 * o + 16, :]
                out_ref[jnp.maximum(entry, 0), s, o] = jnp.where(keep, final[0:rows, :], 0.0).astype(BF16)

    for k in range(blocks):
        acc[k, 0] = acc[k, 1]
        acc[k, 1] = acc[k, 2]
        acc[k, 2] = jnp.zeros(acc.shape[2:], F32)


def restore_kernel(row_block, pick_ref, scale_ref, x_ref, gain_ref, weight_ref, grad_ref, out_ref, band, taps, gains, raw, back, shifted, coming):
    t = pl.program_id(0)
    frames = pl.num_programs(0)
    blocks = x_ref.shape[1] // row_block
    rows = grad_ref.shape[3]

    @pl.when(t == 0)
    def _():
        band[...] = banded(weight_ref, taps, row_block, True)
        gains[...] = half_gains(gain_ref)
        raw[...] = jnp.zeros(raw.shape, F32)
        shifted[...] = jnp.zeros(shifted.shape, BF16)
        lane = lane_iota(rows)

        def one_frame(frame, carry):
            for s in range(2):
                entry = entry_of(pick_ref, s, frame)
                scale = jnp.where(entry >= 0, scale_ref[s], 0.0)
                source = jnp.maximum(entry, 0)
                for o in range(3):
                    value = grad_ref[source, s, o].astype(F32) * scale
                    value = jnp.where(lane < COLS, value, 0.0)
                    for e, moved in enumerate((pltpu.roll(value, 127, 1), value, pltpu.roll(value, 1, 1))):
                        for k in range(blocks):
                            start = k * row_block
                            shifted[frame, k, 48 * e + 16 * o : 48 * e + 16 * o + 16, 128 * s : 128 * s + 128] = moved[
                                start : start + 16
                            ].astype(BF16)
            return carry

        lax.fori_loop(0, frames, one_frame, 0)

    for k in range(blocks):
        operand = jnp.concatenate([shifted[t + 2 - a, k] for a in range(3)], axis=0)
        coming[k] = jnp.dot(band[...], operand, preferred_element_type=F32)

        def one_row(row, at):
            raw[at, 8:176, :] = x_ref[0, k * row_block + row].astype(F32)
            for s in range(2):
                found = [channels_of(raw, at, g, s) for g in range(SPANS)]
                square = found[0] * found[0]
                for g in range(1, SPANS):
                    square = square + found[g] * found[g]
                inv = lax.rsqrt(jnp.sum(square, axis=0, keepdims=True) * (1.0 / CH) + 1e-06)
                outs, total = [], None
                for g in range(SPANS):
                    gain = gains[8 * g : 8 * g + 8, :]
                    half = found[g] * inv * gain
                    th = jnp.tanh(half)
                    start = row * CH + 8 * g
                    cot = coming[k, start : start + 8, 128 * s : 128 * s + 128]
                    out = cot * gain * (1.0 + th) * (1.0 + half * (1.0 - th))
                    outs.append(out)
                    total = out * found[g] if g == 0 else total + out * found[g]
                factor = jnp.sum(total, axis=0, keepdims=True) * (1.0 / CH) * inv * inv * inv
                for g in range(SPANS):
                    result = tiles_of(outs[g] * inv - found[g] * factor)
                    back[at, pl.ds(14 * g + s, 7, stride=2), :] = result[0:7]
            out_ref[0, k * row_block + row] = back[at].astype(BF16)

        for row in range(row_block):
            one_row(row, row)


def nt_dot(one, two):
    return lax.dot_general(one, two, (((1,), (1,)), ((), ())), preferred_element_type=F32)


def tn_dot(one, two):
    return lax.dot_general(one, two, (((0,), (0,)), ((), ())), preferred_element_type=F32)


def nn_dot(one, two):
    return jnp.dot(one, two, preferred_element_type=F32)


def split_two(value):
    high = value.astype(BF16)
    low = (value - high.astype(F32)).astype(BF16)
    return jnp.concatenate([high, low], axis=0)


def reward_kernel(
    row_count, tiles, samples,
    part_ref, packed_ref, head_ref,
    out_ref, score_ref,
    pack, arrived, frame, flip, embed, outw, place, patches, tokens, normed, normed16, slots, weights, dslots, dnormed, rows8, abar,
):
    height = row_count * tiles
    patch_rows = height // PATCH
    lane64 = lane_iota(8) < 64
    lane = lane_iota(NTOK)
    count = samples * NTOK

    copy = pltpu.make_async_copy(packed_ref, pack, arrived)
    copy.start()

    flip[...] = jnp.zeros(flip.shape, F32)
    for f in range(samples):
        frame[...] = jnp.zeros(frame.shape, F32)
        for i in range(tiles):
            at = row_count * i + 7
            for o in range(3):
                frame[o, at : at + row_count + 2, :] += part_ref[i, f, o, 0 : row_count + 2, :].astype(F32)
        for pair in range(patch_rows // 2):
            for local in range(2):
                at = 8 + PATCH * (2 * pair + local)
                for o in range(3):
                    flip[0, 64 * local + PATCH * o : 64 * local + PATCH * o + PATCH, :] = (
                        frame[o, at : at + PATCH, :].astype(BF16).astype(F32)
                    )
            flip[1] = flip[0].T
            token = f * NTOK + pair * 16
            for y in range(PATCH // 2):
                even = flip[1, pl.ds(2 * y, 8, stride=PATCH), :]
                odd = flip[1, pl.ds(2 * y + 1, 8, stride=PATCH), :]
                patches[token : token + 8, 128 * y : 128 * y + 128] = jnp.where(lane64, even, pltpu.roll(odd, 64, 1))
                patches[token + 8 : token + 16, 128 * y : 128 * y + 128] = jnp.where(lane64, pltpu.roll(even, 64, 1), odd)

    copy.wait()

    embed[...] = jnp.zeros(embed.shape, BF16)
    lane96 = lane_iota(96)
    for z in range(NZ):
        for i in range(NT):
            source = pack.at[PLACES[i][z]]
            for xx in range(4):
                x = 4 * z + xx
                if x < PATCH:
                    embed[64 * x : 64 * x + 48, 128 * i : 128 * i + 128] = source[640 + 48 * xx : 688 + 48 * xx, :]
            outw[160 * z : 160 * z + 160, 128 * i : 128 * i + 128] = source[832:992, :]
            place[32 * z : 32 * z + 32, 128 * i : 128 * i + 128] = source[992:1024, :]
        for ib in range(2):
            sources = [pack[PLACES[4 * ib + j][z], 1024:1120, :].astype(F32) for j in range(4)]
            rolled = [[sources[j] if d == 0 else pltpu.roll(sources[j], 32 * d, 1) for d in range(4)] for j in range(4)]
            at = 1024 + 128 * ib
            for q in range(4):
                found = rolled[0][(0 - q) % 4]
                for j in range(1, 4):
                    found = jnp.where(lane96 >= 32 * j, rolled[j][(j - q) % 4], found)
                found = found.astype(BF16)
                if q < 2:
                    for xx in range(2):
                        x = 4 * z + 2 * q + xx
                        if x < PATCH:
                            embed[64 * x : 64 * x + 48, at : at + 128] = found[48 * xx : 48 * xx + 48]
                elif q == 2:
                    outw[160 * z : 160 * z + 96, at : at + 128] = found
                else:
                    outw[160 * z + 96 : 160 * z + 160, at : at + 128] = found[:64]
                    place[32 * z : 32 * z + 32, at : at + 128] = found[64:96]

    token_value = nn_dot(patches[...].astype(BF16), embed[...])
    rows8[...] = jnp.zeros(rows8.shape, F32)
    abar[...] = jnp.zeros(abar.shape, F32)
    place_value = place[...].astype(F32)
    for f in range(samples):
        value = token_value[f * NTOK : f * NTOK + NTOK] + place_value
        rows8[0, f : f + 1, :] = jnp.mean(value, axis=0, keepdims=True)
        centered = value - jnp.mean(value, axis=-1, keepdims=True)
        scale = lax.rsqrt(jnp.mean(centered * centered, axis=-1, keepdims=True) + 1e-05)
        value = centered * scale
        normed[f * NTOK : f * NTOK + NTOK, :] = value
        normed16[f * NTOK : f * NTOK + NTOK, :] = value.astype(BF16)
        tokens[f * NTOK : f * NTOK + NTOK, :] = jnp.broadcast_to(scale, (NTOK, 128))

    def weight_part(i, z):
        source = pack.at[PLACES[i][z]]
        return jnp.concatenate([source[0:256, :], source[320:576, :]], axis=1)

    def weight_rest(i):
        return jnp.concatenate(
            [
                jnp.concatenate([pack[PLACES[i][z], 256:320, :], pack[PLACES[i][z], 576:640, :]], axis=1)
                for z in range(NZ)
            ],
            axis=0,
        )

    lane_all = lane_iota(count)
    for i in range(NT):
        mixed = nn_dot(normed16[:, 1024:1280], weight_rest(i))
        for z in range(NZ):
            mixed = mixed + nn_dot(normed16[:, 256 * z : 256 * z + 256], weight_part(i, z))
        first, second = mixed[:, 0:128], mixed[:, 128:256]
        found = (
            first,
            jnp.where(lane_all < 48, pltpu.roll(first, 48, 1), pltpu.roll(second, 48, 1)),
            pltpu.roll(second, 96, 1),
        )
        for m in range(3):
            slots[3 * i + m] = jnp.where(lane_all < HD, found[m], 0.0).astype(BF16)

    for h in range(HEADS):
        for f in range(samples):
            span = slice(f * NTOK, f * NTOK + NTOK)
            logits = nt_dot(slots[h, span, :], slots[HEADS + h, span, :]) * HD ** (-0.5)
            logits = jnp.exp(logits - jnp.max(logits, axis=-1, keepdims=True))
            prob = logits / jnp.sum(logits, axis=-1, keepdims=True)
            weights[h * samples + f] = prob
            attended = nn_dot(prob.astype(BF16), slots[2 * HEADS + h, span, :]).astype(BF16)
            abar[h, f : f + 1, :] = jnp.mean(attended.astype(F32), axis=0, keepdims=True)

    pooled = rows8[0]
    for h in range(HEADS):
        part = nn_dot(split_two(abar[h])[:, 0:HD], outw[HD * h : HD * h + HD, :])
        pooled = pooled + part[0:8] + part[8:16]
    pooled = pooled - jnp.mean(pooled, axis=-1, keepdims=True)
    scale = lax.rsqrt(jnp.mean(pooled * pooled, axis=-1, keepdims=True) + 1e-05)
    pooled = pooled * scale
    head = head_ref[...]
    score_ref[...] = jnp.broadcast_to(jnp.sum(pooled * head, axis=-1, keepdims=True), (8, 128))
    dpooled = scale * (
        head - jnp.mean(head, axis=-1, keepdims=True) - pooled * jnp.mean(pooled * head, axis=-1, keepdims=True)
    )
    dres = dpooled * (1.0 / NTOK)
    rows8[1] = dres
    dres_two = split_two(dres)

    for h in range(HEADS):
        datt = nt_dot(dres_two, outw[HD * h : HD * h + HD, :])
        datt = (datt[0:8] + datt[8:16]).astype(BF16)
        datt = jnp.concatenate([datt, jnp.zeros((8, 128 - HD), BF16)], axis=1)
        for f in range(samples):
            span = slice(f * NTOK, f * NTOK + NTOK)
            prob = weights[h * samples + f]
            row = datt[f : f + 1, :]
            dweight = nt_dot(datt, slots[2 * HEADS + h, span, :])[f : f + 1, :].astype(BF16).astype(F32)
            inner = jnp.sum(prob * dweight, axis=-1, keepdims=True)
            dlogit = (prob * (dweight - inner) * HD ** (-0.5)).astype(BF16)
            dslots[h, span, :] = nn_dot(dlogit, slots[HEADS + h, span, :])
            dslots[HEADS + h, span, :] = tn_dot(dlogit, slots[h, span, :])
            dslots[2 * HEADS + h, span, :] = tn_dot(
                prob.astype(BF16), jnp.broadcast_to(row.astype(F32), (NTOK, 128)).astype(BF16)
            )

    dnormed[...] = jnp.zeros(dnormed.shape, F32)
    for i in range(NT):
        one, two, three = dslots[3 * i], dslots[3 * i + 1], dslots[3 * i + 2]
        two = pltpu.roll(two, 80, 1)
        three = pltpu.roll(three, 32, 1)
        first = jnp.where(lane_all < HD, one, two)
        second = jnp.where(lane_all < 32, two, jnp.where(lane_all < COLS, three, 0.0))
        dmixed = jnp.concatenate([first, second], axis=1).astype(BF16)
        for z in range(NZ):
            dnormed[:, 256 * z : 256 * z + 256] += nt_dot(dmixed, weight_part(i, z))
        dnormed[:, 1024:1280] += nt_dot(dmixed, weight_rest(i))

    for f in range(samples):
        span = slice(f * NTOK, f * NTOK + NTOK)
        value, dvalue = normed[span, :], dnormed[span, :]
        scale = tokens[span, 0:1]
        dvalue = scale * (
            dvalue
            - jnp.mean(dvalue, axis=-1, keepdims=True)
            - value * jnp.mean(dvalue * value, axis=-1, keepdims=True)
        )
        normed16[span, :] = (dvalue + rows8[1, f : f + 1, :]).astype(BF16)
    patches[...] = nt_dot(normed16[...], embed[...])

    frame[...] = jnp.zeros(frame.shape, F32)
    rows = out_ref.shape[3]
    flip[...] = jnp.zeros(flip.shape, F32)
    for f in range(samples):
        for pair in range(patch_rows // 2):
            token = f * NTOK + pair * 16
            for y in range(PATCH // 2):
                one = patches[token : token + 8, 128 * y : 128 * y + 128]
                two = patches[token + 8 : token + 16, 128 * y : 128 * y + 128]
                flip[1, pl.ds(2 * y, 8, stride=PATCH), :] = jnp.where(lane64, one, pltpu.roll(two, 64, 1))
                flip[1, pl.ds(2 * y + 1, 8, stride=PATCH), :] = jnp.where(lane64, pltpu.roll(one, 64, 1), two)
            flip[0] = flip[1].T
            for local in range(2):
                at = 8 + PATCH * (2 * pair + local)
                for o in range(3):
                    frame[o, at : at + PATCH, :] = flip[0, 64 * local + PATCH * o : 64 * local + PATCH * o + PATCH, :]
        for i in range(tiles):
            at = row_count * i + 7
            for o in range(3):
                out_ref[i, f, o] = frame[o, at : at + rows, :].astype(BF16)


def pack_part(rows_in, embed_part, out_part, place_part):
    ordered = jnp.concatenate([rows_in[0:128], rows_in[160:288], rows_in[128:160], rows_in[288:320]], axis=0)
    upper = jnp.pad(ordered[:, 128:240], ((0, 0), (0, 16)))
    other = jnp.concatenate([embed_part, out_part, place_part], axis=0)
    rest = other[:, 128:160].reshape(4, 96, 32)
    rest = jnp.concatenate([rest[q] for q in range(4)], axis=1)
    return jnp.concatenate([ordered[:, 0:128], upper, other[:, 0:128], rest], axis=0)


def pack_kernel(z_ref, rows_ref, embed_ref, out_ref, place_ref, packed_ref):
    for source, target, count in ((0, 0, 128), (160, 128, 128), (128, 256, 32), (288, 288, 32)):
        packed_ref[target : target + count, :] = rows_ref[source : source + count, 0:128]
        packed_ref[320 + target : 320 + target + count, :] = jnp.concatenate(
            [rows_ref[source : source + count, 128:240], jnp.zeros((count, 16), BF16)], axis=1
        )
    packed_ref[832:992, :] = out_ref[:, 0:128]
    packed_ref[992:1024, :] = place_ref[:, 0:128]
    width = embed_ref.shape[1]
    pixel = lax.broadcasted_iota(jnp.int32, (48, width), 0)
    lane = lax.broadcasted_iota(jnp.int32, (48, width), 1)
    parts = []
    for local in range(4):
        x = 4 * z_ref[0] + local
        hit = (lane == pixel * PATCH + x) & (pixel < 3 * PATCH) & (x < PATCH)
        parts.append(nt_dot(hit.astype(BF16), embed_ref[...]))
    embed_part = jnp.concatenate(parts, axis=0)
    packed_ref[640:832, :] = embed_part[:, 0:128].astype(BF16)
    tail = out_ref[:, 128:160].astype(F32)
    last = place_ref[:, 128:160].astype(F32)
    packed_ref[1024:1120, :] = jnp.concatenate(
        [
            embed_part[0:96, 128:160],
            embed_part[96:192, 128:160],
            tail[0:96],
            jnp.concatenate([tail[96:160], last], axis=0),
        ],
        axis=1,
    ).astype(BF16)


def embed_rows(patch_embed):
    columns = patch_embed.shape[1]
    ordered = patch_embed.reshape(3 * PATCH, PATCH, columns).transpose(1, 0, 2)
    ordered = jnp.pad(ordered, ((0, 16 - PATCH), (0, 48 - 3 * PATCH), (0, 0)))
    return ordered.reshape(16 * 48, columns)


def packed_weights(patch_embed, position, attend_in, attend_out):
    if lax.axis_size(TILE) == NT and lax.axis_size("sample") == NZ:
        z = lax.axis_index("sample").astype(jnp.int32).reshape(1)
        mine = pl.pallas_call(
            pack_kernel,
            in_specs=[pl.BlockSpec(memory_space=pltpu.SMEM)] + [pl.BlockSpec(memory_space=pltpu.VMEM)] * 4,
            out_shape=jax.ShapeDtypeStruct((PACK, 128), BF16),
            compiler_params=params(16),
            name="pack",
        )(z, attend_in, patch_embed.T, attend_out, position)
        return lax.all_gather(mine, TILE + ("sample",), axis=0, axis_index_groups=[CYCLE])

    def whole(value):
        value = lax.all_gather(value, "sample", axis=0, tiled=True)
        return lax.all_gather(value, TILE, axis=1, tiled=True)

    embed_full = embed_rows(lax.all_gather(patch_embed, TILE, axis=1, tiled=True))
    split = [
        value.reshape(NZ, value.shape[0] // NZ, NT, value.shape[1] // NT).transpose(2, 0, 1, 3)
        for value in (whole(attend_in), embed_full, whole(attend_out), whole(position))
    ]
    split = [value.reshape((NT * NZ,) + value.shape[2:])[jnp.array(CYCLE)] for value in split]
    return jax.vmap(pack_part)(*split)


def params(mib=48):
    return pltpu.CompilerParams(vmem_limit_bytes=mib * 1024 * 1024)


def local(
    features,
    norm_gain,
    conv_weight,
    patch_embed,
    position,
    attend_in,
    attend_out,
    reward_head,
    group_index,
    frame_pick,
):
    samples, frames, row_count, merged = features.shape
    tiles, parts = lax.axis_size(TILE), lax.axis_size("sample")
    sent_rows = -(-(row_count + 2) // 16) * 16
    row_block = row_count if row_count <= 14 else 14
    blocks = row_count // row_block
    inner = row_block * CH
    packed = packed_weights(patch_embed, position, attend_in, attend_out)
    order = Layout((1, 2, 3, 0, 4))
    split = (samples, frames, row_count, merged // 128, 128)
    view = with_layout_constraint(features.reshape(split), order).transpose(1, 2, 3, 0, 4)
    view = view.reshape(frames, row_count, samples * merged // 128, 128)
    gain = norm_gain[None, :]

    smem = pl.BlockSpec(memory_space=pltpu.SMEM)
    view_spec = pl.BlockSpec((1,) + view.shape[1:], lambda t: (t, 0, 0, 0))
    gain_spec = pl.BlockSpec((1, CH), lambda t: (0, 0))
    taps_spec = pl.BlockSpec((3, 3, 3, 3, CH), lambda t: (0, 0, 0, 0, 0))
    sent = (SCORED, samples, 3, sent_rows, 128)
    sent_spec = pl.BlockSpec(sent, lambda t: (0, 0, 0, 0, 0))
    decoded = pl.pallas_call(
        functools.partial(decode_kernel, row_block),
        grid=(frames,),
        in_specs=[smem, view_spec, gain_spec, taps_spec],
        out_specs=sent_spec,
        scratch_shapes=[
            pltpu.VMEM((OUT_ROWS, inner), BF16),
            pltpu.VMEM((3, 32, CH), F32),
            pltpu.VMEM((128, 128), F32),
            pltpu.VMEM((row_block, 192, 128), F32),
            pltpu.VMEM((blocks, inner, 256), BF16),
            pltpu.VMEM((blocks, 3, samples, 48, 128), F32),
            pltpu.VMEM((sent_rows + 16, 128), F32),
        ],
        out_shape=jax.ShapeDtypeStruct(sent, BF16),
        compiler_params=params(32),
        name="decode",
    )(frame_pick, view, gain, conv_weight)

    if tiles > SCORED:
        decoded = jnp.pad(decoded, ((0, tiles - SCORED),) + ((0, 0),) * 4)
    owned = lax.all_to_all(decoded, TILE, split_axis=0, concat_axis=0, tiled=True)

    head = reward_head.reshape(NT, D // NT)
    head = jnp.concatenate([head[:, :128].reshape(-1), head[:, 128:].reshape(-1)])[None, :]
    height = row_count * tiles
    count = samples * NTOK
    grads, scores = pl.pallas_call(
        functools.partial(reward_kernel, row_count, tiles, samples),
        out_shape=[
            jax.ShapeDtypeStruct((tiles, samples, 3, sent_rows, 128), BF16),
            jax.ShapeDtypeStruct((8, 128), F32),
        ],
        in_specs=[
            pl.BlockSpec(memory_space=pltpu.VMEM),
            pl.BlockSpec(memory_space=pl.ANY),
            pl.BlockSpec(memory_space=pltpu.VMEM),
        ],
        scratch_shapes=[
            pltpu.VMEM(packed.shape, BF16),
            pltpu.SemaphoreType.DMA,
            pltpu.VMEM((3, height + 48, 128), F32),
            pltpu.VMEM((2, 128, 128), F32),
            pltpu.VMEM((KIN, D), BF16),
            pltpu.VMEM((HEADS * HD, D), BF16),
            pltpu.VMEM((NTOK, D), BF16),
            pltpu.VMEM((count, KIN), F32),
            pltpu.VMEM((count, 128), F32),
            pltpu.VMEM((count, D), F32),
            pltpu.VMEM((count, D), BF16),
            pltpu.VMEM((3 * HEADS, count, 128), BF16),
            pltpu.VMEM((HEADS * samples, NTOK, NTOK), F32),
            pltpu.VMEM((3 * HEADS, count, 128), F32),
            pltpu.VMEM((count, D), F32),
            pltpu.VMEM((2, 8, D), F32),
            pltpu.VMEM((HEADS, 8, 128), F32),
        ],
        compiler_params=params(),
        name="reward",
    )(owned, packed, head)

    mine = jnp.concatenate([scores[:samples, 0], group_index.astype(F32)])
    gathered = [mine]
    for shift in range(1, parts):
        ring = [(z, (z + shift) % parts) for z in range(parts)]
        gathered.append(lax.ppermute(mine, "sample", ring))
    gathered = jnp.stack(gathered)
    groups = gathered[:, samples:].reshape(-1)
    score_row = gathered[:, :samples].reshape(-1)
    high = score_row.astype(BF16)
    low = score_row - high.astype(F32)
    mid = low.astype(BF16)
    low = (low - mid.astype(F32)).astype(BF16)
    total = parts * samples
    carried = jnp.concatenate([high, mid, low])
    grads = grads.at[:, 0, 0, sent_rows - 1, 0 : 3 * total].set(
        jnp.broadcast_to(carried, (tiles, 3 * total))
    )
    returned = lax.all_to_all(grads, TILE, split_axis=0, concat_axis=0, tiled=True)
    returned = returned[:SCORED]

    got = returned[:, 0, 0, sent_rows - 1, 0 : 3 * total].astype(F32).reshape(SCORED, 3, total)
    entry_scores = got[:, 0] + (got[:, 1] + got[:, 2])
    rewards = jnp.sum(entry_scores, axis=0) / SCORED
    member = (groups[:samples, None] == groups[None, :]).astype(F32)
    mean_group = jnp.sum(member * rewards[None, :], axis=1) / GROUP
    second_group = jnp.sum(member * (rewards * rewards)[None, :], axis=1) / GROUP - mean_group * mean_group
    advantage = (rewards[:samples] - mean_group) * lax.rsqrt(second_group + SMOOTH)
    cotangent = -LOSS_SCALE * advantage / SCORED

    result = pl.pallas_call(
        functools.partial(restore_kernel, row_block),
        grid=(frames,),
        in_specs=[smem, smem, view_spec, gain_spec, taps_spec, sent_spec],
        out_specs=view_spec,
        scratch_shapes=[
            pltpu.VMEM((inner, OUT_ROWS), BF16),
            pltpu.VMEM((3, 32, CH), F32),
            pltpu.VMEM((128, 128), F32),
            pltpu.VMEM((row_block, 192, 128), F32),
            pltpu.VMEM((row_block, samples * merged // 128, 128), F32),
            pltpu.VMEM((frames + 2, blocks, 144, 256), BF16),
            pltpu.VMEM((blocks, inner, 256), F32),
        ],
        out_shape=jax.ShapeDtypeStruct(view.shape, BF16),
        compiler_params=params(),
        name="restore",
    )(frame_pick, cotangent, view, gain, conv_weight, returned)
    result = result.reshape(frames, row_count, merged // 128, samples, 128).transpose(3, 0, 1, 2, 4)
    return with_layout_constraint(result, order).reshape(features.shape)


def solution(mesh):
    tiles, parts = mesh.devices.shape
    split = Mesh(mesh.devices.reshape(tiles // 2, 2, parts), ("chip", "core", "sample"))
    in_specs = (
        P("sample", None, TILE, None),
        P(),
        P(),
        P(None, TILE),
        P("sample", TILE),
        P("sample", TILE),
        P("sample", TILE),
        P(),
        P("sample"),
        P("sample", None),
    )
    out_specs = P("sample", None, TILE, None)
    return jax.shard_map(local, mesh=split, in_specs=in_specs, out_specs=out_specs, check_vma=False)
```

time: 204 us -> 175 us (0.86)
  local copies, waits for them, and re-layouts: 37.7 us -> 11.7 us
  other arithmetic: 4.55 us -> 0.44 us
  Pallas kernels: 83.5 us -> 86.8 us
    pallas_call x1 -> x0, local copies, waits for them, and re-layouts: 19.4 us -> none  [local(): pl.pallas_call(functools.partial(restore_kernel, row_count), grid_spec=pl...]
    all_gather x1, waiting for transfers between devices: 30.5 us -> 25.7 us  [packed_weights(): lax.all_gather(mine, TILE + ('sample',), axis=0, axis_index_groups=[CYCLE])]
    pallas_call x2 -> x3, Pallas kernels: 60 us -> 63.9 us  [the longest x1 40.7 us: local(): pl.pallas_call(functools.partial(restore_kernel, row_block), grid=(frames...]
    all_to_all x2, waiting for transfers between devices: 16 us -> 19.7 us  [the longest x1 11.8 us: local(): lax.all_to_all(decoded, TILE, split_axis=0, concat_axis=0, tiled=True)]
    unnamed x7 -> x26, local copies, waits for them, and re-layouts: 12.2 us -> 9.64 us
    slice x8 -> x0, local copies, waits for them, and re-layouts: 2.54 us -> none  [the longest x1 0.88 us: pack_part(): rows_in[0:128]]
  transfers between devices with their start and end apart: 6 -> 6, of which waited for: 5 -> 6; matrix products, arithmetic and copies ran while one was open for 7% -> 0% of each run, Pallas kernels for 12% -> 13%
where the time goes in v2:
time: 175 us
  Pallas kernels  86.8 us (50%)
  waiting for transfers between devices  49.9 us (29%)
  between operations  13.5 us (8%)
  starting transfers between devices  12.5 us (7%)
  local copies, waits for them, and re-layouts  11.7 us (7%)
    pallas_call x1, Pallas kernels, local(): pl.pallas_call(functools.partial(restore_kernel, row_block), grid=(frames...  40.7 us
    all_gather x1, waiting for transfers between devices, packed_weights(): lax.all_gather(mine, TILE + ('sample',), axis=0, axis_index_groups=[CYCLE])  25.7 us
    pallas_call x1, Pallas kernels, local(): pl.pallas_call(functools.partial(reward_kernel, row_count, tiles, samples...  23 us
    pallas_call x1, Pallas kernels, local(): pl.pallas_call(functools.partial(decode_kernel, row_block), grid=(frames,...  22 us
    all_to_all x1, waiting for transfers between devices, local(): lax.all_to_all(decoded, TILE, split_axis=0, concat_axis=0, tiled=True)  11.8 us
    unnamed x26, local copies, waits for them, and re-layouts  9.64 us
    all_to_all x1, waiting for transfers between devices, local(): lax.all_to_all(grads, TILE, split_axis=0, concat_axis=0, tiled=True)  7.9 us
    all_to_all x1, starting transfers between devices, local(): lax.all_to_all(decoded, TILE, split_axis=0, concat_axis=0, tiled=True)  5.17 us
  transfers between devices with their start and end apart: 6, of which 6 were waited for; matrix products, arithmetic and copies ran while one was open for 0% of the time, Pallas kernels for 13%

profile of v2, /device:TPU:0, one launch (start us, length us, event | category | flops | bytes accessed | tf_op | source)
XLA Modules:
  0.0 174.8 jit_solution(9876048304249886322)
XLA Ops:
  6.5 0.0 copy-start.12
  6.5 0.0 copy-start.11
  6.5 0.0 all-gather.3.cloned.1.call-start
  6.5 0.0 copy-start.1
  6.5 1.0 copy-done.1
  7.5 0.0 copy-start.2
  7.5 0.9 copy-done.2
  8.4 0.0 copy-start.5
  8.4 0.9 copy-done.5
  9.3 0.0 copy-start.6
  9.3 0.7 copy-done.6
  10.0 1.2 pack.1
  11.2 0.0 all-gather.3.cloned.1.call-update
  11.3 0.0 copy-start
  11.3 4.1 %copy-done = bf16[2,9,28,10752]{3,0,2,1:T(2,128)(2,1)S(1)} copy-done((bf16[2,9,28,10752]{3,0,2,1:T(2,128)(2,1)S(1)}, bf16[2,9,28,10752]{3,0,2,1:T(2,128)(2,1)}, u32[]{:S(2)}) %copy-start) | copy-done | bytes 10838040
  15.3 0.0 copy-start.3
  15.3 0.7 copy-done.3
  16.1 0.0 copy-start.7
  16.1 0.7 copy-done.7
  16.8 0.0 copy-start.9
  16.8 0.7 copy-done.9
  17.4 0.0 copy-start.4
  17.4 0.0 copy-start.8
  17.4 0.0 copy-start.10
  17.4 22.0 %decode.1 = bf16[8,2,3,32,128]{4,3,2,1,0:T(8,128)(2,1)} custom-call(s32[2,8]{1,0:T(2,128)S(1)} %copy-done.7, bf16[9,28,168,128]{3,2,1,0:T(8,128)(2,1)S(1)} %bitcast.23, f32[1,96]{1,0:T(1,128)S(1)} %bitcast.25, bf16[3,3,3,3,96]{4,3,2,1,0:T(4,128)(2,1)S(1)} %copy-done.3), custom_call_target="tpu_custom_call" | custom-call | tf_op jit(solution)/shard_map/decode/pallas_call | solution.py:565
  39.4 5.2 %all-to-all-start = ((bf16[8,2,3,32,128]{4,3,2,1,0:T(8,128)(2,1)}), bf16[8,2,3,32,128]{4,3,2,1,0:T(8,128)(2,1)S(1)}, u32[]{:S(2)}, u32[]{:S(2)}) async-start(bf16[8,2,3,32,128]{4,3,2,1,0:T(8,128)(2,1)} %decode.1), calls=%async_computation | async-start | bytes 786432 | tf_op jit(solution)/shard_map/all_to_all | solution.py:586
  44.6 0.0 copy-done.12
  44.6 0.0 copy-done.11
  44.6 0.1 reshape.86
  44.7 0.1 reshape.88
  44.8 11.8 %all-to-all-done.part_ref = bf16[8,2,3,32,128]{4,3,2,1,0:T(8,128)(2,1)S(1)} async-done(((bf16[8,2,3,32,128]{4,3,2,1,0:T(8,128)(2,1)}), bf16[8,2,3,32,128]{4,3,2,1,0:T(8,128)(2,1)S(1)}, u32[]{:S(2)}, u32[]{:S(2)}) %all-to-all-start) | async-done | bytes 393248 | tf_op jit(solution)/shard_map/all_to_all | solution.py:586
  56.6 25.7 %all-gather.3.cloned.1.call-done = bf16[35840,128]{1,0:T(8,128)(2,1)} async-done(((bf16[1120,128]{1,0:T(8,128)(2,1)}), bf16[35840,128]{1,0:T(8,128)(2,1)}) %all-gather.3.cloned.1.call-update) | async-done | bytes 9175056 | tf_op jit(solution)/shard_map/all_gather | solution.py:515
  82.4 23.0 %reward.1 = (bf16[8,2,3,32,128]{4,3,2,1,0:T(8,128)(2,1)}, f32[8,128]{1,0:T(8,128)S(1)}) custom-call(bf16[8,2,3,32,128]{4,3,2,1,0:T(8,128)(2,1)S(1)} %all-to-all-done.part_ref, bf16[32,1120,128]{2,1,0:T(8,128)(2,1)} %bitcast.27, f32[1,1280]{1,0:T(1,128)S(1)} %broadcast_in_dim.5.head_ref), custom_call_target="tpu_custom_call" | custom-call | tf_op jit(solution)/shard_map/reward/pallas_call | solution.py:592
  105.3 0.1 slice_reduce_fusion
  105.5 0.1 pad_maximum_fusion.2
  105.5 2.4 %collective-permute-start.2 = (f32[4]{0:T(128)S(1)}, f32[4]{0:T(128)S(1)}, u32[]{:S(2)}, u32[]{:S(2)}) collective-permute-start(f32[4]{0:T(128)S(1)} %pad_maximum_fusion.2), channel_id=1, source_target_pairs={{0,3},{1,0},{2,1},{3,2},{4,7},{5,4},{6,5},{7,6},{8,11},{9,8},{10,9... | collective-permute-start | bytes 56 | tf_op jit(solution)/shard_map/ppermute | solution.py:630
  108.0 0.3 collective-permute-start.1
  108.2 0.9 collective-permute-start
  109.2 0.1 collective-permute-done.2
  109.3 3.1 %collective-permute-done.1 = f32[4]{0:T(128)S(1)} collective-permute-done((f32[4]{0:T(128)S(1)}, f32[4]{0:T(128)S(1)}, u32[]{:S(2)}, u32[]{:S(2)}) %collective-permute-start.1) | collective-permute-done | bytes 48 | tf_op jit(solution)/shard_map/ppermute | solution.py:630
  112.4 1.2 collective-permute-done
  113.6 0.1 fusion.7
  113.6 0.1 reshape.89
  113.7 0.1 pad_maximum_fusion.3
  113.8 1.4 scatter.4
  115.2 3.7 %all-to-all-start.1 = ((bf16[8,2,3,32,128]{4,3,2,1,0:T(8,128)(2,1)}), bf16[8,2,3,32,128]{4,3,2,1,0:T(8,128)(2,1)S(1)}, u32[]{:S(2)}, u32[]{:S(2)}) async-start(bf16[8,2,3,32,128]{4,3,2,1,0:T(8,128)(2,1)} %scatter.4), calls=%async_computation.1 | async-start | bytes 786432 | tf_op jit(solution)/shard_map/all_to_all | solution.py:643
  118.9 0.1 slice_bitcast_fusion.1
  119.0 0.1 eq.19
  119.1 7.9 %all-to-all-done.1.grad_ref = bf16[8,2,3,32,128]{4,3,2,1,0:T(8,128)(2,1)S(1)} async-done(((bf16[8,2,3,32,128]{4,3,2,1,0:T(8,128)(2,1)}), bf16[8,2,3,32,128]{4,3,2,1,0:T(8,128)(2,1)S(1)}, u32[]{:S(2)}, u32[]{:S(2)}) %all-to-all-start.1) | async-done | bytes 393248 | tf_op jit(solution)/shard_map/all_to_all | solution.py:643
  127.0 0.1 reshape.92
  127.1 0.2 fusion.3
  127.3 0.0 copy-done.4
  127.3 0.0 copy-done.8
  127.3 0.0 copy-done.10
  127.3 40.7 %restore.1 = bf16[9,28,168,128]{3,2,1,0:T(8,128)(2,1)} custom-call(s32[2,8]{1,0:T(2,128)S(1)} %copy-done.8, f32[2]{0:T(128)S(1)} %multiply_multiply_fusion.scale_ref, bf16[9,28,168,128]{3,2,1,0:T(8,128)(2,1)} %bitcast.22, f32[1,96]{1,0:T(1,128)S(1)} %bitcast.26, bf16[3,3,3,3,96]{4,3,2,1,0:T(4,128)(2,1)S(1)} %copy-done.4, ...), custom_call_target="tpu_custom_call" | custom-call | tf_op jit(solution)/shard_map/restore/pallas_call | solution.py:655
  (12 shorter events, 0.1 us)
Async XLA Ops:
  6.5 38.1 %copy-start.12 = (s32[2]{0:T(128)S(1)}, s32[2]{0:T(128)}, u32[]{:S(2)}) copy-start(s32[2]{0:T(128)} %param.20) | copy-start | bytes 28
  6.5 38.1 %copy-start.11 = (f32[1280]{0:T(1024)S(1)}, f32[1280]{0:T(1024)}, u32[]{:S(2)}) copy-start(f32[1280]{0:T(1024)} %param.19) | copy-start | bytes 15364
  6.5 75.8 %all-gather.3.cloned.1.call-start = ((), (), s32[]{:S(2)}) async-start(), calls=%async_computation.2 | async-start | bytes 9461760 | tf_op jit(solution)/shard_map/all_gather | solution.py:515
  6.5 1.0 copy-start.1
  7.5 0.9 copy-start.2
  8.4 0.9 copy-start.5
  9.3 0.7 copy-start.6
  11.3 4.1 %copy-start = (bf16[2,9,28,10752]{3,0,2,1:T(2,128)(2,1)S(1)}, bf16[2,9,28,10752]{3,0,2,1:T(2,128)(2,1)}, u32[]{:S(2)}) copy-start(bf16[2,9,28,10752]{3,0,2,1:T(2,128)(2,1)} %param.12) | copy-start | bytes 32514052
  15.3 0.7 copy-start.3
  16.1 0.7 copy-start.7
  16.8 0.7 copy-start.9
  17.4 109.9 %copy-start.4 = (bf16[3,3,3,3,96]{4,3,2,1,0:T(4,128)(2,1)S(1)}, bf16[3,3,3,3,96]{4,3,2,1,0:T(4,128)(2,1)}, u32[]{:S(2)}) copy-start(bf16[3,3,3,3,96]{4,3,2,1,0:T(4,128)(2,1)} %weight_ref.3) | copy-start | bytes 46660
  17.4 109.9 %copy-start.8 = (s32[2,8]{1,0:T(2,128)S(1)}, s32[2,8]{1,0:T(2,128)}, u32[]{:S(2)}) copy-start(s32[2,8]{1,0:T(2,128)} %pick_ref.3) | copy-start | bytes 196
  17.4 109.9 %copy-start.10 = (f32[96]{0:T(128)S(1)}, f32[96]{0:T(128)}, u32[]{:S(2)}) copy-start(f32[96]{0:T(128)} %param.13) | copy-start | bytes 1156
  39.4 17.2 %all-to-all-start = ((bf16[8,2,3,32,128]{4,3,2,1,0:T(8,128)(2,1)}), bf16[8,2,3,32,128]{4,3,2,1,0:T(8,128)(2,1)S(1)}, u32[]{:S(2)}, u32[]{:S(2)}) async-start(bf16[8,2,3,32,128]{4,3,2,1,0:T(8,128)(2,1)} %decode.1), calls=%async_computation | async-start | bytes 786432 | tf_op jit(solution)/shard_map/all_to_all | solution.py:586
  105.5 3.7 %collective-permute-start.2 = (f32[4]{0:T(128)S(1)}, f32[4]{0:T(128)S(1)}, u32[]{:S(2)}, u32[]{:S(2)}) collective-permute-start(f32[4]{0:T(128)S(1)} %pad_maximum_fusion.2), channel_id=1, source_target_pairs={{0,3},{1,0},{2,1},{3,2},{4,7},{5,4},{6,5},{7,6},{8,11},{9,8},{10,9... | collective-permute-start | bytes 56 | tf_op jit(solution)/shard_map/ppermute | solution.py:630
  108.0 4.4 %collective-permute-start.1 = (f32[4]{0:T(128)S(1)}, f32[4]{0:T(128)S(1)}, u32[]{:S(2)}, u32[]{:S(2)}) collective-permute-start(f32[4]{0:T(128)S(1)} %pad_maximum_fusion.2), channel_id=1, source_target_pairs={{0,2},{1,3},{2,0},{3,1},{4,6},{5,7},{6,4},{7,5},{8,10},{9,11},{10,... | collective-permute-start | bytes 56 | tf_op jit(solution)/shard_map/ppermute | solution.py:630
  108.2 5.3 %collective-permute-start = (f32[4]{0:T(128)S(1)}, f32[4]{0:T(128)S(1)}, u32[]{:S(2)}, u32[]{:S(2)}) collective-permute-start(f32[4]{0:T(128)S(1)} %pad_maximum_fusion.2), channel_id=1, source_target_pairs={{0,1},{1,2},{2,3},{3,0},{4,5},{5,6},{6,7},{7,4},{8,9},{9,10},{10,1... | collective-permute-start | bytes 56 | tf_op jit(solution)/shard_map/ppermute | solution.py:630
  115.2 11.7 %all-to-all-start.1 = ((bf16[8,2,3,32,128]{4,3,2,1,0:T(8,128)(2,1)}), bf16[8,2,3,32,128]{4,3,2,1,0:T(8,128)(2,1)S(1)}, u32[]{:S(2)}, u32[]{:S(2)}) async-start(bf16[8,2,3,32,128]{4,3,2,1,0:T(8,128)(2,1)} %scatter.4), calls=%async_computation.1 | async-start | bytes 786432 | tf_op jit(solution)/shard_map/all_to_all | solution.py:643
Sparse Core Ops, SparseCore 0:
  11.4 70.9 all-gather.2

commit v3 on v2

--- a/solution.py
+++ b/solution.py
@@ -23,7 +23,7 @@
 OUT_ROWS = 27 * 16
 NT = 8
 NZ = 4
-PACK = 1120
+PACK = 880
 CYCLE = [
     (2 * chip + core) * NZ + z
     for chip, heights in ((0, (0, 1, 2, 3)), (1, (3, 2, 1, 0)), (3, (0, 1, 2, 3)), (2, (3, 2, 1, 0)))
@@ -109,7 +109,7 @@
     return found
 
 
-def decode_kernel(row_block, pick_ref, x_ref, gain_ref, weight_ref, out_ref, band, taps, gains, raw, operand, acc, final):
+def decode_kernel(row_block, pick_ref, x_ref, gain_ref, weight_ref, out_ref, x_out, inv_out, band, taps, gains, raw, operand, acc, final):
     t = pl.program_id(0)
     blocks = x_ref.shape[1] // row_block
     rows = out_ref.shape[3]
@@ -132,7 +132,11 @@
                     square = square + found[g] * found[g]
                 second = jnp.sum(square, axis=0, keepdims=True) * (1.0 / CH)
                 inv = lax.rsqrt(second + 1e-06)
+                inv_out[0, k * row_block + row, s : s + 1, :] = inv
                 for m in range(SPANS // 2):
+                    x_out[0, k * row_block + row, s, 16 * m : 16 * m + 16, :] = jnp.concatenate(
+                        [found[2 * m], found[2 * m + 1]], axis=0
+                    ).astype(BF16)
                     acts = []
                     for g in (2 * m, 2 * m + 1):
                         half = found[g] * inv * gains[8 * g : 8 * g + 8, :]
@@ -173,7 +177,7 @@
         acc[k, 2] = jnp.zeros(acc.shape[2:], F32)
 
 
-def restore_kernel(row_block, pick_ref, scale_ref, x_ref, gain_ref, weight_ref, grad_ref, out_ref, band, taps, gains, raw, back, shifted, coming):
+def restore_kernel(row_block, pick_ref, scale_ref, x_ref, inv_ref, gain_ref, weight_ref, grad_ref, out_ref, band, taps, gains, back, shifted, coming):
     t = pl.program_id(0)
     frames = pl.num_programs(0)
     blocks = x_ref.shape[1] // row_block
@@ -183,7 +187,6 @@
     def _():
         band[...] = banded(weight_ref, taps, row_block, True)
         gains[...] = half_gains(gain_ref)
-        raw[...] = jnp.zeros(raw.shape, F32)
         shifted[...] = jnp.zeros(shifted.shape, BF16)
         lane = lane_iota(rows)
 
@@ -210,26 +213,26 @@
         coming[k] = jnp.dot(band[...], operand, preferred_element_type=F32)
 
         def one_row(row, at):
-            raw[at, 8:176, :] = x_ref[0, k * row_block + row].astype(F32)
             for s in range(2):
-                found = [channels_of(raw, at, g, s) for g in range(SPANS)]
-                square = found[0] * found[0]
-                for g in range(1, SPANS):
-                    square = square + found[g] * found[g]
-                inv = lax.rsqrt(jnp.sum(square, axis=0, keepdims=True) * (1.0 / CH) + 1e-06)
-                outs, total = [], None
+                inv = inv_ref[0, k * row_block + row, s : s + 1, :]
+                outs, units, total = [], [], None
+                for m in range(SPANS // 2):
+                    pair = x_ref[0, k * row_block + row, s, 16 * m : 16 * m + 16, :].astype(F32)
+                    for local in range(2):
+                        g = 2 * m + local
+                        unit = pair[8 * local : 8 * local + 8] * inv
+                        gain = gains[8 * g : 8 * g + 8, :]
+                        half = unit * gain
+                        th = jnp.tanh(half)
+                        start = row * CH + 8 * g
+                        cot = coming[k, start : start + 8, 128 * s : 128 * s + 128]
+                        out = cot * gain * (1.0 + th) * (1.0 + half * (1.0 - th))
+                        outs.append(out)
+                        units.append(unit)
+                        total = out * unit if g == 0 else total + out * unit
+                factor = jnp.sum(total, axis=0, keepdims=True) * (1.0 / CH)
                 for g in range(SPANS):
-                    gain = gains[8 * g : 8 * g + 8, :]
-                    half = found[g] * inv * gain
-                    th = jnp.tanh(half)
-                    start = row * CH + 8 * g
-                    cot = coming[k, start : start + 8, 128 * s : 128 * s + 128]
-                    out = cot * gain * (1.0 + th) * (1.0 + half * (1.0 - th))
-                    outs.append(out)
-                    total = out * found[g] if g == 0 else total + out * found[g]
-                factor = jnp.sum(total, axis=0, keepdims=True) * (1.0 / CH) * inv * inv * inv
-                for g in range(SPANS):
-                    result = tiles_of(outs[g] * inv - found[g] * factor)
+                    result = tiles_of((outs[g] - units[g] * factor) * inv)
                     back[at, pl.ds(14 * g + s, 7, stride=2), :] = result[0:7]
             out_ref[0, k * row_block + row] = back[at].astype(BF16)
 
@@ -257,9 +260,9 @@
 
 def reward_kernel(
     row_count, tiles, samples,
-    part_ref, packed_ref, head_ref,
+    part_ref, embed_ref, packed_ref, head_ref,
     out_ref, score_ref,
-    pack, arrived, frame, flip, embed, outw, place, patches, tokens, normed, normed16, slots, weights, dslots, dnormed, rows8, abar,
+    pack, arrived, frame, flip, embed, outw, place, patches, tokens, normed, normed16, slots, weights, dslots, dnormed, rows8, abar, order,
 ):
     height = row_count * tiles
     patch_rows = height // PATCH
@@ -270,62 +273,66 @@
     copy = pltpu.make_async_copy(packed_ref, pack, arrived)
     copy.start()
 
+    inputs = 3 * PATCH * PATCH
+    for i in range(NT):
+        embed[128 * i : 128 * i + 128, :] = embed_ref[i, 0:128, :]
+        embed[1024 + 32 * i : 1056 + 32 * i, :] = embed_ref[i, 128:160, :]
+    pixel = lax.broadcasted_iota(jnp.int32, (64, inputs), 0)
+    column = lax.broadcasted_iota(jnp.int32, (64, inputs), 1)
+    for x in range(PATCH):
+        order[64 * x : 64 * x + 64, :] = (
+            (column == pixel * PATCH + x) & (pixel < 3 * PATCH)
+        ).astype(BF16)
+
     flip[...] = jnp.zeros(flip.shape, F32)
+    frame[...] = jnp.zeros(frame.shape, F32)
     for f in range(samples):
-        frame[...] = jnp.zeros(frame.shape, F32)
         for i in range(tiles):
             at = row_count * i + 7
             for o in range(3):
-                frame[o, at : at + row_count + 2, :] += part_ref[i, f, o, 0 : row_count + 2, :].astype(F32)
+                frame[f, o, at : at + row_count + 2, :] += part_ref[i, f, o, 0 : row_count + 2, :].astype(F32)
+    for f in range(samples):
         for pair in range(patch_rows // 2):
+            turn = flip.at[f * (patch_rows // 2) + pair]
             for local in range(2):
                 at = 8 + PATCH * (2 * pair + local)
                 for o in range(3):
-                    flip[0, 64 * local + PATCH * o : 64 * local + PATCH * o + PATCH, :] = (
-                        frame[o, at : at + PATCH, :].astype(BF16).astype(F32)
+                    turn[0, 64 * local + PATCH * o : 64 * local + PATCH * o + PATCH, :] = (
+                        frame[f, o, at : at + PATCH, :].astype(BF16).astype(F32)
                     )
-            flip[1] = flip[0].T
+            turn[1] = turn[0].T
             token = f * NTOK + pair * 16
             for y in range(PATCH // 2):
-                even = flip[1, pl.ds(2 * y, 8, stride=PATCH), :]
-                odd = flip[1, pl.ds(2 * y + 1, 8, stride=PATCH), :]
+                even = turn[1, pl.ds(2 * y, 8, stride=PATCH), :]
+                odd = turn[1, pl.ds(2 * y + 1, 8, stride=PATCH), :]
                 patches[token : token + 8, 128 * y : 128 * y + 128] = jnp.where(lane64, even, pltpu.roll(odd, 64, 1))
                 patches[token + 8 : token + 16, 128 * y : 128 * y + 128] = jnp.where(lane64, pltpu.roll(even, 64, 1), odd)
 
     copy.wait()
 
-    embed[...] = jnp.zeros(embed.shape, BF16)
-    lane96 = lane_iota(96)
+    lane48 = lane_iota(48)
     for z in range(NZ):
         for i in range(NT):
             source = pack.at[PLACES[i][z]]
-            for xx in range(4):
-                x = 4 * z + xx
-                if x < PATCH:
-                    embed[64 * x : 64 * x + 48, 128 * i : 128 * i + 128] = source[640 + 48 * xx : 688 + 48 * xx, :]
-            outw[160 * z : 160 * z + 160, 128 * i : 128 * i + 128] = source[832:992, :]
-            place[32 * z : 32 * z + 32, 128 * i : 128 * i + 128] = source[992:1024, :]
+            outw[160 * z : 160 * z + 160, 128 * i : 128 * i + 128] = source[640:800, :]
+            place[32 * z : 32 * z + 32, 128 * i : 128 * i + 128] = source[800:832, :]
         for ib in range(2):
-            sources = [pack[PLACES[4 * ib + j][z], 1024:1120, :].astype(F32) for j in range(4)]
+            sources = [pack[PLACES[4 * ib + j][z], 832:880, :].astype(F32) for j in range(4)]
             rolled = [[sources[j] if d == 0 else pltpu.roll(sources[j], 32 * d, 1) for d in range(4)] for j in range(4)]
             at = 1024 + 128 * ib
             for q in range(4):
                 found = rolled[0][(0 - q) % 4]
                 for j in range(1, 4):
-                    found = jnp.where(lane96 >= 32 * j, rolled[j][(j - q) % 4], found)
+                    found = jnp.where(lane48 >= 32 * j, rolled[j][(j - q) % 4], found)
                 found = found.astype(BF16)
-                if q < 2:
-                    for xx in range(2):
-                        x = 4 * z + 2 * q + xx
-                        if x < PATCH:
-                            embed[64 * x : 64 * x + 48, at : at + 128] = found[48 * xx : 48 * xx + 48]
-                elif q == 2:
-                    outw[160 * z : 160 * z + 96, at : at + 128] = found
+                if q < 3:
+                    outw[160 * z + 48 * q : 160 * z + 48 * q + 48, at : at + 128] = found
                 else:
-                    outw[160 * z + 96 : 160 * z + 160, at : at + 128] = found[:64]
-                    place[32 * z : 32 * z + 32, at : at + 128] = found[64:96]
-
-    token_value = nn_dot(patches[...].astype(BF16), embed[...])
+                    outw[160 * z + 144 : 160 * z + 160, at : at + 128] = found[:16]
+                    place[32 * z : 32 * z + 32, at : at + 128] = found[16:48]
+
+    patches16 = nn_dot(patches[...].astype(BF16), order[...]).astype(BF16)
+    token_value = nt_dot(patches16, embed[...])
     rows8[...] = jnp.zeros(rows8.shape, F32)
     abar[...] = jnp.zeros(abar.shape, F32)
     place_value = place[...].astype(F32)
@@ -354,9 +361,9 @@
 
     lane_all = lane_iota(count)
     for i in range(NT):
-        mixed = nn_dot(normed16[:, 1024:1280], weight_rest(i))
-        for z in range(NZ):
-            mixed = mixed + nn_dot(normed16[:, 256 * z : 256 * z + 256], weight_part(i, z))
+        mixed = nn_dot(
+            normed16[...], jnp.concatenate([weight_part(i, z) for z in range(NZ)] + [weight_rest(i)], axis=0)
+        )
         first, second = mixed[:, 0:128], mixed[:, 128:256]
         found = (
             first,
@@ -409,17 +416,20 @@
                 prob.astype(BF16), jnp.broadcast_to(row.astype(F32), (NTOK, 128)).astype(BF16)
             )
 
-    dnormed[...] = jnp.zeros(dnormed.shape, F32)
+    parts = []
     for i in range(NT):
         one, two, three = dslots[3 * i], dslots[3 * i + 1], dslots[3 * i + 2]
         two = pltpu.roll(two, 80, 1)
         three = pltpu.roll(three, 32, 1)
         first = jnp.where(lane_all < HD, one, two)
         second = jnp.where(lane_all < 32, two, jnp.where(lane_all < COLS, three, 0.0))
-        dmixed = jnp.concatenate([first, second], axis=1).astype(BF16)
-        for z in range(NZ):
-            dnormed[:, 256 * z : 256 * z + 256] += nt_dot(dmixed, weight_part(i, z))
-        dnormed[:, 1024:1280] += nt_dot(dmixed, weight_rest(i))
+        parts += [first.astype(BF16), second.astype(BF16)]
+    dmixed = jnp.concatenate(parts, axis=1)
+    for z in range(NZ):
+        wide = jnp.concatenate([weight_part(i, z) for i in range(NT)], axis=1)
+        dnormed[:, 256 * z : 256 * z + 256] = nt_dot(dmixed, wide)
+    wide = jnp.concatenate([weight_rest(i) for i in range(NT)], axis=1)
+    dnormed[:, 1024:1280] = nt_dot(dmixed, wide)
 
     for f in range(samples):
         span = slice(f * NTOK, f * NTOK + NTOK)
@@ -431,103 +441,86 @@
             - value * jnp.mean(dvalue * value, axis=-1, keepdims=True)
         )
         normed16[span, :] = (dvalue + rows8[1, f : f + 1, :]).astype(BF16)
-    patches[...] = nt_dot(normed16[...], embed[...])
+    patches[...] = nt_dot(nn_dot(normed16[...], embed[...]).astype(BF16), order[...])
 
     frame[...] = jnp.zeros(frame.shape, F32)
     rows = out_ref.shape[3]
-    flip[...] = jnp.zeros(flip.shape, F32)
     for f in range(samples):
         for pair in range(patch_rows // 2):
+            turn = flip.at[f * (patch_rows // 2) + pair]
             token = f * NTOK + pair * 16
             for y in range(PATCH // 2):
                 one = patches[token : token + 8, 128 * y : 128 * y + 128]
                 two = patches[token + 8 : token + 16, 128 * y : 128 * y + 128]
-                flip[1, pl.ds(2 * y, 8, stride=PATCH), :] = jnp.where(lane64, one, pltpu.roll(two, 64, 1))
-                flip[1, pl.ds(2 * y + 1, 8, stride=PATCH), :] = jnp.where(lane64, pltpu.roll(one, 64, 1), two)
-            flip[0] = flip[1].T
+                turn[1, pl.ds(2 * y, 8, stride=PATCH), :] = jnp.where(lane64, one, pltpu.roll(two, 64, 1))
+                turn[1, pl.ds(2 * y + 1, 8, stride=PATCH), :] = jnp.where(lane64, pltpu.roll(one, 64, 1), two)
+            turn[0] = turn[1].T
             for local in range(2):
                 at = 8 + PATCH * (2 * pair + local)
                 for o in range(3):
-                    frame[o, at : at + PATCH, :] = flip[0, 64 * local + PATCH * o : 64 * local + PATCH * o + PATCH, :]
+                    frame[f, o, at : at + PATCH, :] = turn[0, 64 * local + PATCH * o : 64 * local + PATCH * o + PATCH, :]
+    for f in range(samples):
         for i in range(tiles):
             at = row_count * i + 7
             for o in range(3):
-                out_ref[i, f, o] = frame[o, at : at + rows, :].astype(BF16)
-
-
-def pack_part(rows_in, embed_part, out_part, place_part):
+                out_ref[i, f, o] = frame[f, o, at : at + rows, :].astype(BF16)
+
+
+def pack_part(rows_in, out_part, place_part):
     ordered = jnp.concatenate([rows_in[0:128], rows_in[160:288], rows_in[128:160], rows_in[288:320]], axis=0)
     upper = jnp.pad(ordered[:, 128:240], ((0, 0), (0, 16)))
-    other = jnp.concatenate([embed_part, out_part, place_part], axis=0)
-    rest = other[:, 128:160].reshape(4, 96, 32)
+    other = jnp.concatenate([out_part, place_part], axis=0)
+    rest = other[:, 128:160].reshape(4, 48, 32)
     rest = jnp.concatenate([rest[q] for q in range(4)], axis=1)
     return jnp.concatenate([ordered[:, 0:128], upper, other[:, 0:128], rest], axis=0)
 
 
-def pack_kernel(z_ref, rows_ref, embed_ref, out_ref, place_ref, packed_ref):
+def pack_kernel(rows_ref, out_ref, place_ref, packed_ref):
     for source, target, count in ((0, 0, 128), (160, 128, 128), (128, 256, 32), (288, 288, 32)):
         packed_ref[target : target + count, :] = rows_ref[source : source + count, 0:128]
         packed_ref[320 + target : 320 + target + count, :] = jnp.concatenate(
             [rows_ref[source : source + count, 128:240], jnp.zeros((count, 16), BF16)], axis=1
         )
-    packed_ref[832:992, :] = out_ref[:, 0:128]
-    packed_ref[992:1024, :] = place_ref[:, 0:128]
-    width = embed_ref.shape[1]
-    pixel = lax.broadcasted_iota(jnp.int32, (48, width), 0)
-    lane = lax.broadcasted_iota(jnp.int32, (48, width), 1)
-    parts = []
-    for local in range(4):
-        x = 4 * z_ref[0] + local
-        hit = (lane == pixel * PATCH + x) & (pixel < 3 * PATCH) & (x < PATCH)
-        parts.append(nt_dot(hit.astype(BF16), embed_ref[...]))
-    embed_part = jnp.concatenate(parts, axis=0)
-    packed_ref[640:832, :] = embed_part[:, 0:128].astype(BF16)
+    packed_ref[640:800, :] = out_ref[:, 0:128]
+    packed_ref[800:832, :] = place_ref[:, 0:128]
     tail = out_ref[:, 128:160].astype(F32)
     last = place_ref[:, 128:160].astype(F32)
-    packed_ref[1024:1120, :] = jnp.concatenate(
-        [
-            embed_part[0:96, 128:160],
-            embed_part[96:192, 128:160],
-            tail[0:96],
-            jnp.concatenate([tail[96:160], last], axis=0),
-        ],
+    packed_ref[832:880, :] = jnp.concatenate(
+        [tail[0:48], tail[48:96], tail[96:144], jnp.concatenate([tail[144:160], last], axis=0)],
         axis=1,
     ).astype(BF16)
 
 
-def embed_rows(patch_embed):
-    columns = patch_embed.shape[1]
-    ordered = patch_embed.reshape(3 * PATCH, PATCH, columns).transpose(1, 0, 2)
-    ordered = jnp.pad(ordered, ((0, 16 - PATCH), (0, 48 - 3 * PATCH), (0, 0)))
-    return ordered.reshape(16 * 48, columns)
-
-
-def packed_weights(patch_embed, position, attend_in, attend_out):
+def packed_weights(position, attend_in, attend_out):
     if lax.axis_size(TILE) == NT and lax.axis_size("sample") == NZ:
-        z = lax.axis_index("sample").astype(jnp.int32).reshape(1)
         mine = pl.pallas_call(
             pack_kernel,
-            in_specs=[pl.BlockSpec(memory_space=pltpu.SMEM)] + [pl.BlockSpec(memory_space=pltpu.VMEM)] * 4,
             out_shape=jax.ShapeDtypeStruct((PACK, 128), BF16),
-            compiler_params=params(16),
+            compiler_params=params(),
             name="pack",
-        )(z, attend_in, patch_embed.T, attend_out, position)
+        )(attend_in, attend_out, position)
         return lax.all_gather(mine, TILE + ("sample",), axis=0, axis_index_groups=[CYCLE])
 
     def whole(value):
         value = lax.all_gather(value, "sample", axis=0, tiled=True)
         return lax.all_gather(value, TILE, axis=1, tiled=True)
 
-    embed_full = embed_rows(lax.all_gather(patch_embed, TILE, axis=1, tiled=True))
     split = [
         value.reshape(NZ, value.shape[0] // NZ, NT, value.shape[1] // NT).transpose(2, 0, 1, 3)
-        for value in (whole(attend_in), embed_full, whole(attend_out), whole(position))
+        for value in (whole(attend_in), whole(attend_out), whole(position))
     ]
     split = [value.reshape((NT * NZ,) + value.shape[2:])[jnp.array(CYCLE)] for value in split]
     return jax.vmap(pack_part)(*split)
 
 
-def params(mib=48):
+def embed_parts(patch_embed):
+    tiles = lax.axis_size(TILE)
+    copies = jnp.broadcast_to(patch_embed.T[None], (tiles,) + patch_embed.shape[::-1])
+    found = lax.all_to_all(copies, TILE, split_axis=0, concat_axis=0, tiled=True)
+    return found.reshape(NT, D // NT, patch_embed.shape[0])
+
+
+def params(mib=58):
     return pltpu.CompilerParams(vmem_limit_bytes=mib * 1024 * 1024)
 
 
@@ -549,7 +542,8 @@
     row_block = row_count if row_count <= 14 else 14
     blocks = row_count // row_block
     inner = row_block * CH
-    packed = packed_weights(patch_embed, position, attend_in, attend_out)
+    packed = packed_weights(position, attend_in, attend_out)
+    embed = embed_parts(patch_embed)
     order = Layout((1, 2, 3, 0, 4))
     split = (samples, frames, row_count, merged // 128, 128)
     view = with_layout_constraint(features.reshape(split), order).transpose(1, 2, 3, 0, 4)
@@ -562,11 +556,14 @@
     taps_spec = pl.BlockSpec((3, 3, 3, 3, CH), lambda t: (0, 0, 0, 0, 0))
     sent = (SCORED, samples, 3, sent_rows, 128)
     sent_spec = pl.BlockSpec(sent, lambda t: (0, 0, 0, 0, 0))
-    decoded = pl.pallas_call(
+    aligned = (frames, row_count, samples, CH, 128)
+    aligned_spec = pl.BlockSpec((1,) + aligned[1:], lambda t: (t, 0, 0, 0, 0))
+    inv_spec = pl.BlockSpec((1, row_count, samples, 128), lambda t: (t, 0, 0, 0))
+    decoded, x_aligned, inverse = pl.pallas_call(
         functools.partial(decode_kernel, row_block),
         grid=(frames,),
         in_specs=[smem, view_spec, gain_spec, taps_spec],
-        out_specs=sent_spec,
+        out_specs=[sent_spec, aligned_spec, inv_spec],
         scratch_shapes=[
             pltpu.VMEM((OUT_ROWS, inner), BF16),
             pltpu.VMEM((3, 32, CH), F32),
@@ -576,8 +573,12 @@
             pltpu.VMEM((blocks, 3, samples, 48, 128), F32),
             pltpu.VMEM((sent_rows + 16, 128), F32),
         ],
-        out_shape=jax.ShapeDtypeStruct(sent, BF16),
-        compiler_params=params(32),
+        out_shape=[
+            jax.ShapeDtypeStruct(sent, BF16),
+            jax.ShapeDtypeStruct(aligned, BF16),
+            jax.ShapeDtypeStruct((frames, row_count, samples, 128), F32),
+        ],
+        compiler_params=params(),
         name="decode",
     )(frame_pick, view, gain, conv_weight)
 
@@ -597,15 +598,16 @@
         ],
         in_specs=[
             pl.BlockSpec(memory_space=pltpu.VMEM),
+            pl.BlockSpec(memory_space=pltpu.VMEM),
             pl.BlockSpec(memory_space=pl.ANY),
             pl.BlockSpec(memory_space=pltpu.VMEM),
         ],
         scratch_shapes=[
             pltpu.VMEM(packed.shape, BF16),
             pltpu.SemaphoreType.DMA,
-            pltpu.VMEM((3, height + 48, 128), F32),
-            pltpu.VMEM((2, 128, 128), F32),
-            pltpu.VMEM((KIN, D), BF16),
+            pltpu.VMEM((samples, 3, height + 48, 128), F32),
+            pltpu.VMEM((samples * height // (2 * PATCH), 2, 128, 128), F32),
+            pltpu.VMEM((D, embed.shape[2]), BF16),
             pltpu.VMEM((HEADS * HD, D), BF16),
             pltpu.VMEM((NTOK, D), BF16),
             pltpu.VMEM((count, KIN), F32),
@@ -618,10 +620,11 @@
             pltpu.VMEM((count, D), F32),
             pltpu.VMEM((2, 8, D), F32),
             pltpu.VMEM((HEADS, 8, 128), F32),
+            pltpu.VMEM((KIN, embed.shape[2]), BF16),
         ],
         compiler_params=params(),
         name="reward",
-    )(owned, packed, head)
+    )(owned, embed, packed, head)
 
     mine = jnp.concatenate([scores[:samples, 0], group_index.astype(F32)])
     gathered = [mine]
@@ -655,13 +658,12 @@
     result = pl.pallas_call(
         functools.partial(restore_kernel, row_block),
         grid=(frames,),
-        in_specs=[smem, smem, view_spec, gain_spec, taps_spec, sent_spec],
+        in_specs=[smem, smem, aligned_spec, inv_spec, gain_spec, taps_spec, sent_spec],
         out_specs=view_spec,
         scratch_shapes=[
             pltpu.VMEM((inner, OUT_ROWS), BF16),
             pltpu.VMEM((3, 32, CH), F32),
             pltpu.VMEM((128, 128), F32),
-            pltpu.VMEM((row_block, 192, 128), F32),
             pltpu.VMEM((row_block, samples * merged // 128, 128), F32),
             pltpu.VMEM((frames + 2, blocks, 144, 256), BF16),
             pltpu.VMEM((blocks, inner, 256), F32),
@@ -669,7 +671,7 @@
         out_shape=jax.ShapeDtypeStruct(view.shape, BF16),
         compiler_params=params(),
         name="restore",
-    )(frame_pick, cotangent, view, gain, conv_weight, returned)
+    )(frame_pick, cotangent, x_aligned, inverse, gain, conv_weight, returned)
     result = result.reshape(frames, row_count, merged // 128, samples, 128).transpose(3, 0, 1, 2, 4)
     return with_layout_constraint(result, order).reshape(features.shape)
 

time: 175 us -> 176 us (level)
  blocking collectives: 0 us -> 16.4 us
  Pallas kernels: 86.8 us -> 79.5 us
  local copies, waits for them, and re-layouts: 11.7 us -> 4.63 us
    all_gather x1, waiting for transfers between devices: 25.7 us -> 5.85 us  [packed_weights(): lax.all_gather(mine, TILE + ('sample',), axis=0, axis_index_groups=[CYCLE])]
    all_to_all x1, waiting for transfers between devices: 11.8 us -> 29.7 us  [embed_parts(): lax.all_to_all(copies, TILE, split_axis=0, concat_axis=0, tiled=True)]
    all_to_all x0 -> x1, blocking collectives: none -> 16.4 us  [local(): lax.all_to_all(decoded, TILE, split_axis=0, concat_axis=0, tiled=True)]
    pallas_call x1, Pallas kernels: 40.7 us -> 30.1 us  [local(): pl.pallas_call(functools.partial(restore_kernel, row_block), grid=(frames...]
    unnamed x26 -> x10, local copies, waits for them, and re-layouts: 9.64 us -> 0.02 us
  transfers between devices with their start and end apart: 6 -> 6, of which waited for: 6 -> 6; matrix products, arithmetic and copies ran while one was open for 0% -> 1% of each run, Pallas kernels for 13% -> 14%
where the time goes in v3:
time: 176 us; the launch traced here: 175 us
  Pallas kernels  79.5 us (45%)
  waiting for transfers between devices  49.1 us (28%)
  blocking collectives  16.4 us (9%)
  between operations  13.5 us (8%)
  starting transfers between devices  11 us (6%)
  local copies, waits for them, and re-layouts  4.63 us (3%)
    pallas_call x1, Pallas kernels, local(): pl.pallas_call(functools.partial(restore_kernel, row_block), grid=(frames...  30.1 us
    all_to_all x1, waiting for transfers between devices, embed_parts(): lax.all_to_all(copies, TILE, split_axis=0, concat_axis=0, tiled=True)  29.7 us
    pallas_call x1, Pallas kernels, local(): pl.pallas_call(functools.partial(reward_kernel, row_count, tiles, samples...  23.9 us
    pallas_call x1, Pallas kernels, local(): pl.pallas_call(functools.partial(decode_kernel, row_block), grid=(frames,...  23.7 us
    all_to_all x1, blocking collectives, local(): lax.all_to_all(decoded, TILE, split_axis=0, concat_axis=0, tiled=True)  16.4 us
    all_to_all x1, waiting for transfers between devices, local(): lax.all_to_all(grads, TILE, split_axis=0, concat_axis=0, tiled=True)  8.19 us
    all_gather x1, waiting for transfers between devices, packed_weights(): lax.all_gather(mine, TILE + ('sample',), axis=0, axis_index_groups=[CYCLE])  5.85 us
    ppermute x3, waiting for transfers between devices, local(): gathered.append(lax.ppermute(mine, 'sample', ring))  5.33 us
  transfers between devices with their start and end apart: 6, of which 6 were waited for; matrix products, arithmetic and copies ran while one was open for 1% of the time, Pallas kernels for 14%

profile of v3, /device:TPU:0, one launch (start us, length us, event | category | flops | bytes accessed | tf_op | source)
XLA Modules:
  0.0 175.1 jit_solution(8718268389834703790)
XLA Ops:
  6.5 0.0 copy-start.2
  6.5 0.0 copy-start.4
  6.5 0.0 copy-start.3
  6.5 0.0 all-gather.3.cloned.1.call-start
  6.5 1.8 %pack.1 = bf16[880,128]{1,0:T(8,128)(2,1)} custom-call(bf16[320,240]{1,0:T(8,128)(2,1)} %rows_ref.1, bf16[160,160]{1,0:T(8,128)(2,1)} %out_ref.1, bf16[32,160]{1,0:T(8,128)(2,1)} %place_ref.1), custom_call_target="tpu_custom_call" | custom-call | tf_op jit(solution)/shard_map/pack/pallas_call | solution.py:496
  8.3 0.0 all-gather.3.cloned.1.call-update
  8.3 23.7 %decode.1 = (bf16[8,2,3,32,128]{4,3,2,1,0:T(8,128)(2,1)}, bf16[9,28,2,96,128]{4,3,2,1,0:T(8,128)(2,1)}, f32[9,28,2,128]{3,2,1,0:T(2,128)}) custom-call(s32[2,8]{1,0:T(2,128)} %pick_ref.3, bf16[9,28,168,128]{3,2,1,0:T(8,128)(2,1)} %bitcast.21, f32[1,96]{1,0:T(1,128)} %bitcast.24, bf16[3,3,3,3,96]{4,3,2,1,0:T(4,128)(2,1)} %weight_ref.3), custom_call_target="tpu_custom_call" | custom-call | tf_op jit(solution)/shard_map/decode/pallas_call | solution.py:562
  32.1 16.4 %all_to_all.15.part_ref = bf16[8,2,3,32,128]{4,3,2,1,0:T(8,128)(2,1)} all-to-all(bf16[8,2,3,32,128]{4,3,2,1,0:T(8,128)(2,1)} %get-tuple-element.22), channel_id=1, replica_groups=mesh['chip'=4,'core'=2,'sample'=4] {'chip','core'}, dimensions={0} | all-to-all | bytes 786432 | tf_op jit(solution)/shard_map/all_to_all | solution.py:587
  48.5 0.0 copy-done.2
  48.5 1.3 broadcast_in_dim.7
  49.8 3.8 %all-to-all-start.1 = ((bf16[8,160,588]{2,1,0:T(8,128)(2,1)}), bf16[8,160,588]{2,1,0:T(8,128)(2,1)S(1)}, u32[]{:S(2)}, u32[]{:S(2)}) async-start(bf16[8,160,588]{2,1,0:T(8,128)(2,1)} %broadcast_in_dim.7), calls=%async_computation.1 | async-start | bytes 3276800 | tf_op jit(solution)/shard_map/all_to_all | solution.py:519
  53.5 0.0 copy-done.4
  53.6 0.0 copy-done.3
  53.6 0.1 reshape.83
  53.7 0.1 reshape.85
  53.7 0.6 broadcast_in_dim.8.head_ref
  54.3 29.7 %all-to-all-done.1.embed_ref = bf16[8,160,588]{2,1,0:T(8,128)(2,1)S(1)} async-done(((bf16[8,160,588]{2,1,0:T(8,128)(2,1)}), bf16[8,160,588]{2,1,0:T(8,128)(2,1)S(1)}, u32[]{:S(2)}, u32[]{:S(2)}) %all-to-all-start.1) | async-done | bytes 1505312 | tf_op jit(solution)/shard_map/all_to_all | solution.py:519
  84.0 0.0 copy-start
  84.0 5.9 %all-gather.3.cloned.1.call-done = bf16[28160,128]{1,0:T(8,128)(2,1)} async-done(((bf16[880,128]{1,0:T(8,128)(2,1)}), bf16[28160,128]{1,0:T(8,128)(2,1)}) %all-gather.3.cloned.1.call-update) | async-done | bytes 7208976 | tf_op jit(solution)/shard_map/all_gather | solution.py:502
  89.9 0.0 copy-done
  89.9 23.9 %reward.1 = (bf16[8,2,3,32,128]{4,3,2,1,0:T(8,128)(2,1)}, f32[8,128]{1,0:T(8,128)}) custom-call(bf16[8,2,3,32,128]{4,3,2,1,0:T(8,128)(2,1)} %all_to_all.15.part_ref, bf16[8,160,588]{2,1,0:T(8,128)(2,1)} %copy-done, bf16[32,880,128]{2,1,0:T(8,128)(2,1)} %bitcast.22, f32[1,1280]{1,0:T(1,128)} %broadcast_in_dim.8.head_ref), custom_call_target="tpu_custom_call" | custom-call | tf_op jit(solution)/shard_map/reward/pallas_call | solution.py:593
  113.8 0.8 slice_reduce_fusion
  114.6 0.1 pad_maximum_fusion.2
  114.7 1.1 collective-permute-start.2
  115.7 2.1 %collective-permute-start.1 = (f32[4]{0:T(128)S(1)}, f32[4]{0:T(128)S(1)}, u32[]{:S(2)}, u32[]{:S(2)}) collective-permute-start(f32[4]{0:T(128)S(1)} %pad_maximum_fusion.2), channel_id=1, source_target_pairs={{0,2},{1,3},{2,0},{3,1},{4,6},{5,7},{6,4},{7,5},{8,10},{9,11},{10,... | collective-permute-start | bytes 56 | tf_op jit(solution)/shard_map/ppermute | solution.py:633
  117.9 0.0 collective-permute-start
  117.9 0.3 collective-permute-done.2
  118.2 2.0 %collective-permute-done.1 = f32[4]{0:T(128)S(1)} collective-permute-done((f32[4]{0:T(128)S(1)}, f32[4]{0:T(128)S(1)}, u32[]{:S(2)}, u32[]{:S(2)}) %collective-permute-start.1) | collective-permute-done | bytes 48 | tf_op jit(solution)/shard_map/ppermute | solution.py:633
  120.2 3.0 %collective-permute-done = f32[4]{0:T(128)S(1)} collective-permute-done((f32[4]{0:T(128)S(1)}, f32[4]{0:T(128)S(1)}, u32[]{:S(2)}, u32[]{:S(2)}) %collective-permute-start) | collective-permute-done | bytes 48 | tf_op jit(solution)/shard_map/ppermute | solution.py:633
  123.2 0.1 fusion.7
  123.3 0.1 reshape.86
  123.4 0.1 pad_maximum_fusion.3
  123.5 1.4 scatter.4
  124.8 4.0 %all-to-all-start.2 = ((bf16[8,2,3,32,128]{4,3,2,1,0:T(8,128)(2,1)}), bf16[8,2,3,32,128]{4,3,2,1,0:T(8,128)(2,1)S(1)}, u32[]{:S(2)}, u32[]{:S(2)}) async-start(bf16[8,2,3,32,128]{4,3,2,1,0:T(8,128)(2,1)} %scatter.4), calls=%async_computation.2 | async-start | bytes 786432 | tf_op jit(solution)/shard_map/all_to_all | solution.py:646
  128.8 0.1 slice_bitcast_fusion.1
  128.9 0.1 eq.19
  129.0 8.2 %all-to-all-done.2.grad_ref = bf16[8,2,3,32,128]{4,3,2,1,0:T(8,128)(2,1)S(1)} async-done(((bf16[8,2,3,32,128]{4,3,2,1,0:T(8,128)(2,1)}), bf16[8,2,3,32,128]{4,3,2,1,0:T(8,128)(2,1)S(1)}, u32[]{:S(2)}, u32[]{:S(2)}) %all-to-all-start.2) | async-done | bytes 393248 | tf_op jit(solution)/shard_map/all_to_all | solution.py:646
  137.2 0.0 copy-start.1
  137.2 0.1 reshape.89
  137.3 0.2 fusion.3
  137.5 0.6 multiply_multiply_fusion.scale_ref
  138.1 0.0 copy-done.1
  138.1 30.1 %restore.1 = bf16[9,28,168,128]{3,2,1,0:T(8,128)(2,1)} custom-call(s32[2,8]{1,0:T(2,128)} %pick_ref.3, f32[2]{0:T(128)} %multiply_multiply_fusion.scale_ref, bf16[9,28,2,96,128]{4,3,2,1,0:T(8,128)(2,1)} %get-tuple-element.25.x_ref, f32[9,28,2,128]{3,2,1,0:T(2,128)} %get-tuple-element.26.inv_ref, f32[1,96]{1,0:T(1,128)} %bitcast.25, ...), custom_call_target="tpu_custom_call" | custom-call | tf_op jit(solution)/shard_map/restore/pallas_call | solution.py:658
  (10 shorter events, 0.1 us)
Async XLA Ops:
  6.5 41.9 %copy-start.2 = (bf16[588,160]{0,1:T(8,128)(2,1)S(1)}, bf16[588,160]{0,1:T(8,128)(2,1)}, u32[]{:S(2)}) copy-start(bf16[588,160]{0,1:T(8,128)(2,1)} %param.15) | copy-start | bytes 564484
  6.5 47.0 %copy-start.4 = (s32[2]{0:T(128)S(1)}, s32[2]{0:T(128)}, u32[]{:S(2)}) copy-start(s32[2]{0:T(128)} %param.20) | copy-start | bytes 28
  6.5 47.0 %copy-start.3 = (f32[1280]{0:T(1024)S(1)}, f32[1280]{0:T(1024)}, u32[]{:S(2)}) copy-start(f32[1280]{0:T(1024)} %param.19) | copy-start | bytes 15364
  6.5 83.4 %all-gather.3.cloned.1.call-start = ((), (), s32[]{:S(2)}) async-start(), calls=%async_computation.3 | async-start | bytes 7434240 | tf_op jit(solution)/shard_map/all_gather | solution.py:502
  49.8 34.3 %all-to-all-start.1 = ((bf16[8,160,588]{2,1,0:T(8,128)(2,1)}), bf16[8,160,588]{2,1,0:T(8,128)(2,1)S(1)}, u32[]{:S(2)}, u32[]{:S(2)}) async-start(bf16[8,160,588]{2,1,0:T(8,128)(2,1)} %broadcast_in_dim.7), calls=%async_computation.1 | async-start | bytes 3276800 | tf_op jit(solution)/shard_map/all_to_all | solution.py:519
  84.0 5.9 %copy-start = (bf16[8,160,588]{2,1,0:T(8,128)(2,1)}, bf16[8,160,588]{2,1,0:T(8,128)(2,1)S(1)}, u32[]{:S(2)}) copy-start(bf16[8,160,588]{2,1,0:T(8,128)(2,1)S(1)} %all-to-all-done.1.embed_ref) | copy-start | bytes 4515844
  114.7 3.5 %collective-permute-start.2 = (f32[4]{0:T(128)S(1)}, f32[4]{0:T(128)S(1)}, u32[]{:S(2)}, u32[]{:S(2)}) collective-permute-start(f32[4]{0:T(128)S(1)} %pad_maximum_fusion.2), channel_id=1, source_target_pairs={{0,3},{1,0},{2,1},{3,2},{4,7},{5,4},{6,5},{7,6},{8,11},{9,8},{10,9... | collective-permute-start | bytes 56 | tf_op jit(solution)/shard_map/ppermute | solution.py:633
  115.7 4.4 %collective-permute-start.1 = (f32[4]{0:T(128)S(1)}, f32[4]{0:T(128)S(1)}, u32[]{:S(2)}, u32[]{:S(2)}) collective-permute-start(f32[4]{0:T(128)S(1)} %pad_maximum_fusion.2), channel_id=1, source_target_pairs={{0,2},{1,3},{2,0},{3,1},{4,6},{5,7},{6,4},{7,5},{8,10},{9,11},{10,... | collective-permute-start | bytes 56 | tf_op jit(solution)/shard_map/ppermute | solution.py:633
  117.9 5.3 %collective-permute-start = (f32[4]{0:T(128)S(1)}, f32[4]{0:T(128)S(1)}, u32[]{:S(2)}, u32[]{:S(2)}) collective-permute-start(f32[4]{0:T(128)S(1)} %pad_maximum_fusion.2), channel_id=1, source_target_pairs={{0,1},{1,2},{2,3},{3,0},{4,5},{5,6},{6,7},{7,4},{8,9},{9,10},{10,1... | collective-permute-start | bytes 56 | tf_op jit(solution)/shard_map/ppermute | solution.py:633
  124.8 12.3 %all-to-all-start.2 = ((bf16[8,2,3,32,128]{4,3,2,1,0:T(8,128)(2,1)}), bf16[8,2,3,32,128]{4,3,2,1,0:T(8,128)(2,1)S(1)}, u32[]{:S(2)}, u32[]{:S(2)}) async-start(bf16[8,2,3,32,128]{4,3,2,1,0:T(8,128)(2,1)} %scatter.4), calls=%async_computation.2 | async-start | bytes 786432 | tf_op jit(solution)/shard_map/all_to_all | solution.py:646
  137.2 0.9 copy-start.1
Sparse Core Ops, SparseCore 0:
  9.0 80.8 all-gather.2

commit v4 on v3

--- a/solution.py
+++ b/solution.py
@@ -23,14 +23,15 @@
 OUT_ROWS = 27 * 16
 NT = 8
 NZ = 4
-PACK = 880
+PACK = 1120
 CYCLE = [
-    (2 * chip + core) * NZ + z
+    (chip, z)
     for chip, heights in ((0, (0, 1, 2, 3)), (1, (3, 2, 1, 0)), (3, (0, 1, 2, 3)), (2, (3, 2, 1, 0)))
     for z in heights
-    for core in range(2)
 ]
-PLACES = [[CYCLE.index(i * NZ + z) for z in range(NZ)] for i in range(NT)]
+RINGS = (CYCLE, CYCLE[::-1])
+PLACES = [[RINGS[i % 2].index((i // 2, z)) for z in range(NZ)] for i in range(NT)]
+STARTS = (0, 48, 96, 112)
 KIN = 896
 D = 1280
 NTOK = 128
@@ -260,7 +261,7 @@
 
 def reward_kernel(
     row_count, tiles, samples,
-    part_ref, embed_ref, packed_ref, head_ref,
+    core_ref, part_ref, mine_ref, other_ref, head_ref,
     out_ref, score_ref,
     pack, arrived, frame, flip, embed, outw, place, patches, tokens, normed, normed16, slots, weights, dslots, dnormed, rows8, abar, order,
 ):
@@ -270,13 +271,21 @@
     lane = lane_iota(NTOK)
     count = samples * NTOK
 
-    copy = pltpu.make_async_copy(packed_ref, pack, arrived)
-    copy.start()
-
-    inputs = 3 * PATCH * PATCH
-    for i in range(NT):
-        embed[128 * i : 128 * i + 128, :] = embed_ref[i, 0:128, :]
-        embed[1024 + 32 * i : 1056 + 32 * i, :] = embed_ref[i, 128:160, :]
+    core = core_ref[0]
+    copies = []
+    for part, (begin, end) in enumerate(((880, 1120), (640, 880), (0, 640))):
+        copies.append(
+            [
+                pltpu.make_async_copy(
+                    source.at[:, begin:end, :], pack.at[at, :, begin:end, :], arrived.at[part, which]
+                )
+                for which, (source, at) in enumerate(((mine_ref, core), (other_ref, 1 - core)))
+            ]
+        )
+        for copy in copies[-1]:
+            copy.start()
+
+    inputs = order.shape[1]
     pixel = lax.broadcasted_iota(jnp.int32, (64, inputs), 0)
     column = lax.broadcasted_iota(jnp.int32, (64, inputs), 1)
     for x in range(PATCH):
@@ -308,16 +317,29 @@
                 patches[token : token + 8, 128 * y : 128 * y + 128] = jnp.where(lane64, even, pltpu.roll(odd, 64, 1))
                 patches[token + 8 : token + 16, 128 * y : 128 * y + 128] = jnp.where(lane64, pltpu.roll(even, 64, 1), odd)
 
-    copy.wait()
-
+    for copy in copies[0] + copies[1]:
+        copy.wait()
+
+    for i in range(NT):
+        for z, (begin, height, target) in enumerate(
+            ((0, 48, 128 * i), (0, 48, 128 * i + 48), (0, 32, 128 * i + 96), (16, 32, 1024 + 32 * i))
+        ):
+            source = pack.at[i % 2, PLACES[i][z]]
+            for part in range(5):
+                at = 880 + 48 * part + begin
+                embed[target : target + height, 128 * part : 128 * part + 128] = source[at : at + height, :]
     lane48 = lane_iota(48)
+    for h in range(HEADS):
+        outw[128 * h + HD : 128 * h + 128, :] = jnp.zeros((128 - HD, D), BF16)
     for z in range(NZ):
         for i in range(NT):
-            source = pack.at[PLACES[i][z]]
-            outw[160 * z : 160 * z + 160, 128 * i : 128 * i + 128] = source[640:800, :]
+            source = pack.at[i % 2, PLACES[i][z]]
+            for local in range(2):
+                at, begin = 128 * (2 * z + local), 640 + HD * local
+                outw[at : at + HD, 128 * i : 128 * i + 128] = source[begin : begin + HD, :]
             place[32 * z : 32 * z + 32, 128 * i : 128 * i + 128] = source[800:832, :]
         for ib in range(2):
-            sources = [pack[PLACES[4 * ib + j][z], 832:880, :].astype(F32) for j in range(4)]
+            sources = [pack[j % 2, PLACES[4 * ib + j][z], 832:880, :].astype(F32) for j in range(4)]
             rolled = [[sources[j] if d == 0 else pltpu.roll(sources[j], 32 * d, 1) for d in range(4)] for j in range(4)]
             at = 1024 + 128 * ib
             for q in range(4):
@@ -325,10 +347,15 @@
                 for j in range(1, 4):
                     found = jnp.where(lane48 >= 32 * j, rolled[j][(j - q) % 4], found)
                 found = found.astype(BF16)
-                if q < 3:
-                    outw[160 * z + 48 * q : 160 * z + 48 * q + 48, at : at + 128] = found
-                else:
-                    outw[160 * z + 144 : 160 * z + 160, at : at + 128] = found[:16]
+                for begin, end, row in (
+                    ((0, 48, 0),),
+                    ((0, 32, 48), (32, 48, 128)),
+                    ((0, 48, 144),),
+                    ((0, 16, 192),),
+                )[q]:
+                    row = 256 * z + row
+                    outw[row : row + end - begin, at : at + 128] = found[begin:end]
+                if q == 3:
                     place[32 * z : 32 * z + 32, at : at + 128] = found[16:48]
 
     patches16 = nn_dot(patches[...].astype(BF16), order[...]).astype(BF16)
@@ -347,19 +374,23 @@
         tokens[f * NTOK : f * NTOK + NTOK, :] = jnp.broadcast_to(scale, (NTOK, 128))
 
     def weight_part(i, z):
-        source = pack.at[PLACES[i][z]]
+        source = pack.at[i % 2, PLACES[i][z]]
         return jnp.concatenate([source[0:256, :], source[320:576, :]], axis=1)
 
     def weight_rest(i):
         return jnp.concatenate(
             [
-                jnp.concatenate([pack[PLACES[i][z], 256:320, :], pack[PLACES[i][z], 576:640, :]], axis=1)
+                jnp.concatenate(
+                    [pack[i % 2, PLACES[i][z], 256:320, :], pack[i % 2, PLACES[i][z], 576:640, :]], axis=1
+                )
                 for z in range(NZ)
             ],
             axis=0,
         )
 
     lane_all = lane_iota(count)
+    for copy in copies[2]:
+        copy.wait()
     for i in range(NT):
         mixed = nn_dot(
             normed16[...], jnp.concatenate([weight_part(i, z) for z in range(NZ)] + [weight_rest(i)], axis=0)
@@ -381,12 +412,10 @@
             prob = logits / jnp.sum(logits, axis=-1, keepdims=True)
             weights[h * samples + f] = prob
             attended = nn_dot(prob.astype(BF16), slots[2 * HEADS + h, span, :]).astype(BF16)
-            abar[h, f : f + 1, :] = jnp.mean(attended.astype(F32), axis=0, keepdims=True)
-
-    pooled = rows8[0]
-    for h in range(HEADS):
-        part = nn_dot(split_two(abar[h])[:, 0:HD], outw[HD * h : HD * h + HD, :])
-        pooled = pooled + part[0:8] + part[8:16]
+            abar[f : f + 1, 128 * h : 128 * h + 128] = jnp.mean(attended.astype(F32), axis=0, keepdims=True)
+
+    part = nn_dot(split_two(abar[...]), outw[...])
+    pooled = rows8[0] + part[0:8] + part[8:16]
     pooled = pooled - jnp.mean(pooled, axis=-1, keepdims=True)
     scale = lax.rsqrt(jnp.mean(pooled * pooled, axis=-1, keepdims=True) + 1e-05)
     pooled = pooled * scale
@@ -397,12 +426,11 @@
     )
     dres = dpooled * (1.0 / NTOK)
     rows8[1] = dres
-    dres_two = split_two(dres)
+    datts = nt_dot(split_two(dres), outw[...])
+    datts = (datts[0:8] + datts[8:16]).astype(BF16)
 
     for h in range(HEADS):
-        datt = nt_dot(dres_two, outw[HD * h : HD * h + HD, :])
-        datt = (datt[0:8] + datt[8:16]).astype(BF16)
-        datt = jnp.concatenate([datt, jnp.zeros((8, 128 - HD), BF16)], axis=1)
+        datt = datts[:, 128 * h : 128 * h + 128]
         for f in range(samples):
             span = slice(f * NTOK, f * NTOK + NTOK)
             prob = weights[h * samples + f]
@@ -466,16 +494,18 @@
                 out_ref[i, f, o] = frame[f, o, at : at + rows, :].astype(BF16)
 
 
-def pack_part(rows_in, out_part, place_part):
+def pack_part(rows_in, out_part, place_part, embed_part):
     ordered = jnp.concatenate([rows_in[0:128], rows_in[160:288], rows_in[128:160], rows_in[288:320]], axis=0)
     upper = jnp.pad(ordered[:, 128:240], ((0, 0), (0, 16)))
     other = jnp.concatenate([out_part, place_part], axis=0)
     rest = other[:, 128:160].reshape(4, 48, 32)
     rest = jnp.concatenate([rest[q] for q in range(4)], axis=1)
-    return jnp.concatenate([ordered[:, 0:128], upper, other[:, 0:128], rest], axis=0)
-
-
-def pack_kernel(rows_ref, out_ref, place_ref, packed_ref):
+    embed_part = jnp.pad(embed_part, ((0, 0), (0, 640 - embed_part.shape[1])))
+    embed_part = embed_part.reshape(48, 5, 128).transpose(1, 0, 2).reshape(240, 128)
+    return jnp.concatenate([ordered[:, 0:128], upper, other[:, 0:128], rest, embed_part], axis=0)
+
+
+def pack_kernel(z_ref, rows_ref, out_ref, place_ref, embed_ref, packed_ref):
     for source, target, count in ((0, 0, 128), (160, 128, 128), (128, 256, 32), (288, 288, 32)):
         packed_ref[target : target + count, :] = rows_ref[source : source + count, 0:128]
         packed_ref[320 + target : 320 + target + count, :] = jnp.concatenate(
@@ -489,17 +519,29 @@
         [tail[0:48], tail[48:96], tail[96:144], jnp.concatenate([tail[144:160], last], axis=0)],
         axis=1,
     ).astype(BF16)
-
-
-def packed_weights(position, attend_in, attend_out):
+    width = embed_ref.shape[1]
+    start = pl.multiple_of(jnp.where(z_ref[0] == NZ - 1, STARTS[-1], 48 * z_ref[0]), 16)
+    for part in range(5):
+        count = min(128, width - 128 * part)
+        value = embed_ref[pl.ds(start, 48), 128 * part : 128 * part + count]
+        if count < 128:
+            value = jnp.concatenate([value, jnp.zeros((48, 128 - count), BF16)], axis=1)
+        packed_ref[880 + 48 * part : 928 + 48 * part, :] = value
+
+
+def packed_weights(patch_embed, position, attend_in, attend_out):
     if lax.axis_size(TILE) == NT and lax.axis_size("sample") == NZ:
+        z = lax.axis_index("sample").astype(jnp.int32).reshape(1)
         mine = pl.pallas_call(
             pack_kernel,
+            in_specs=[pl.BlockSpec(memory_space=pltpu.SMEM)] + [pl.BlockSpec(memory_space=pltpu.VMEM)] * 4,
             out_shape=jax.ShapeDtypeStruct((PACK, 128), BF16),
             compiler_params=params(),
             name="pack",
-        )(attend_in, attend_out, position)
-        return lax.all_gather(mine, TILE + ("sample",), axis=0, axis_index_groups=[CYCLE])
+        )(z, attend_in, attend_out, position, patch_embed.T)
+        groups = [[(2 * chip + core) * NZ + z for chip, z in RINGS[core]] for core in range(2)]
+        mine = lax.all_gather(mine, TILE + ("sample",), axis=0, axis_index_groups=groups)
+        return mine, None, lax.axis_index("core").astype(jnp.int32).reshape(1)
 
     def whole(value):
         value = lax.all_gather(value, "sample", axis=0, tiled=True)
@@ -509,15 +551,13 @@
         value.reshape(NZ, value.shape[0] // NZ, NT, value.shape[1] // NT).transpose(2, 0, 1, 3)
         for value in (whole(attend_in), whole(attend_out), whole(position))
     ]
-    split = [value.reshape((NT * NZ,) + value.shape[2:])[jnp.array(CYCLE)] for value in split]
-    return jax.vmap(pack_part)(*split)
-
-
-def embed_parts(patch_embed):
-    tiles = lax.axis_size(TILE)
-    copies = jnp.broadcast_to(patch_embed.T[None], (tiles,) + patch_embed.shape[::-1])
-    found = lax.all_to_all(copies, TILE, split_axis=0, concat_axis=0, tiled=True)
-    return found.reshape(NT, D // NT, patch_embed.shape[0])
+    columns = lax.all_gather(patch_embed.T, TILE, axis=0, tiled=True).reshape(NT, D // NT, -1)
+    split.append(jnp.stack([columns[:, start : start + 48] for start in STARTS], axis=1))
+    packed = jax.vmap(jax.vmap(pack_part))(*split)
+    mine, other = (
+        jnp.stack([packed[2 * chip + core, z] for chip, z in RINGS[core]]) for core in range(2)
+    )
+    return mine, other, jnp.zeros(1, jnp.int32)
 
 
 def params(mib=58):
@@ -542,8 +582,7 @@
     row_block = row_count if row_count <= 14 else 14
     blocks = row_count // row_block
     inner = row_block * CH
-    packed = packed_weights(position, attend_in, attend_out)
-    embed = embed_parts(patch_embed)
+    packed, other, core = packed_weights(patch_embed, position, attend_in, attend_out)
     order = Layout((1, 2, 3, 0, 4))
     split = (samples, frames, row_count, merged // 128, 128)
     view = with_layout_constraint(features.reshape(split), order).transpose(1, 2, 3, 0, 4)
@@ -585,6 +624,9 @@
     if tiles > SCORED:
         decoded = jnp.pad(decoded, ((0, tiles - SCORED),) + ((0, 0),) * 4)
     owned = lax.all_to_all(decoded, TILE, split_axis=0, concat_axis=0, tiled=True)
+    if other is None:
+        packed, owned = lax.optimization_barrier((packed, owned))
+        other = lax.ppermute(packed, "core", [(0, 1), (1, 0)])
 
     head = reward_head.reshape(NT, D // NT)
     head = jnp.concatenate([head[:, :128].reshape(-1), head[:, 128:].reshape(-1)])[None, :]
@@ -597,18 +639,19 @@
             jax.ShapeDtypeStruct((8, 128), F32),
         ],
         in_specs=[
+            smem,
             pl.BlockSpec(memory_space=pltpu.VMEM),
-            pl.BlockSpec(memory_space=pltpu.VMEM),
+            pl.BlockSpec(memory_space=pl.ANY),
             pl.BlockSpec(memory_space=pl.ANY),
             pl.BlockSpec(memory_space=pltpu.VMEM),
         ],
         scratch_shapes=[
-            pltpu.VMEM(packed.shape, BF16),
-            pltpu.SemaphoreType.DMA,
+            pltpu.VMEM((2,) + packed.shape, BF16),
+            pltpu.SemaphoreType.DMA((3, 2)),
             pltpu.VMEM((samples, 3, height + 48, 128), F32),
             pltpu.VMEM((samples * height // (2 * PATCH), 2, 128, 128), F32),
-            pltpu.VMEM((D, embed.shape[2]), BF16),
-            pltpu.VMEM((HEADS * HD, D), BF16),
+            pltpu.VMEM((D, 640), BF16),
+            pltpu.VMEM((HEADS * 128, D), BF16),
             pltpu.VMEM((NTOK, D), BF16),
             pltpu.VMEM((count, KIN), F32),
             pltpu.VMEM((count, 128), F32),
@@ -619,40 +662,29 @@
             pltpu.VMEM((3 * HEADS, count, 128), F32),
             pltpu.VMEM((count, D), F32),
             pltpu.VMEM((2, 8, D), F32),
-            pltpu.VMEM((HEADS, 8, 128), F32),
-            pltpu.VMEM((KIN, embed.shape[2]), BF16),
+            pltpu.VMEM((8, HEADS * 128), F32),
+            pltpu.VMEM((KIN, 640), BF16),
         ],
         compiler_params=params(),
         name="reward",
-    )(owned, embed, packed, head)
+    )(core, owned, packed, other, head)
 
     mine = jnp.concatenate([scores[:samples, 0], group_index.astype(F32)])
-    gathered = [mine]
-    for shift in range(1, parts):
-        ring = [(z, (z + shift) % parts) for z in range(parts)]
-        gathered.append(lax.ppermute(mine, "sample", ring))
-    gathered = jnp.stack(gathered)
-    groups = gathered[:, samples:].reshape(-1)
-    score_row = gathered[:, :samples].reshape(-1)
-    high = score_row.astype(BF16)
-    low = score_row - high.astype(F32)
-    mid = low.astype(BF16)
-    low = (low - mid.astype(F32)).astype(BF16)
-    total = parts * samples
-    carried = jnp.concatenate([high, mid, low])
-    grads = grads.at[:, 0, 0, sent_rows - 1, 0 : 3 * total].set(
-        jnp.broadcast_to(carried, (tiles, 3 * total))
-    )
+    mine = jnp.broadcast_to(mine[None], (tiles * parts, 2 * samples))
+    everyone = lax.all_to_all(mine, TILE + ("sample",), split_axis=0, concat_axis=0, tiled=True)
+    everyone = everyone.reshape(tiles, parts, 2, samples)
     returned = lax.all_to_all(grads, TILE, split_axis=0, concat_axis=0, tiled=True)
     returned = returned[:SCORED]
 
-    got = returned[:, 0, 0, sent_rows - 1, 0 : 3 * total].astype(F32).reshape(SCORED, 3, total)
-    entry_scores = got[:, 0] + (got[:, 1] + got[:, 2])
-    rewards = jnp.sum(entry_scores, axis=0) / SCORED
-    member = (groups[:samples, None] == groups[None, :]).astype(F32)
+    rewards = jnp.sum(everyone[:SCORED, :, 0], axis=0).reshape(-1) / SCORED
+    groups = everyone[0, :, 1].reshape(-1)
+    here = (lax.axis_index("sample") * samples).astype(jnp.int32)
+    own_rewards = lax.dynamic_slice_in_dim(rewards, here, samples)
+    own_groups = lax.dynamic_slice_in_dim(groups, here, samples)
+    member = (own_groups[:, None] == groups[None, :]).astype(F32)
     mean_group = jnp.sum(member * rewards[None, :], axis=1) / GROUP
     second_group = jnp.sum(member * (rewards * rewards)[None, :], axis=1) / GROUP - mean_group * mean_group
-    advantage = (rewards[:samples] - mean_group) * lax.rsqrt(second_group + SMOOTH)
+    advantage = (own_rewards - mean_group) * lax.rsqrt(second_group + SMOOTH)
     cotangent = -LOSS_SCALE * advantage / SCORED
 
     result = pl.pallas_call(

time: 176 us -> 170 us (0.966)
  starting transfers between devices: 11 us -> 6.59 us
  waiting for transfers between devices: 49.1 us -> 52.6 us
    all_gather x1, waiting for transfers between devices: 5.85 us -> 31.3 us  [packed_weights(): lax.all_gather(mine, TILE + ('sample',), axis=0, axis_index_groups=groups)]
    all_to_all x1, waiting for transfers between devices: 29.7 us -> 7.16 us  [local(): lax.all_to_all(mine, TILE + ('sample',), split_axis=0, concat_axis=0, til...]
    ppermute x3 -> x1, starting transfers between devices: 3.22 us -> 0.01 us  [local(): other = lax.ppermute(packed, 'core', [(0, 1), (1, 0)])]
    ppermute x3 -> x1, waiting for transfers between devices: 5.33 us -> 7.29 us  [local(): other = lax.ppermute(packed, 'core', [(0, 1), (1, 0)])]
  transfers between devices with their start and end apart: 6 -> 4, of which waited for: 6 -> 4; matrix products, arithmetic and copies ran while one was open for 1% -> 1% of each run, Pallas kernels for 14% -> 14%
where the time goes in v4:
time: 170 us
  Pallas kernels  78 us (46%)
  waiting for transfers between devices  52.6 us (31%)
  blocking collectives  14.8 us (9%)
  between operations  13.5 us (8%)
  starting transfers between devices  6.59 us (4%)
  local copies, waits for them, and re-layouts  3.5 us (2%)
    all_gather x1, waiting for transfers between devices, packed_weights(): lax.all_gather(mine, TILE + ('sample',), axis=0, axis_index_groups=groups)  31.3 us
    pallas_call x1, Pallas kernels, local(): pl.pallas_call(functools.partial(restore_kernel, row_block), grid=(frames...  30.1 us
    pallas_call x1, Pallas kernels, local(): pl.pallas_call(functools.partial(decode_kernel, row_block), grid=(frames,...  23.7 us
    pallas_call x1, Pallas kernels, local(): pl.pallas_call(functools.partial(reward_kernel, row_count, tiles, samples...  22.3 us
    all_to_all x1, blocking collectives, local(): lax.all_to_all(decoded, TILE, split_axis=0, concat_axis=0, tiled=True)  14.8 us
    ppermute x1, waiting for transfers between devices, local(): other = lax.ppermute(packed, 'core', [(0, 1), (1, 0)])  7.29 us
    all_to_all x1, waiting for transfers between devices, local(): lax.all_to_all(mine, TILE + ('sample',), split_axis=0, concat_axis=0, til...  7.16 us
    all_to_all x1, waiting for transfers between devices, local(): lax.all_to_all(grads, TILE, split_axis=0, concat_axis=0, tiled=True)  6.82 us
  transfers between devices with their start and end apart: 4, of which 4 were waited for; matrix products, arithmetic and copies ran while one was open for 1% of the time, Pallas kernels for 14%

profile of v4, /device:TPU:0, one launch (start us, length us, event | category | flops | bytes accessed | tf_op | source)
XLA Modules:
  0.0 169.9 jit_solution(14468496303096767420)
XLA Ops:
  6.5 0.0 copy-start.2
  6.5 0.0 copy-start.1
  6.5 0.0 all-gather.3.cloned.1.call-start
  6.5 1.9 %pack.1 = bf16[1120,128]{1,0:T(8,128)(2,1)} custom-call(s32[1]{0:T(128)} %bitcast.1.z_ref, bf16[320,240]{1,0:T(8,128)(2,1)} %rows_ref.1, bf16[160,160]{1,0:T(8,128)(2,1)} %out_ref.1, bf16[32,160]{1,0:T(8,128)(2,1)} %place_ref.1, bf16[160,588]{1,0:T(8,128)(2,1)} %bitcast.24), custom_call_target="tpu_custom_call" | custom-call | tf_op jit(solution)/shard_map/pack/pallas_call | solution.py:535
  8.4 0.0 all-gather.3.cloned.1.call-update
  8.4 23.7 %decode.1 = (bf16[8,2,3,32,128]{4,3,2,1,0:T(8,128)(2,1)}, bf16[9,28,2,96,128]{4,3,2,1,0:T(8,128)(2,1)}, f32[9,28,2,128]{3,2,1,0:T(2,128)}) custom-call(s32[2,8]{1,0:T(2,128)} %pick_ref.3, bf16[9,28,168,128]{3,2,1,0:T(8,128)(2,1)} %bitcast.21, f32[1,96]{1,0:T(1,128)} %bitcast.25, bf16[3,3,3,3,96]{4,3,2,1,0:T(4,128)(2,1)} %weight_ref.3), custom_call_target="tpu_custom_call" | custom-call | tf_op jit(solution)/shard_map/decode/pallas_call | solution.py:601
  32.2 14.8 %all_to_all.16.part_ref = bf16[8,2,3,32,128]{4,3,2,1,0:T(8,128)(2,1)} all-to-all(bf16[8,2,3,32,128]{4,3,2,1,0:T(8,128)(2,1)} %get-tuple-element.12), channel_id=1, replica_groups=mesh['chip'=4,'core'=2,'sample'=4] {'chip','core'}, dimensions={0} | all-to-all | bytes 786432 | tf_op jit(solution)/shard_map/all_to_all | solution.py:626
  47.0 31.3 %all-gather.3.cloned.1.call-done = bf16[17920,128]{1,0:T(8,128)(2,1)} async-done(((bf16[1120,128]{1,0:T(8,128)(2,1)}), bf16[17920,128]{1,0:T(8,128)(2,1)}) %all-gather.3.cloned.1.call-update) | async-done | bytes 4587536 | tf_op jit(solution)/shard_map/all_gather | solution.py:543
  78.3 0.0 collective-permute-start
  78.3 0.0 copy-done.2
  78.3 0.0 copy-done.1
  78.3 0.1 reshape.55
  78.4 0.1 reshape.57
  78.5 0.6 broadcast_in_dim.7.head_ref
  79.1 7.3 %collective-permute-done.other_ref = bf16[16,1120,128]{2,1,0:T(8,128)(2,1)} collective-permute-done((bf16[16,1120,128]{2,1,0:T(8,128)(2,1)}, bf16[16,1120,128]{2,1,0:T(8,128)(2,1)}, u32[]{:S(2)}, u32[]{:S(2)}) %collective-permute-start) | collective-permute-done | bytes 4587552 | tf_op jit(solution)/shard_map/ppermute | solution.py:629
  86.4 22.3 %reward.1 = (bf16[8,2,3,32,128]{4,3,2,1,0:T(8,128)(2,1)}, f32[8,128]{1,0:T(8,128)}) custom-call(s32[1]{0:T(128)} %bitcast.core_ref, bf16[8,2,3,32,128]{4,3,2,1,0:T(8,128)(2,1)} %all_to_all.16.part_ref, bf16[16,1120,128]{2,1,0:T(8,128)(2,1)} %bitcast.23, bf16[16,1120,128]{2,1,0:T(8,128)(2,1)} %collective-permute-done.other_ref, ...), custom_call_target="tpu_custom_call" | custom-call | tf_op jit(solution)/shard_map/reward/pallas_call | solution.py:635
  108.7 0.8 slice_reduce_fusion.1
  109.5 0.1 pad_maximum_fusion.1
  109.5 0.6 broadcast_in_dim.8
  110.1 3.1 %all-to-all-start.1 = ((f32[32,1,4]{2,1,0:T(1,128)}), f32[32,1,4]{2,1,0:T(1,128)S(1)}, u32[]{:S(2)}, u32[]{:S(2)}) async-start(f32[32,1,4]{2,1,0:T(1,128)} %broadcast_in_dim.8), calls=%async_computation.1 | async-start | bytes 32768 | tf_op jit(solution)/shard_map/all_to_all | solution.py:674
  113.3 7.2 %all-to-all-done.1 = f32[32,1,4]{2,1,0:T(1,128)S(1)} async-done(((f32[32,1,4]{2,1,0:T(1,128)}), f32[32,1,4]{2,1,0:T(1,128)S(1)}, u32[]{:S(2)}, u32[]{:S(2)}) %all-to-all-start.1) | async-done | bytes 544 | tf_op jit(solution)/shard_map/all_to_all | solution.py:674
  120.4 3.5 %all-to-all-start.2 = ((bf16[8,2,3,32,128]{4,3,2,1,0:T(8,128)(2,1)}), bf16[8,2,3,32,128]{4,3,2,1,0:T(8,128)(2,1)S(1)}, u32[]{:S(2)}, u32[]{:S(2)}) async-start(bf16[8,2,3,32,128]{4,3,2,1,0:T(8,128)(2,1)} %get-tuple-element.18), calls=%async_computation.2 | async-start | bytes 786432 | tf_op jit(solution)/shard_map/all_to_all | solution.py:676
  123.9 0.1 copy.16
  124.0 0.1 reshape.58
  124.1 0.1 copy.17
  124.2 0.1 div.17
  124.3 0.1 copy.18
  124.4 0.1 reshape_squeeze.3
  124.5 0.1 dynamic_slice.7
  124.6 0.2 fusion
  124.7 0.6 multiply_multiply_fusion.scale_ref
  125.4 6.8 %all-to-all-done.2.grad_ref = bf16[8,2,3,32,128]{4,3,2,1,0:T(8,128)(2,1)S(1)} async-done(((bf16[8,2,3,32,128]{4,3,2,1,0:T(8,128)(2,1)}), bf16[8,2,3,32,128]{4,3,2,1,0:T(8,128)(2,1)S(1)}, u32[]{:S(2)}, u32[]{:S(2)}) %all-to-all-start.2) | async-done | bytes 393248 | tf_op jit(solution)/shard_map/all_to_all | solution.py:676
  132.2 0.0 copy-start
  132.2 0.8 copy-done
  132.9 30.1 %restore.1 = bf16[9,28,168,128]{3,2,1,0:T(8,128)(2,1)} custom-call(s32[2,8]{1,0:T(2,128)} %pick_ref.3, f32[2]{0:T(128)} %multiply_multiply_fusion.scale_ref, bf16[9,28,2,96,128]{4,3,2,1,0:T(8,128)(2,1)} %get-tuple-element.16.x_ref, f32[9,28,2,128]{3,2,1,0:T(2,128)} %get-tuple-element.17.inv_ref, f32[1,96]{1,0:T(1,128)} %bitcast.26, ...), custom_call_target="tpu_custom_call" | custom-call | tf_op jit(solution)/shard_map/restore/pallas_call | solution.py:690
  (8 shorter events, 0.1 us)
Async XLA Ops:
  6.5 71.8 %copy-start.2 = (s32[2]{0:T(128)S(1)}, s32[2]{0:T(128)}, u32[]{:S(2)}) copy-start(s32[2]{0:T(128)} %param.18) | copy-start | bytes 28
  6.5 71.8 %copy-start.1 = (f32[1280]{0:T(1024)S(1)}, f32[1280]{0:T(1024)}, u32[]{:S(2)}) copy-start(f32[1280]{0:T(1024)} %param.17) | copy-start | bytes 15364
  6.5 71.8 %all-gather.3.cloned.1.call-start = ((), (), s32[]{:S(2)}) async-start(), calls=%async_computation.3 | async-start | bytes 4874240 | tf_op jit(solution)/shard_map/all_gather | solution.py:543
  78.3 8.1 %collective-permute-start = (bf16[16,1120,128]{2,1,0:T(8,128)(2,1)}, bf16[16,1120,128]{2,1,0:T(8,128)(2,1)}, u32[]{:S(2)}, u32[]{:S(2)}) collective-permute-start(bf16[16,1120,128]{2,1,0:T(8,128)(2,1)} %bitcast.22), channel_id=1, source_target_pairs={{0,4},{4,0},{1,5},{5,1},{2,6},{6,2},{3,7},{7,3},{8,12},{12,8},{9,1... | collective-permute-start | bytes 13762568 | tf_op jit(solution)/shard_map/ppermute | solution.py:629
  110.1 10.3 %all-to-all-start.1 = ((f32[32,1,4]{2,1,0:T(1,128)}), f32[32,1,4]{2,1,0:T(1,128)S(1)}, u32[]{:S(2)}, u32[]{:S(2)}) async-start(f32[32,1,4]{2,1,0:T(1,128)} %broadcast_in_dim.8), calls=%async_computation.1 | async-start | bytes 32768 | tf_op jit(solution)/shard_map/all_to_all | solution.py:674
  120.4 11.7 %all-to-all-start.2 = ((bf16[8,2,3,32,128]{4,3,2,1,0:T(8,128)(2,1)}), bf16[8,2,3,32,128]{4,3,2,1,0:T(8,128)(2,1)S(1)}, u32[]{:S(2)}, u32[]{:S(2)}) async-start(bf16[8,2,3,32,128]{4,3,2,1,0:T(8,128)(2,1)} %get-tuple-element.18), calls=%async_computation.2 | async-start | bytes 786432 | tf_op jit(solution)/shard_map/all_to_all | solution.py:676
  132.2 0.8 copy-start
Sparse Core Ops, SparseCore 0:
  8.9 69.3 all-gather.2

commit v5 on v4

--- a/solution.py
+++ b/solution.py
@@ -25,12 +25,12 @@
 NZ = 4
 PACK = 1120
 CYCLE = [
-    (chip, z)
+    (2 * chip + core, z)
     for chip, heights in ((0, (0, 1, 2, 3)), (1, (3, 2, 1, 0)), (3, (0, 1, 2, 3)), (2, (3, 2, 1, 0)))
     for z in heights
+    for core in range(2)
 ]
-RINGS = (CYCLE, CYCLE[::-1])
-PLACES = [[RINGS[i % 2].index((i // 2, z)) for z in range(NZ)] for i in range(NT)]
+PLACES = [[CYCLE.index((i, z)) for z in range(NZ)] for i in range(NT)]
 STARTS = (0, 48, 96, 112)
 KIN = 896
 D = 1280
@@ -110,7 +110,7 @@
     return found
 
 
-def decode_kernel(row_block, pick_ref, x_ref, gain_ref, weight_ref, out_ref, x_out, inv_out, band, taps, gains, raw, operand, acc, final):
+def decode_kernel(row_block, pick_ref, x_ref, gain_ref, weight_ref, out_ref, x_out, inv_out, slope_out, turned_out, band, taps, gains, raw, operand, acc, final):
     t = pl.program_id(0)
     blocks = x_ref.shape[1] // row_block
     rows = out_ref.shape[3]
@@ -118,6 +118,7 @@
     @pl.when(t == 0)
     def _():
         band[...] = banded(weight_ref, taps, row_block, False)
+        turned_out[...] = banded(weight_ref, taps, row_block, True)
         gains[...] = half_gains(gain_ref)
         acc[...] = jnp.zeros(acc.shape, F32)
         raw[...] = jnp.zeros(raw.shape, F32)
@@ -138,10 +139,17 @@
                     x_out[0, k * row_block + row, s, 16 * m : 16 * m + 16, :] = jnp.concatenate(
                         [found[2 * m], found[2 * m + 1]], axis=0
                     ).astype(BF16)
-                    acts = []
+                    acts, slopes = [], []
                     for g in (2 * m, 2 * m + 1):
-                        half = found[g] * inv * gains[8 * g : 8 * g + 8, :]
-                        acts.append(half + half * jnp.tanh(half))
+                        gain = gains[8 * g : 8 * g + 8, :]
+                        half = found[g] * inv * gain
+                        th = jnp.tanh(half)
+                        rest = half - half * th
+                        acts.append(half + half * th)
+                        slopes.append((gain + gain * th) * (1.0 + rest))
+                    slope_out[0, k * row_block + row, s, 16 * m : 16 * m + 16, :] = jnp.concatenate(
+                        slopes, axis=0
+                    ).astype(BF16)
                     start = row * CH + 16 * m
                     operand[k, start : start + 16, 128 * s : 128 * s + 128] = jnp.concatenate(
                         acts, axis=0
@@ -178,7 +186,7 @@
         acc[k, 2] = jnp.zeros(acc.shape[2:], F32)
 
 
-def restore_kernel(row_block, pick_ref, scale_ref, x_ref, inv_ref, gain_ref, weight_ref, grad_ref, out_ref, band, taps, gains, back, shifted, coming):
+def restore_kernel(row_block, pick_ref, scale_ref, x_ref, inv_ref, slope_ref, band, grad_ref, out_ref, back, shifted, coming):
     t = pl.program_id(0)
     frames = pl.num_programs(0)
     blocks = x_ref.shape[1] // row_block
@@ -186,8 +194,6 @@
 
     @pl.when(t == 0)
     def _():
-        band[...] = banded(weight_ref, taps, row_block, True)
-        gains[...] = half_gains(gain_ref)
         shifted[...] = jnp.zeros(shifted.shape, BF16)
         lane = lane_iota(rows)
 
@@ -219,15 +225,13 @@
                 outs, units, total = [], [], None
                 for m in range(SPANS // 2):
                     pair = x_ref[0, k * row_block + row, s, 16 * m : 16 * m + 16, :].astype(F32)
+                    slopes = slope_ref[0, k * row_block + row, s, 16 * m : 16 * m + 16, :].astype(F32)
                     for local in range(2):
                         g = 2 * m + local
                         unit = pair[8 * local : 8 * local + 8] * inv
-                        gain = gains[8 * g : 8 * g + 8, :]
-                        half = unit * gain
-                        th = jnp.tanh(half)
                         start = row * CH + 8 * g
                         cot = coming[k, start : start + 8, 128 * s : 128 * s + 128]
-                        out = cot * gain * (1.0 + th) * (1.0 + half * (1.0 - th))
+                        out = cot * slopes[8 * local : 8 * local + 8]
                         outs.append(out)
                         units.append(unit)
                         total = out * unit if g == 0 else total + out * unit
@@ -261,7 +265,7 @@
 
 def reward_kernel(
     row_count, tiles, samples,
-    core_ref, part_ref, mine_ref, other_ref, head_ref,
+    part_ref, packed_ref, head_ref,
     out_ref, score_ref,
     pack, arrived, frame, flip, embed, outw, place, patches, tokens, normed, normed16, slots, weights, dslots, dnormed, rows8, abar, order,
 ):
@@ -271,19 +275,14 @@
     lane = lane_iota(NTOK)
     count = samples * NTOK
 
-    core = core_ref[0]
     copies = []
     for part, (begin, end) in enumerate(((880, 1120), (640, 880), (0, 640))):
         copies.append(
-            [
-                pltpu.make_async_copy(
-                    source.at[:, begin:end, :], pack.at[at, :, begin:end, :], arrived.at[part, which]
-                )
-                for which, (source, at) in enumerate(((mine_ref, core), (other_ref, 1 - core)))
-            ]
+            pltpu.make_async_copy(
+                packed_ref.at[:, begin:end, :], pack.at[:, begin:end, :], arrived.at[part]
+            )
         )
-        for copy in copies[-1]:
-            copy.start()
+        copies[-1].start()
 
     inputs = order.shape[1]
     pixel = lax.broadcasted_iota(jnp.int32, (64, inputs), 0)
@@ -317,14 +316,14 @@
                 patches[token : token + 8, 128 * y : 128 * y + 128] = jnp.where(lane64, even, pltpu.roll(odd, 64, 1))
                 patches[token + 8 : token + 16, 128 * y : 128 * y + 128] = jnp.where(lane64, pltpu.roll(even, 64, 1), odd)
 
-    for copy in copies[0] + copies[1]:
-        copy.wait()
+    copies[0].wait()
+    copies[1].wait()
 
     for i in range(NT):
         for z, (begin, height, target) in enumerate(
             ((0, 48, 128 * i), (0, 48, 128 * i + 48), (0, 32, 128 * i + 96), (16, 32, 1024 + 32 * i))
         ):
-            source = pack.at[i % 2, PLACES[i][z]]
+            source = pack.at[PLACES[i][z]]
             for part in range(5):
                 at = 880 + 48 * part + begin
                 embed[target : target + height, 128 * part : 128 * part + 128] = source[at : at + height, :]
@@ -333,13 +332,13 @@
         outw[128 * h + HD : 128 * h + 128, :] = jnp.zeros((128 - HD, D), BF16)
     for z in range(NZ):
         for i in range(NT):
-            source = pack.at[i % 2, PLACES[i][z]]
+            source = pack.at[PLACES[i][z]]
             for local in range(2):
                 at, begin = 128 * (2 * z + local), 640 + HD * local
                 outw[at : at + HD, 128 * i : 128 * i + 128] = source[begin : begin + HD, :]
             place[32 * z : 32 * z + 32, 128 * i : 128 * i + 128] = source[800:832, :]
         for ib in range(2):
-            sources = [pack[j % 2, PLACES[4 * ib + j][z], 832:880, :].astype(F32) for j in range(4)]
+            sources = [pack[PLACES[4 * ib + j][z], 832:880, :].astype(F32) for j in range(4)]
             rolled = [[sources[j] if d == 0 else pltpu.roll(sources[j], 32 * d, 1) for d in range(4)] for j in range(4)]
             at = 1024 + 128 * ib
             for q in range(4):
@@ -374,23 +373,20 @@
         tokens[f * NTOK : f * NTOK + NTOK, :] = jnp.broadcast_to(scale, (NTOK, 128))
 
     def weight_part(i, z):
-        source = pack.at[i % 2, PLACES[i][z]]
+        source = pack.at[PLACES[i][z]]
         return jnp.concatenate([source[0:256, :], source[320:576, :]], axis=1)
 
     def weight_rest(i):
         return jnp.concatenate(
             [
-                jnp.concatenate(
-                    [pack[i % 2, PLACES[i][z], 256:320, :], pack[i % 2, PLACES[i][z], 576:640, :]], axis=1
-                )
+                jnp.concatenate([pack[PLACES[i][z], 256:320, :], pack[PLACES[i][z], 576:640, :]], axis=1)
                 for z in range(NZ)
             ],
             axis=0,
         )
 
     lane_all = lane_iota(count)
-    for copy in copies[2]:
-        copy.wait()
+    copies[2].wait()
     for i in range(NT):
         mixed = nn_dot(
             normed16[...], jnp.concatenate([weight_part(i, z) for z in range(NZ)] + [weight_rest(i)], axis=0)
@@ -539,9 +535,8 @@
             compiler_params=params(),
             name="pack",
         )(z, attend_in, attend_out, position, patch_embed.T)
-        groups = [[(2 * chip + core) * NZ + z for chip, z in RINGS[core]] for core in range(2)]
-        mine = lax.all_gather(mine, TILE + ("sample",), axis=0, axis_index_groups=groups)
-        return mine, None, lax.axis_index("core").astype(jnp.int32).reshape(1)
+        group = [i * NZ + z for i, z in CYCLE]
+        return lax.all_gather(mine, TILE + ("sample",), axis=0, axis_index_groups=[group])
 
     def whole(value):
         value = lax.all_gather(value, "sample", axis=0, tiled=True)
@@ -554,10 +549,7 @@
     columns = lax.all_gather(patch_embed.T, TILE, axis=0, tiled=True).reshape(NT, D // NT, -1)
     split.append(jnp.stack([columns[:, start : start + 48] for start in STARTS], axis=1))
     packed = jax.vmap(jax.vmap(pack_part))(*split)
-    mine, other = (
-        jnp.stack([packed[2 * chip + core, z] for chip, z in RINGS[core]]) for core in range(2)
-    )
-    return mine, other, jnp.zeros(1, jnp.int32)
+    return jnp.stack([packed[i, z] for i, z in CYCLE])
 
 
 def params(mib=58):
@@ -582,7 +574,7 @@
     row_block = row_count if row_count <= 14 else 14
     blocks = row_count // row_block
     inner = row_block * CH
-    packed, other, core = packed_weights(patch_embed, position, attend_in, attend_out)
+    packed = packed_weights(patch_embed, position, attend_in, attend_out)
     order = Layout((1, 2, 3, 0, 4))
     split = (samples, frames, row_count, merged // 128, 128)
     view = with_layout_constraint(features.reshape(split), order).transpose(1, 2, 3, 0, 4)
@@ -598,11 +590,12 @@
     aligned = (frames, row_count, samples, CH, 128)
     aligned_spec = pl.BlockSpec((1,) + aligned[1:], lambda t: (t, 0, 0, 0, 0))
     inv_spec = pl.BlockSpec((1, row_count, samples, 128), lambda t: (t, 0, 0, 0))
-    decoded, x_aligned, inverse = pl.pallas_call(
+    band_spec = pl.BlockSpec((inner, OUT_ROWS), lambda t: (0, 0))
+    decoded, x_aligned, inverse, slopes, band = pl.pallas_call(
         functools.partial(decode_kernel, row_block),
         grid=(frames,),
         in_specs=[smem, view_spec, gain_spec, taps_spec],
-        out_specs=[sent_spec, aligned_spec, inv_spec],
+        out_specs=[sent_spec, aligned_spec, inv_spec, aligned_spec, band_spec],
         scratch_shapes=[
             pltpu.VMEM((OUT_ROWS, inner), BF16),
             pltpu.VMEM((3, 32, CH), F32),
@@ -616,6 +609,8 @@
             jax.ShapeDtypeStruct(sent, BF16),
             jax.ShapeDtypeStruct(aligned, BF16),
             jax.ShapeDtypeStruct((frames, row_count, samples, 128), F32),
+            jax.ShapeDtypeStruct(aligned, BF16),
+            jax.ShapeDtypeStruct((inner, OUT_ROWS), BF16),
         ],
         compiler_params=params(),
         name="decode",
@@ -624,9 +619,6 @@
     if tiles > SCORED:
         decoded = jnp.pad(decoded, ((0, tiles - SCORED),) + ((0, 0),) * 4)
     owned = lax.all_to_all(decoded, TILE, split_axis=0, concat_axis=0, tiled=True)
-    if other is None:
-        packed, owned = lax.optimization_barrier((packed, owned))
-        other = lax.ppermute(packed, "core", [(0, 1), (1, 0)])
 
     head = reward_head.reshape(NT, D // NT)
     head = jnp.concatenate([head[:, :128].reshape(-1), head[:, 128:].reshape(-1)])[None, :]
@@ -639,15 +631,13 @@
             jax.ShapeDtypeStruct((8, 128), F32),
         ],
         in_specs=[
-            smem,
             pl.BlockSpec(memory_space=pltpu.VMEM),
-            pl.BlockSpec(memory_space=pl.ANY),
             pl.BlockSpec(memory_space=pl.ANY),
             pl.BlockSpec(memory_space=pltpu.VMEM),
         ],
         scratch_shapes=[
-            pltpu.VMEM((2,) + packed.shape, BF16),
-            pltpu.SemaphoreType.DMA((3, 2)),
+            pltpu.VMEM(packed.shape, BF16),
+            pltpu.SemaphoreType.DMA((3,)),
             pltpu.VMEM((samples, 3, height + 48, 128), F32),
             pltpu.VMEM((samples * height // (2 * PATCH), 2, 128, 128), F32),
             pltpu.VMEM((D, 640), BF16),
@@ -667,7 +657,7 @@
         ],
         compiler_params=params(),
         name="reward",
-    )(core, owned, packed, other, head)
+    )(owned, packed, head)
 
     mine = jnp.concatenate([scores[:samples, 0], group_index.astype(F32)])
     mine = jnp.broadcast_to(mine[None], (tiles * parts, 2 * samples))
@@ -690,12 +680,9 @@
     result = pl.pallas_call(
         functools.partial(restore_kernel, row_block),
         grid=(frames,),
-        in_specs=[smem, smem, aligned_spec, inv_spec, gain_spec, taps_spec, sent_spec],
+        in_specs=[smem, smem, aligned_spec, inv_spec, aligned_spec, band_spec, sent_spec],
         out_specs=view_spec,
         scratch_shapes=[
-            pltpu.VMEM((inner, OUT_ROWS), BF16),
-            pltpu.VMEM((3, 32, CH), F32),
-            pltpu.VMEM((128, 128), F32),
             pltpu.VMEM((row_block, samples * merged // 128, 128), F32),
             pltpu.VMEM((frames + 2, blocks, 144, 256), BF16),
             pltpu.VMEM((blocks, inner, 256), F32),
@@ -703,7 +690,7 @@
         out_shape=jax.ShapeDtypeStruct(view.shape, BF16),
         compiler_params=params(),
         name="restore",
-    )(frame_pick, cotangent, x_aligned, inverse, gain, conv_weight, returned)
+    )(frame_pick, cotangent, x_aligned, inverse, slopes, band, returned)
     result = result.reshape(frames, row_count, merged // 128, samples, 128).transpose(3, 0, 1, 2, 4)
     return with_layout_constraint(result, order).reshape(features.shape)
 

time: 170 us -> 158 us (0.929)
  blocking collectives: 14.8 us -> 0 us
  starting transfers between devices: 6.59 us -> 11.8 us
  waiting for transfers between devices: 52.6 us -> 48.1 us
  Pallas kernels: 78 us -> 79.7 us
    all_to_all x1 -> x0, blocking collectives: 14.8 us -> none  [local(): lax.all_to_all(decoded, TILE, split_axis=0, concat_axis=0, tiled=True)]
    all_to_all x0 -> x1, waiting for transfers between devices: none -> 11.2 us  [local(): lax.all_to_all(decoded, TILE, split_axis=0, concat_axis=0, tiled=True)]
    all_gather x1, waiting for transfers between devices: 31.3 us -> 22.9 us  [packed_weights(): lax.all_gather(mine, TILE + ('sample',), axis=0, axis_index_groups=[group])]
    pallas_call x1, Pallas kernels: 23.7 us -> 31.7 us  [local(): pl.pallas_call(functools.partial(decode_kernel, row_block), grid=(frames,...]
    ppermute x1 -> x0, waiting for transfers between devices: 7.29 us -> none  [local(): other = lax.ppermute(packed, 'core', [(0, 1), (1, 0)])]
    pallas_call x1, Pallas kernels: 30.1 us -> 23.8 us  [local(): pl.pallas_call(functools.partial(restore_kernel, row_block), grid=(frames...]
    all_to_all x0 -> x1, starting transfers between devices: none -> 5.18 us  [local(): lax.all_to_all(decoded, TILE, split_axis=0, concat_axis=0, tiled=True)]
  transfers between devices with their start and end apart: 4 -> 4, of which waited for: 4 -> 4; matrix products, arithmetic and copies ran while one was open for 1% -> 1% of each run, Pallas kernels for 14% -> 20%
where the time goes in v5:
time: 158 us; the launch traced here: 157 us
  Pallas kernels  79.7 us (50%)
  waiting for transfers between devices  48.1 us (30%)
  between operations  13.5 us (9%)
  starting transfers between devices  11.8 us (7%)
  local copies, waits for them, and re-layouts  3.56 us (2%)
    pallas_call x1, Pallas kernels, local(): pl.pallas_call(functools.partial(decode_kernel, row_block), grid=(frames,...  31.7 us
    pallas_call x1, Pallas kernels, local(): pl.pallas_call(functools.partial(restore_kernel, row_block), grid=(frames...  23.8 us
    all_gather x1, waiting for transfers between devices, packed_weights(): lax.all_gather(mine, TILE + ('sample',), axis=0, axis_index_groups=[group])  22.9 us
    pallas_call x1, Pallas kernels, local(): pl.pallas_call(functools.partial(reward_kernel, row_count, tiles, samples...  22.3 us
    all_to_all x1, waiting for transfers between devices, local(): lax.all_to_all(decoded, TILE, split_axis=0, concat_axis=0, tiled=True)  11.2 us
    all_to_all x1, waiting for transfers between devices, local(): lax.all_to_all(mine, TILE + ('sample',), split_axis=0, concat_axis=0, til...  7.1 us
    all_to_all x1, waiting for transfers between devices, local(): lax.all_to_all(grads, TILE, split_axis=0, concat_axis=0, tiled=True)  6.88 us
    all_to_all x1, starting transfers between devices, local(): lax.all_to_all(decoded, TILE, split_axis=0, concat_axis=0, tiled=True)  5.18 us
  transfers between devices with their start and end apart: 4, of which 4 were waited for; matrix products, arithmetic and copies ran while one was open for 1% of the time, Pallas kernels for 20%

profile of v5, /device:TPU:0, one launch (start us, length us, event | category | flops | bytes accessed | tf_op | source)
XLA Modules:
  0.0 157.4 jit_solution(13575483625086451585)
XLA Ops:
  6.5 0.0 copy-start.3
  6.5 0.0 copy-start.2
  6.5 0.0 all-gather.3.cloned.1.call-start
  6.5 1.9 %pack.1 = bf16[1120,128]{1,0:T(8,128)(2,1)} custom-call(s32[1]{0:T(128)} %bitcast.4.z_ref, bf16[320,240]{1,0:T(8,128)(2,1)} %rows_ref.1, bf16[160,160]{1,0:T(8,128)(2,1)} %out_ref.1, bf16[32,160]{1,0:T(8,128)(2,1)} %place_ref.1, bf16[160,588]{1,0:T(8,128)(2,1)} %bitcast.22), custom_call_target="tpu_custom_call" | custom-call | tf_op jit(solution)/shard_map/pack/pallas_call | solution.py:531
  8.4 0.0 all-gather.3.cloned.1.call-update
  8.4 31.7 %decode.1 = (bf16[8,2,3,32,128]{4,3,2,1,0:T(8,128)(2,1)}, bf16[9,28,2,96,128]{4,3,2,1,0:T(8,128)(2,1)}, f32[9,28,2,128]{3,2,1,0:T(2,128)}, bf16[9,28,2,96,128]{4,3,2,1,0:T(8,128)(2,1)}, bf16[1344,432]{1,0:T(8,128)(2,1)}) custom-call(s32[2,8]{1,0:T(2,128)} %pick_ref.3, bf16[9,28,168,128]{3,2,1,0:T(8,128)(2,1)} %bitcast.20, f32[1,96]{1,0:T(1,128)} %bitcast.23, ...), custom_call_target="tpu_custom_call" | custom-call | tf_op jit(solution)/shard_map/decode/pallas_call | solution.py:594
  40.2 5.2 %all-to-all-start = ((bf16[8,2,3,32,128]{4,3,2,1,0:T(8,128)(2,1)}), bf16[8,2,3,32,128]{4,3,2,1,0:T(8,128)(2,1)S(1)}, u32[]{:S(2)}, u32[]{:S(2)}) async-start(bf16[8,2,3,32,128]{4,3,2,1,0:T(8,128)(2,1)} %get-tuple-element.12), calls=%async_computation | async-start | bytes 786432 | tf_op jit(solution)/shard_map/all_to_all | solution.py:621
  45.3 0.0 copy-done.3
  45.4 0.0 copy-done.2
  45.4 0.1 reshape.51
  45.5 0.1 reshape.53
  45.5 0.6 broadcast_in_dim.7.head_ref
  46.1 11.2 %all-to-all-done.part_ref = bf16[8,2,3,32,128]{4,3,2,1,0:T(8,128)(2,1)S(1)} async-done(((bf16[8,2,3,32,128]{4,3,2,1,0:T(8,128)(2,1)}), bf16[8,2,3,32,128]{4,3,2,1,0:T(8,128)(2,1)S(1)}, u32[]{:S(2)}, u32[]{:S(2)}) %all-to-all-start) | async-done | bytes 393248 | tf_op jit(solution)/shard_map/all_to_all | solution.py:621
  57.3 0.0 copy-start.1
  57.3 22.9 %all-gather.3.cloned.1.call-done = bf16[35840,128]{1,0:T(8,128)(2,1)} async-done(((bf16[1120,128]{1,0:T(8,128)(2,1)}), bf16[35840,128]{1,0:T(8,128)(2,1)}) %all-gather.3.cloned.1.call-update) | async-done | bytes 9175056 | tf_op jit(solution)/shard_map/all_gather | solution.py:539
  80.2 0.0 copy-done.1
  80.2 22.3 %reward.1 = (bf16[8,2,3,32,128]{4,3,2,1,0:T(8,128)(2,1)}, f32[8,128]{1,0:T(8,128)}) custom-call(bf16[8,2,3,32,128]{4,3,2,1,0:T(8,128)(2,1)} %copy-done.1, bf16[32,1120,128]{2,1,0:T(8,128)(2,1)} %bitcast.21, f32[1,1280]{1,0:T(1,128)} %broadcast_in_dim.7.head_ref), custom_call_target="tpu_custom_call" | custom-call | tf_op jit(solution)/shard_map/reward/pallas_call | solution.py:627
  102.5 0.8 slice_reduce_fusion.1
  103.3 0.1 pad_maximum_fusion.1
  103.4 0.6 broadcast_in_dim.8
  104.0 3.2 %all-to-all-start.1 = ((f32[32,1,4]{2,1,0:T(1,128)}), f32[32,1,4]{2,1,0:T(1,128)S(1)}, u32[]{:S(2)}, u32[]{:S(2)}) async-start(f32[32,1,4]{2,1,0:T(1,128)} %broadcast_in_dim.8), calls=%async_computation.1 | async-start | bytes 32768 | tf_op jit(solution)/shard_map/all_to_all | solution.py:664
  107.2 7.1 %all-to-all-done.1 = f32[32,1,4]{2,1,0:T(1,128)S(1)} async-done(((f32[32,1,4]{2,1,0:T(1,128)}), f32[32,1,4]{2,1,0:T(1,128)S(1)}, u32[]{:S(2)}, u32[]{:S(2)}) %all-to-all-start.1) | async-done | bytes 544 | tf_op jit(solution)/shard_map/all_to_all | solution.py:664
  114.3 3.5 %all-to-all-start.2 = ((bf16[8,2,3,32,128]{4,3,2,1,0:T(8,128)(2,1)}), bf16[8,2,3,32,128]{4,3,2,1,0:T(8,128)(2,1)S(1)}, u32[]{:S(2)}, u32[]{:S(2)}) async-start(bf16[8,2,3,32,128]{4,3,2,1,0:T(8,128)(2,1)} %get-tuple-element.18), calls=%async_computation.2 | async-start | bytes 786432 | tf_op jit(solution)/shard_map/all_to_all | solution.py:666
  117.7 0.1 copy.16
  117.8 0.1 reshape.54
  117.9 0.1 copy.17
  118.0 0.1 div.17
  118.1 0.1 copy.18
  118.2 0.1 reshape_squeeze.3
  118.3 0.1 dynamic_slice.7
  118.4 0.2 fusion
  118.6 0.6 multiply_multiply_fusion.scale_ref
  119.1 6.9 %all-to-all-done.2.grad_ref = bf16[8,2,3,32,128]{4,3,2,1,0:T(8,128)(2,1)S(1)} async-done(((bf16[8,2,3,32,128]{4,3,2,1,0:T(8,128)(2,1)}), bf16[8,2,3,32,128]{4,3,2,1,0:T(8,128)(2,1)S(1)}, u32[]{:S(2)}, u32[]{:S(2)}) %all-to-all-start.2) | async-done | bytes 393248 | tf_op jit(solution)/shard_map/all_to_all | solution.py:666
  126.0 0.0 copy-start
  126.0 0.8 copy-done
  126.8 23.8 %restore.1 = bf16[9,28,168,128]{3,2,1,0:T(8,128)(2,1)} custom-call(s32[2,8]{1,0:T(2,128)} %pick_ref.3, f32[2]{0:T(128)} %multiply_multiply_fusion.scale_ref, bf16[9,28,2,96,128]{4,3,2,1,0:T(8,128)(2,1)} %get-tuple-element.14.x_ref, f32[9,28,2,128]{3,2,1,0:T(2,128)} %get-tuple-element.15.inv_ref, bf16[9,28,2,96,128]{4,3,2,1,0:T(8,128)(2,1)} %get-tuple-element.16.slope_ref, ...), custom_call_target="tpu_custom_call" | custom-call | tf_op jit(solution)/shard_map/restore/pallas_call | solution.py:680
  (8 shorter events, 0.1 us)
Async XLA Ops:
  6.5 38.8 %copy-start.3 = (s32[2]{0:T(128)S(1)}, s32[2]{0:T(128)}, u32[]{:S(2)}) copy-start(s32[2]{0:T(128)} %param.18) | copy-start | bytes 28
  6.5 38.8 %copy-start.2 = (f32[1280]{0:T(1024)S(1)}, f32[1280]{0:T(1024)}, u32[]{:S(2)}) copy-start(f32[1280]{0:T(1024)} %param.17) | copy-start | bytes 15364
  6.5 73.7 %all-gather.3.cloned.1.call-start = ((), (), s32[]{:S(2)}) async-start(), calls=%async_computation.3 | async-start | bytes 9461760 | tf_op jit(solution)/shard_map/all_gather | solution.py:539
  40.2 17.2 %all-to-all-start = ((bf16[8,2,3,32,128]{4,3,2,1,0:T(8,128)(2,1)}), bf16[8,2,3,32,128]{4,3,2,1,0:T(8,128)(2,1)S(1)}, u32[]{:S(2)}, u32[]{:S(2)}) async-start(bf16[8,2,3,32,128]{4,3,2,1,0:T(8,128)(2,1)} %get-tuple-element.12), calls=%async_computation | async-start | bytes 786432 | tf_op jit(solution)/shard_map/all_to_all | solution.py:621
  57.3 22.9 %copy-start.1 = (bf16[8,2,3,32,128]{4,3,2,1,0:T(8,128)(2,1)}, bf16[8,2,3,32,128]{4,3,2,1,0:T(8,128)(2,1)S(1)}, u32[]{:S(2)}) copy-start(bf16[8,2,3,32,128]{4,3,2,1,0:T(8,128)(2,1)S(1)} %all-to-all-done.part_ref) | copy-start | bytes 1179652
  104.0 10.3 %all-to-all-start.1 = ((f32[32,1,4]{2,1,0:T(1,128)}), f32[32,1,4]{2,1,0:T(1,128)S(1)}, u32[]{:S(2)}, u32[]{:S(2)}) async-start(f32[32,1,4]{2,1,0:T(1,128)} %broadcast_in_dim.8), calls=%async_computation.1 | async-start | bytes 32768 | tf_op jit(solution)/shard_map/all_to_all | solution.py:664
  114.3 11.7 %all-to-all-start.2 = ((bf16[8,2,3,32,128]{4,3,2,1,0:T(8,128)(2,1)}), bf16[8,2,3,32,128]{4,3,2,1,0:T(8,128)(2,1)S(1)}, u32[]{:S(2)}, u32[]{:S(2)}) async-start(bf16[8,2,3,32,128]{4,3,2,1,0:T(8,128)(2,1)} %get-tuple-element.18), calls=%async_computation.2 | async-start | bytes 786432 | tf_op jit(solution)/shard_map/all_to_all | solution.py:666
  126.0 0.8 copy-start
Sparse Core Ops, SparseCore 0:
  9.0 71.1 all-gather.2

commit v6 on v5

--- a/solution.py
+++ b/solution.py
@@ -21,6 +21,8 @@
 COLS = 112
 SPANS = CH // 8
 OUT_ROWS = 27 * 16
+BACK = 6
+BACK_ROWS = 3 * 80
 NT = 8
 NZ = 4
 PACK = 1120
@@ -60,7 +62,7 @@
     return jnp.where(lane_iota(8) < COLS - 16 * sub_iota(8), turned, pltpu.roll(turned, 7, 0))
 
 
-def banded(weight_ref, taps, row_block, transposed):
+def load_taps(weight_ref, taps):
     taps[...] = jnp.zeros(taps.shape, F32)
     for a in range(3):
         for b in range(3):
@@ -68,33 +70,51 @@
                 for o in range(3):
                     at = (a * 3 + e) * 3 + o
                     taps[b, at : at + 1, :] = weight_ref[a, b, e, o : o + 1, :].astype(F32)
+
+
+def row_of(shape, dim):
+    at = lax.broadcasted_iota(jnp.int32, shape, dim)
+    return ((at.astype(F32) + 0.5) * (1.0 / CH)).astype(jnp.int32)
+
+
+def banded(taps, row_block):
     inner = row_block * CH
     pick = (
         lax.broadcasted_iota(jnp.int32, (OUT_ROWS, 32), 0) // 16
         == lax.broadcasted_iota(jnp.int32, (OUT_ROWS, 32), 1)
     ).astype(BF16)
-    if transposed:
-        shape, p_dim, r_dim = (inner, OUT_ROWS), 1, 0
-        grow_shape, grow_dim = (inner, CH), 0
-    else:
-        shape, p_dim, r_dim = (OUT_ROWS, inner), 0, 1
-        grow_shape, grow_dim = (CH, inner), 1
-    at = lax.broadcasted_iota(jnp.int32, grow_shape, grow_dim)
-    at = at - CH * ((at.astype(F32) + 0.5) * (1.0 / CH)).astype(jnp.int32)
-    grow = (at == lax.broadcasted_iota(jnp.int32, grow_shape, 1 - grow_dim)).astype(BF16)
-    p_at = lax.broadcasted_iota(jnp.int32, shape, p_dim) % 16
-    r_at = lax.broadcasted_iota(jnp.int32, shape, r_dim)
-    r_at = ((r_at.astype(F32) + 0.5) * (1.0 / CH)).astype(jnp.int32)
+    at = lax.broadcasted_iota(jnp.int32, (CH, inner), 1) - CH * row_of((CH, inner), 1)
+    grow = (at == lax.broadcasted_iota(jnp.int32, (CH, inner), 0)).astype(BF16)
+    shape = (OUT_ROWS, inner)
+    p_at = lax.broadcasted_iota(jnp.int32, shape, 0) % 16
+    r_at = row_of(shape, 1)
     total = jnp.zeros(shape, F32)
     for b in range(3):
-        rows = jnp.dot(pick, taps[b].astype(BF16), preferred_element_type=F32).astype(BF16)
-        if transposed:
-            full = lax.dot_general(
-                grow, rows, (((1,), (1,)), ((), ())), preferred_element_type=F32
-            )
-        else:
-            full = jnp.dot(rows, grow, preferred_element_type=F32)
-        total = jnp.where(p_at == r_at + 2 - b, full, total)
+        rows = nn_dot(pick, taps[b].astype(BF16)).astype(BF16)
+        total = jnp.where(p_at == r_at + 2 - b, nn_dot(rows, grow), total)
+    return total.astype(BF16)
+
+
+def banded_back(taps):
+    inner = BACK * CH
+
+    def column_of(shape, dim):
+        at = lax.broadcasted_iota(jnp.int32, shape, dim)
+        a = (at >= 80).astype(jnp.int32) + (at >= 160).astype(jnp.int32)
+        return a, at - 80 * a
+
+    a, rest = column_of((BACK_ROWS, 32), 0)
+    tap = jnp.where(rest // 8 < 9, 9 * a + rest // 8, 31)
+    pick = (tap == lax.broadcasted_iota(jnp.int32, (BACK_ROWS, 32), 1)).astype(BF16)
+    at = lax.broadcasted_iota(jnp.int32, (inner, CH), 0) - CH * row_of((inner, CH), 0)
+    grow = (at == lax.broadcasted_iota(jnp.int32, (inner, CH), 1)).astype(BF16)
+    shape = (inner, BACK_ROWS)
+    p_at = column_of(shape, 1)[1] % 8
+    r_at = row_of(shape, 0)
+    total = jnp.zeros(shape, F32)
+    for b in range(3):
+        rows = nn_dot(pick, taps[b].astype(BF16)).astype(BF16)
+        total = jnp.where(p_at == r_at + 2 - b, nt_dot(grow, rows), total)
     return total.astype(BF16)
 
 
@@ -110,15 +130,16 @@
     return found
 
 
-def decode_kernel(row_block, pick_ref, x_ref, gain_ref, weight_ref, out_ref, x_out, inv_out, slope_out, turned_out, band, taps, gains, raw, operand, acc, final):
+def decode_kernel(row_block, pick_ref, x_ref, gain_ref, weight_ref, out_ref, x_out, slope_out, turned_out, band, taps, gains, raw, operand, acc, final):
     t = pl.program_id(0)
     blocks = x_ref.shape[1] // row_block
     rows = out_ref.shape[3]
 
     @pl.when(t == 0)
     def _():
-        band[...] = banded(weight_ref, taps, row_block, False)
-        turned_out[...] = banded(weight_ref, taps, row_block, True)
+        load_taps(weight_ref, taps)
+        band[...] = banded(taps, row_block)
+        turned_out[...] = banded_back(taps)
         gains[...] = half_gains(gain_ref)
         acc[...] = jnp.zeros(acc.shape, F32)
         raw[...] = jnp.zeros(raw.shape, F32)
@@ -134,10 +155,9 @@
                     square = square + found[g] * found[g]
                 second = jnp.sum(square, axis=0, keepdims=True) * (1.0 / CH)
                 inv = lax.rsqrt(second + 1e-06)
-                inv_out[0, k * row_block + row, s : s + 1, :] = inv
                 for m in range(SPANS // 2):
                     x_out[0, k * row_block + row, s, 16 * m : 16 * m + 16, :] = jnp.concatenate(
-                        [found[2 * m], found[2 * m + 1]], axis=0
+                        [found[2 * m] * inv, found[2 * m + 1] * inv], axis=0
                     ).astype(BF16)
                     acts, slopes = [], []
                     for g in (2 * m, 2 * m + 1):
@@ -146,7 +166,7 @@
                         th = jnp.tanh(half)
                         rest = half - half * th
                         acts.append(half + half * th)
-                        slopes.append((gain + gain * th) * (1.0 + rest))
+                        slopes.append((gain * inv) * (1.0 + th) * (1.0 + rest))
                     slope_out[0, k * row_block + row, s, 16 * m : 16 * m + 16, :] = jnp.concatenate(
                         slopes, axis=0
                     ).astype(BF16)
@@ -186,63 +206,63 @@
         acc[k, 2] = jnp.zeros(acc.shape[2:], F32)
 
 
-def restore_kernel(row_block, pick_ref, scale_ref, x_ref, inv_ref, slope_ref, band, grad_ref, out_ref, back, shifted, coming):
+def restore_kernel(pick_ref, scale_ref, x_ref, slope_ref, band, grad_ref, out_ref, back, shifted, coming):
     t = pl.program_id(0)
     frames = pl.num_programs(0)
-    blocks = x_ref.shape[1] // row_block
+    row_count = x_ref.shape[1]
+    starts = range(0, row_count, BACK)
     rows = grad_ref.shape[3]
 
     @pl.when(t == 0)
     def _():
         shifted[...] = jnp.zeros(shifted.shape, BF16)
         lane = lane_iota(rows)
+        blank = jnp.zeros((8, 128), F32)
 
         def one_frame(frame, carry):
             for s in range(2):
                 entry = entry_of(pick_ref, s, frame)
                 scale = jnp.where(entry >= 0, scale_ref[s], 0.0)
                 source = jnp.maximum(entry, 0)
+                moved = [[], [], []]
                 for o in range(3):
                     value = grad_ref[source, s, o].astype(F32) * scale
                     value = jnp.where(lane < COLS, value, 0.0)
-                    for e, moved in enumerate((pltpu.roll(value, 127, 1), value, pltpu.roll(value, 1, 1))):
-                        for k in range(blocks):
-                            start = k * row_block
-                            shifted[frame, k, 48 * e + 16 * o : 48 * e + 16 * o + 16, 128 * s : 128 * s + 128] = moved[
-                                start : start + 16
-                            ].astype(BF16)
+                    for e, turned in enumerate((pltpu.roll(value, 127, 1), value, pltpu.roll(value, 1, 1))):
+                        moved[e].append(turned)
+                for k, start in enumerate(starts):
+                    block = [turned[start : start + 8] for some in moved for turned in some]
+                    shifted[frame, k, :, 128 * s : 128 * s + 128] = jnp.concatenate(
+                        block + [blank], axis=0
+                    ).astype(BF16)
             return carry
 
         lax.fori_loop(0, frames, one_frame, 0)
 
-    for k in range(blocks):
+    for k, start in enumerate(starts):
+        count = min(BACK, row_count - start)
         operand = jnp.concatenate([shifted[t + 2 - a, k] for a in range(3)], axis=0)
-        coming[k] = jnp.dot(band[...], operand, preferred_element_type=F32)
-
-        def one_row(row, at):
+        coming[k, 0 : count * CH, :] = nn_dot(band[0 : count * CH, :], operand)
+        for local in range(count):
+            row = start + local
             for s in range(2):
-                inv = inv_ref[0, k * row_block + row, s : s + 1, :]
                 outs, units, total = [], [], None
                 for m in range(SPANS // 2):
-                    pair = x_ref[0, k * row_block + row, s, 16 * m : 16 * m + 16, :].astype(F32)
-                    slopes = slope_ref[0, k * row_block + row, s, 16 * m : 16 * m + 16, :].astype(F32)
-                    for local in range(2):
-                        g = 2 * m + local
-                        unit = pair[8 * local : 8 * local + 8] * inv
-                        start = row * CH + 8 * g
-                        cot = coming[k, start : start + 8, 128 * s : 128 * s + 128]
-                        out = cot * slopes[8 * local : 8 * local + 8]
+                    pair = x_ref[0, row, s, 16 * m : 16 * m + 16, :].astype(F32)
+                    slopes = slope_ref[0, row, s, 16 * m : 16 * m + 16, :].astype(F32)
+                    for part in range(2):
+                        g = 2 * m + part
+                        unit = pair[8 * part : 8 * part + 8]
+                        at = local * CH + 8 * g
+                        out = coming[k, at : at + 8, 128 * s : 128 * s + 128] * slopes[8 * part : 8 * part + 8]
                         outs.append(out)
                         units.append(unit)
                         total = out * unit if g == 0 else total + out * unit
                 factor = jnp.sum(total, axis=0, keepdims=True) * (1.0 / CH)
                 for g in range(SPANS):
-                    result = tiles_of((outs[g] - units[g] * factor) * inv)
-                    back[at, pl.ds(14 * g + s, 7, stride=2), :] = result[0:7]
-            out_ref[0, k * row_block + row] = back[at].astype(BF16)
-
-        for row in range(row_block):
-            one_row(row, row)
+                    result = tiles_of(outs[g] - units[g] * factor)
+                    back[row % back.shape[0], pl.ds(14 * g + s, 7, stride=2), :] = result[0:7]
+            out_ref[0, row] = back[row % back.shape[0]].astype(BF16)
 
 
 def nt_dot(one, two):
@@ -263,27 +283,10 @@
     return jnp.concatenate([high, low], axis=0)
 
 
-def reward_kernel(
-    row_count, tiles, samples,
-    part_ref, packed_ref, head_ref,
-    out_ref, score_ref,
-    pack, arrived, frame, flip, embed, outw, place, patches, tokens, normed, normed16, slots, weights, dslots, dnormed, rows8, abar, order,
-):
+def patch_kernel(row_count, tiles, samples, part_ref, inputs_ref, order, frame, flip, patches):
     height = row_count * tiles
     patch_rows = height // PATCH
     lane64 = lane_iota(8) < 64
-    lane = lane_iota(NTOK)
-    count = samples * NTOK
-
-    copies = []
-    for part, (begin, end) in enumerate(((880, 1120), (640, 880), (0, 640))):
-        copies.append(
-            pltpu.make_async_copy(
-                packed_ref.at[:, begin:end, :], pack.at[:, begin:end, :], arrived.at[part]
-            )
-        )
-        copies[-1].start()
-
     inputs = order.shape[1]
     pixel = lax.broadcasted_iota(jnp.int32, (64, inputs), 0)
     column = lax.broadcasted_iota(jnp.int32, (64, inputs), 1)
@@ -316,6 +319,31 @@
                 patches[token : token + 8, 128 * y : 128 * y + 128] = jnp.where(lane64, even, pltpu.roll(odd, 64, 1))
                 patches[token + 8 : token + 16, 128 * y : 128 * y + 128] = jnp.where(lane64, pltpu.roll(even, 64, 1), odd)
 
+    inputs_ref[...] = nn_dot(patches[...].astype(BF16), order[...]).astype(BF16)
+
+
+def reward_kernel(
+    row_count, tiles, samples,
+    inputs_ref, order, packed_ref, head_ref,
+    out_ref, score_ref,
+    pack, arrived, frame, flip, embed, outw, place, patches, tokens, normed, normed16, slots, weights, dslots, dnormed, rows8, abar,
+):
+    height = row_count * tiles
+    patch_rows = height // PATCH
+    lane64 = lane_iota(8) < 64
+    lane = lane_iota(NTOK)
+    count = samples * NTOK
+
+    copies = []
+    for part, (begin, end) in enumerate(((880, 1120), (640, 880), (0, 640))):
+        copies.append(
+            pltpu.make_async_copy(
+                packed_ref.at[:, begin:end, :], pack.at[:, begin:end, :], arrived.at[part]
+            )
+        )
+        copies[-1].start()
+
+    flip[...] = jnp.zeros(flip.shape, F32)
     copies[0].wait()
     copies[1].wait()
 
@@ -357,8 +385,7 @@
                 if q == 3:
                     place[32 * z : 32 * z + 32, at : at + 128] = found[16:48]
 
-    patches16 = nn_dot(patches[...].astype(BF16), order[...]).astype(BF16)
-    token_value = nt_dot(patches16, embed[...])
+    token_value = nt_dot(inputs_ref[...], embed[...])
     rows8[...] = jnp.zeros(rows8.shape, F32)
     abar[...] = jnp.zeros(abar.shape, F32)
     place_value = place[...].astype(F32)
@@ -589,13 +616,12 @@
     sent_spec = pl.BlockSpec(sent, lambda t: (0, 0, 0, 0, 0))
     aligned = (frames, row_count, samples, CH, 128)
     aligned_spec = pl.BlockSpec((1,) + aligned[1:], lambda t: (t, 0, 0, 0, 0))
-    inv_spec = pl.BlockSpec((1, row_count, samples, 128), lambda t: (t, 0, 0, 0))
-    band_spec = pl.BlockSpec((inner, OUT_ROWS), lambda t: (0, 0))
-    decoded, x_aligned, inverse, slopes, band = pl.pallas_call(
+    band_spec = pl.BlockSpec((BACK * CH, BACK_ROWS), lambda t: (0, 0))
+    decoded, x_aligned, slopes, band = pl.pallas_call(
         functools.partial(decode_kernel, row_block),
         grid=(frames,),
         in_specs=[smem, view_spec, gain_spec, taps_spec],
-        out_specs=[sent_spec, aligned_spec, inv_spec, aligned_spec, band_spec],
+        out_specs=[sent_spec, aligned_spec, aligned_spec, band_spec],
         scratch_shapes=[
             pltpu.VMEM((OUT_ROWS, inner), BF16),
             pltpu.VMEM((3, 32, CH), F32),
@@ -608,9 +634,8 @@
         out_shape=[
             jax.ShapeDtypeStruct(sent, BF16),
             jax.ShapeDtypeStruct(aligned, BF16),
-            jax.ShapeDtypeStruct((frames, row_count, samples, 128), F32),
             jax.ShapeDtypeStruct(aligned, BF16),
-            jax.ShapeDtypeStruct((inner, OUT_ROWS), BF16),
+            jax.ShapeDtypeStruct((BACK * CH, BACK_ROWS), BF16),
         ],
         compiler_params=params(),
         name="decode",
@@ -624,6 +649,15 @@
     head = jnp.concatenate([head[:, :128].reshape(-1), head[:, 128:].reshape(-1)])[None, :]
     height = row_count * tiles
     count = samples * NTOK
+    frame_scratch = pltpu.VMEM((samples, 3, height + 48, 128), F32)
+    flip_scratch = pltpu.VMEM((samples * height // (2 * PATCH), 2, 128, 128), F32)
+    inputs, input_order = pl.pallas_call(
+        functools.partial(patch_kernel, row_count, tiles, samples),
+        out_shape=[jax.ShapeDtypeStruct((count, 640), BF16), jax.ShapeDtypeStruct((KIN, 640), BF16)],
+        scratch_shapes=[frame_scratch, flip_scratch, pltpu.VMEM((count, KIN), F32)],
+        compiler_params=params(),
+        name="patches",
+    )(owned)
     grads, scores = pl.pallas_call(
         functools.partial(reward_kernel, row_count, tiles, samples),
         out_shape=[
@@ -632,14 +666,15 @@
         ],
         in_specs=[
             pl.BlockSpec(memory_space=pltpu.VMEM),
+            pl.BlockSpec(memory_space=pltpu.VMEM),
             pl.BlockSpec(memory_space=pl.ANY),
             pl.BlockSpec(memory_space=pltpu.VMEM),
         ],
         scratch_shapes=[
             pltpu.VMEM(packed.shape, BF16),
             pltpu.SemaphoreType.DMA((3,)),
-            pltpu.VMEM((samples, 3, height + 48, 128), F32),
-            pltpu.VMEM((samples * height // (2 * PATCH), 2, 128, 128), F32),
+            frame_scratch,
+            flip_scratch,
             pltpu.VMEM((D, 640), BF16),
             pltpu.VMEM((HEADS * 128, D), BF16),
             pltpu.VMEM((NTOK, D), BF16),
@@ -653,11 +688,10 @@
             pltpu.VMEM((count, D), F32),
             pltpu.VMEM((2, 8, D), F32),
             pltpu.VMEM((8, HEADS * 128), F32),
-            pltpu.VMEM((KIN, 640), BF16),
         ],
         compiler_params=params(),
         name="reward",
-    )(owned, packed, head)
+    )(inputs, input_order, packed, head)
 
     mine = jnp.concatenate([scores[:samples, 0], group_index.astype(F32)])
     mine = jnp.broadcast_to(mine[None], (tiles * parts, 2 * samples))
@@ -678,19 +712,19 @@
     cotangent = -LOSS_SCALE * advantage / SCORED
 
     result = pl.pallas_call(
-        functools.partial(restore_kernel, row_block),
+        restore_kernel,
         grid=(frames,),
-        in_specs=[smem, smem, aligned_spec, inv_spec, aligned_spec, band_spec, sent_spec],
+        in_specs=[smem, smem, aligned_spec, aligned_spec, band_spec, sent_spec],
         out_specs=view_spec,
         scratch_shapes=[
             pltpu.VMEM((row_block, samples * merged // 128, 128), F32),
-            pltpu.VMEM((frames + 2, blocks, 144, 256), BF16),
-            pltpu.VMEM((blocks, inner, 256), F32),
+            pltpu.VMEM((frames + 2, -(-row_count // BACK), 80, 256), BF16),
+            pltpu.VMEM((-(-row_count // BACK), BACK * CH, 256), F32),
         ],
         out_shape=jax.ShapeDtypeStruct(view.shape, BF16),
         compiler_params=params(),
         name="restore",
-    )(frame_pick, cotangent, x_aligned, inverse, slopes, band, returned)
+    )(frame_pick, cotangent, x_aligned, slopes, band, returned)
     result = result.reshape(frames, row_count, merged // 128, samples, 128).transpose(3, 0, 1, 2, 4)
     return with_layout_constraint(result, order).reshape(features.shape)
 

time: 158 us -> 155 us (0.981)
  waiting for transfers between devices: 48.1 us -> 44.8 us
    all_gather x1, waiting for transfers between devices: 22.9 us -> 19.6 us  [packed_weights(): lax.all_gather(mine, TILE + ('sample',), axis=0, axis_index_groups=[group])]
    pallas_call x1 -> x2, Pallas kernels: 23.8 us -> 23.6 us  [the longest x1 20.4 us: local(): pl.pallas_call(restore_kernel, grid=(frames,), in_specs=[smem, smem, alig...]
  transfers between devices with their start and end apart: 4 -> 4, of which waited for: 4 -> 4; matrix products, arithmetic and copies ran while one was open for 1% -> 1% of each run, Pallas kernels for 20% -> 22%
where the time goes in v6:
time: 155 us; the launch traced here: 154 us
  Pallas kernels  78.3 us (51%)
  waiting for transfers between devices  44.8 us (29%)
  between operations  13.5 us (9%)
  starting transfers between devices  12.2 us (8%)
  local copies, waits for them, and re-layouts  4.32 us (3%)
    pallas_call x1, Pallas kernels, local(): pl.pallas_call(functools.partial(decode_kernel, row_block), grid=(frames,...  30.8 us
    pallas_call x1, Pallas kernels, local(): pl.pallas_call(functools.partial(reward_kernel, row_count, tiles, samples...  22 us
    pallas_call x1, Pallas kernels, local(): pl.pallas_call(restore_kernel, grid=(frames,), in_specs=[smem, smem, alig...  20.4 us
    all_gather x1, waiting for transfers between devices, packed_weights(): lax.all_gather(mine, TILE + ('sample',), axis=0, axis_index_groups=[group])  19.6 us
    all_to_all x1, waiting for transfers between devices, local(): lax.all_to_all(decoded, TILE, split_axis=0, concat_axis=0, tiled=True)  11.2 us
    all_to_all x1, waiting for transfers between devices, local(): lax.all_to_all(mine, TILE + ('sample',), split_axis=0, concat_axis=0, til...  7.1 us
    all_to_all x1, waiting for transfers between devices, local(): lax.all_to_all(grads, TILE, split_axis=0, concat_axis=0, tiled=True)  6.86 us
    all_to_all x1, starting transfers between devices, local(): lax.all_to_all(decoded, TILE, split_axis=0, concat_axis=0, tiled=True)  5.17 us
  transfers between devices with their start and end apart: 4, of which 4 were waited for; matrix products, arithmetic and copies ran while one was open for 1% of the time, Pallas kernels for 22%

profile of v6, /device:TPU:0, one launch (start us, length us, event | category | flops | bytes accessed | tf_op | source)
XLA Modules:
  0.0 154.0 jit_solution(1180307348076156420)
XLA Ops:
  6.5 0.0 copy-start.3
  6.5 0.0 copy-start.2
  6.5 0.0 all-gather.3.cloned.1.call-start
  6.5 1.9 %pack.1 = bf16[1120,128]{1,0:T(8,128)(2,1)} custom-call(s32[1]{0:T(128)} %bitcast.4.z_ref, bf16[320,240]{1,0:T(8,128)(2,1)} %rows_ref.1, bf16[160,160]{1,0:T(8,128)(2,1)} %out_ref.1, bf16[32,160]{1,0:T(8,128)(2,1)} %place_ref.1, bf16[160,588]{1,0:T(8,128)(2,1)} %bitcast.22), custom_call_target="tpu_custom_call" | custom-call | tf_op jit(solution)/shard_map/pack/pallas_call | solution.py:558
  8.4 0.0 all-gather.3.cloned.1.call-update
  8.5 30.8 %decode.1 = (bf16[8,2,3,32,128]{4,3,2,1,0:T(8,128)(2,1)}, bf16[9,28,2,96,128]{4,3,2,1,0:T(8,128)(2,1)}, bf16[9,28,2,96,128]{4,3,2,1,0:T(8,128)(2,1)}, bf16[576,240]{1,0:T(8,128)(2,1)}) custom-call(s32[2,8]{1,0:T(2,128)} %pick_ref.3, bf16[9,28,168,128]{3,2,1,0:T(8,128)(2,1)} %bitcast.20, f32[1,96]{1,0:T(1,128)} %bitcast.23, bf16[3,3,3,3,96]{4,3,2,1,0:T(4,128)(2,1)} %weight_ref.1), custom_call_target="tpu_custom_call" | custom-call | tf_op jit(solution)/shard_map/decode/pallas_call | solution.py:620
  39.2 5.2 %all-to-all-start = ((bf16[8,2,3,32,128]{4,3,2,1,0:T(8,128)(2,1)}), bf16[8,2,3,32,128]{4,3,2,1,0:T(8,128)(2,1)S(1)}, u32[]{:S(2)}, u32[]{:S(2)}) async-start(bf16[8,2,3,32,128]{4,3,2,1,0:T(8,128)(2,1)} %get-tuple-element.13), calls=%async_computation | async-start | bytes 786432 | tf_op jit(solution)/shard_map/all_to_all | solution.py:646
  44.4 0.0 copy-done.3
  44.4 0.0 copy-done.2
  44.4 0.1 reshape.51
  44.5 0.1 reshape.53
  44.6 0.6 broadcast_in_dim.7.head_ref
  45.2 11.2 %all-to-all-done.part_ref = bf16[8,2,3,32,128]{4,3,2,1,0:T(8,128)(2,1)S(1)} async-done(((bf16[8,2,3,32,128]{4,3,2,1,0:T(8,128)(2,1)}), bf16[8,2,3,32,128]{4,3,2,1,0:T(8,128)(2,1)S(1)}, u32[]{:S(2)}, u32[]{:S(2)}) %all-to-all-start) | async-done | bytes 393248 | tf_op jit(solution)/shard_map/all_to_all | solution.py:646
  56.4 0.0 copy-start.1
  56.4 0.7 copy-done.1
  57.1 3.2 %patches.1 = (bf16[256,640]{1,0:T(8,128)(2,1)}, bf16[896,640]{1,0:T(8,128)(2,1)}) custom-call(bf16[8,2,3,32,128]{4,3,2,1,0:T(8,128)(2,1)} %copy-done.1), custom_call_target="tpu_custom_call" | custom-call | tf_op jit(solution)/shard_map/patches/pallas_call | solution.py:654
  60.3 19.6 %all-gather.3.cloned.1.call-done = bf16[35840,128]{1,0:T(8,128)(2,1)} async-done(((bf16[1120,128]{1,0:T(8,128)(2,1)}), bf16[35840,128]{1,0:T(8,128)(2,1)}) %all-gather.3.cloned.1.call-update) | async-done | bytes 9175056 | tf_op jit(solution)/shard_map/all_gather | solution.py:566
  79.9 22.0 %reward.1 = (bf16[8,2,3,32,128]{4,3,2,1,0:T(8,128)(2,1)}, f32[8,128]{1,0:T(8,128)}) custom-call(bf16[256,640]{1,0:T(8,128)(2,1)} %get-tuple-element.14.inputs_ref, bf16[896,640]{1,0:T(8,128)(2,1)} %get-tuple-element.15.order, bf16[32,1120,128]{2,1,0:T(8,128)(2,1)} %bitcast.21, f32[1,1280]{1,0:T(1,128)} %broadcast_in_dim.7.head_ref), custom_call_target="tpu_custom_call" | custom-call | tf_op jit(solution)/shard_map/reward/pallas_call | solution.py:661
  101.9 0.8 slice_reduce_fusion.1
  102.7 0.1 pad_maximum_fusion.1
  102.8 0.6 broadcast_in_dim.8
  103.4 3.6 %all-to-all-start.1 = ((f32[32,1,4]{2,1,0:T(1,128)}), f32[32,1,4]{2,1,0:T(1,128)S(1)}, u32[]{:S(2)}, u32[]{:S(2)}) async-start(f32[32,1,4]{2,1,0:T(1,128)} %broadcast_in_dim.8), calls=%async_computation.1 | async-start | bytes 32768 | tf_op jit(solution)/shard_map/all_to_all | solution.py:698
  107.0 7.1 %all-to-all-done.1 = f32[32,1,4]{2,1,0:T(1,128)S(1)} async-done(((f32[32,1,4]{2,1,0:T(1,128)}), f32[32,1,4]{2,1,0:T(1,128)S(1)}, u32[]{:S(2)}, u32[]{:S(2)}) %all-to-all-start.1) | async-done | bytes 544 | tf_op jit(solution)/shard_map/all_to_all | solution.py:698
  114.1 3.5 %all-to-all-start.2 = ((bf16[8,2,3,32,128]{4,3,2,1,0:T(8,128)(2,1)}), bf16[8,2,3,32,128]{4,3,2,1,0:T(8,128)(2,1)S(1)}, u32[]{:S(2)}, u32[]{:S(2)}) async-start(bf16[8,2,3,32,128]{4,3,2,1,0:T(8,128)(2,1)} %get-tuple-element.20), calls=%async_computation.2 | async-start | bytes 786432 | tf_op jit(solution)/shard_map/all_to_all | solution.py:700
  117.6 0.1 copy.16
  117.7 0.1 reshape.54
  117.8 0.1 copy.17
  117.9 0.1 div.17
  118.0 0.1 copy.18
  118.1 0.1 reshape_squeeze.3
  118.2 0.1 dynamic_slice.7
  118.2 0.2 fusion
  118.4 0.6 multiply_multiply_fusion.scale_ref
  119.0 6.9 %all-to-all-done.2.grad_ref = bf16[8,2,3,32,128]{4,3,2,1,0:T(8,128)(2,1)S(1)} async-done(((bf16[8,2,3,32,128]{4,3,2,1,0:T(8,128)(2,1)}), bf16[8,2,3,32,128]{4,3,2,1,0:T(8,128)(2,1)S(1)}, u32[]{:S(2)}, u32[]{:S(2)}) %all-to-all-start.2) | async-done | bytes 393248 | tf_op jit(solution)/shard_map/all_to_all | solution.py:700
  125.9 0.0 copy-start
  125.9 0.8 copy-done
  126.7 20.4 %restore.1 = bf16[9,28,168,128]{3,2,1,0:T(8,128)(2,1)} custom-call(s32[2,8]{1,0:T(2,128)} %pick_ref.3, f32[2]{0:T(128)} %multiply_multiply_fusion.scale_ref, bf16[9,28,2,96,128]{4,3,2,1,0:T(8,128)(2,1)} %get-tuple-element.17.x_ref, bf16[9,28,2,96,128]{4,3,2,1,0:T(8,128)(2,1)} %get-tuple-element.18.slope_ref, bf16[576,240]{1,0:T(8,128)(2,1)} %get-tuple-element.19.band, ...), custom_call_target="tpu_custom_call" | custom-call | tf_op jit(solution)/shard_map/restore/pallas_call | solution.py:714
  (8 shorter events, 0.1 us)
Async XLA Ops:
  6.5 37.9 %copy-start.3 = (s32[2]{0:T(128)S(1)}, s32[2]{0:T(128)}, u32[]{:S(2)}) copy-start(s32[2]{0:T(128)} %param.18) | copy-start | bytes 28
  6.5 37.9 %copy-start.2 = (f32[1280]{0:T(1024)S(1)}, f32[1280]{0:T(1024)}, u32[]{:S(2)}) copy-start(f32[1280]{0:T(1024)} %param.17) | copy-start | bytes 15364
  6.5 73.4 %all-gather.3.cloned.1.call-start = ((), (), s32[]{:S(2)}) async-start(), calls=%async_computation.3 | async-start | bytes 9461760 | tf_op jit(solution)/shard_map/all_gather | solution.py:566
  39.2 17.2 %all-to-all-start = ((bf16[8,2,3,32,128]{4,3,2,1,0:T(8,128)(2,1)}), bf16[8,2,3,32,128]{4,3,2,1,0:T(8,128)(2,1)S(1)}, u32[]{:S(2)}, u32[]{:S(2)}) async-start(bf16[8,2,3,32,128]{4,3,2,1,0:T(8,128)(2,1)} %get-tuple-element.13), calls=%async_computation | async-start | bytes 786432 | tf_op jit(solution)/shard_map/all_to_all | solution.py:646
  56.4 0.7 copy-start.1
  103.4 10.7 %all-to-all-start.1 = ((f32[32,1,4]{2,1,0:T(1,128)}), f32[32,1,4]{2,1,0:T(1,128)S(1)}, u32[]{:S(2)}, u32[]{:S(2)}) async-start(f32[32,1,4]{2,1,0:T(1,128)} %broadcast_in_dim.8), calls=%async_computation.1 | async-start | bytes 32768 | tf_op jit(solution)/shard_map/all_to_all | solution.py:698
  114.1 11.7 %all-to-all-start.2 = ((bf16[8,2,3,32,128]{4,3,2,1,0:T(8,128)(2,1)}), bf16[8,2,3,32,128]{4,3,2,1,0:T(8,128)(2,1)S(1)}, u32[]{:S(2)}, u32[]{:S(2)}) async-start(bf16[8,2,3,32,128]{4,3,2,1,0:T(8,128)(2,1)} %get-tuple-element.20), calls=%async_computation.2 | async-start | bytes 786432 | tf_op jit(solution)/shard_map/all_to_all | solution.py:700
  125.9 0.8 copy-start
Sparse Core Ops, SparseCore 0:
  9.0 70.9 all-gather.2

commit v7 on v6

--- a/solution.py
+++ b/solution.py
@@ -43,6 +43,10 @@
 
 def lane_iota(rows):
     return lax.broadcasted_iota(jnp.int32, (rows, 128), 1)
+
+
+def left(value, amount):
+    return pltpu.roll(value, 128 - amount, 1)
 
 
 def sub_iota(rows):
@@ -206,7 +210,30 @@
         acc[k, 2] = jnp.zeros(acc.shape[2:], F32)
 
 
-def restore_kernel(pick_ref, scale_ref, x_ref, slope_ref, band, grad_ref, out_ref, back, shifted, coming):
+def cotangents(parts, here, everyone):
+    row = lax.broadcasted_iota(jnp.int32, everyone.shape, 0)
+    own = jnp.zeros((1, 128), F32)
+    layers = []
+    for z in range(parts):
+        mine = (row % parts == z) & (row < SCORED * parts)
+        found = jnp.sum(jnp.where(mine, everyone, 0.0), axis=0, keepdims=True) / SCORED
+        own = jnp.where(here == z, found, own)
+        layers.append(found)
+    prompt = left(own, 2)
+    total = jnp.zeros((1, 128), F32)
+    square = jnp.zeros((1, 128), F32)
+    for found in layers:
+        for s in range(2):
+            member = prompt == found[:, 2 + s : 3 + s]
+            reward = found[:, s : s + 1]
+            total = total + jnp.where(member, reward, 0.0)
+            square = square + jnp.where(member, reward * reward, 0.0)
+    mean = total / GROUP
+    second = square / GROUP - mean * mean
+    return -LOSS_SCALE * ((own - mean) * lax.rsqrt(second + SMOOTH)) / SCORED
+
+
+def restore_kernel(parts, pick_ref, here_ref, everyone_ref, x_ref, slope_ref, band, grad_ref, out_ref, back, shifted, coming):
     t = pl.program_id(0)
     frames = pl.num_programs(0)
     row_count = x_ref.shape[1]
@@ -218,11 +245,12 @@
         shifted[...] = jnp.zeros(shifted.shape, BF16)
         lane = lane_iota(rows)
         blank = jnp.zeros((8, 128), F32)
+        scales = cotangents(parts, here_ref[0], everyone_ref[...])
 
         def one_frame(frame, carry):
             for s in range(2):
                 entry = entry_of(pick_ref, s, frame)
-                scale = jnp.where(entry >= 0, scale_ref[s], 0.0)
+                scale = jnp.where(entry >= 0, scales[:, s : s + 1], 0.0)
                 source = jnp.maximum(entry, 0)
                 moved = [[], [], []]
                 for o in range(3):
@@ -324,9 +352,9 @@
 
 def reward_kernel(
     row_count, tiles, samples,
-    inputs_ref, order, packed_ref, head_ref,
+    group_ref, inputs_ref, order, packed_ref, head_ref,
     out_ref, score_ref,
-    pack, arrived, frame, flip, embed, outw, place, patches, tokens, normed, normed16, slots, weights, dslots, dnormed, rows8, abar,
+    pack, arrived, frame, flip, embed, outw, place, patches, tokens, normed, normed16, slots, weights, dslots, dnormed, rows8, abar, both,
 ):
     height = row_count * tiles
     patch_rows = height // PATCH
@@ -434,8 +462,11 @@
             logits = jnp.exp(logits - jnp.max(logits, axis=-1, keepdims=True))
             prob = logits / jnp.sum(logits, axis=-1, keepdims=True)
             weights[h * samples + f] = prob
-            attended = nn_dot(prob.astype(BF16), slots[2 * HEADS + h, span, :]).astype(BF16)
-            abar[f : f + 1, 128 * h : 128 * h + 128] = jnp.mean(attended.astype(F32), axis=0, keepdims=True)
+            sums = jnp.sum(prob.astype(BF16).astype(F32), axis=0, keepdims=True)
+            sums = split_two(jnp.broadcast_to(sums, (8, 128)))
+            both[h * samples + f] = sums
+            mean = nn_dot(sums, slots[2 * HEADS + h, span, :]) * (1.0 / NTOK)
+            abar[f : f + 1, 128 * h : 128 * h + 128] = mean[0:1] + mean[8:9]
 
     part = nn_dot(split_two(abar[...]), outw[...])
     pooled = rows8[0] + part[0:8] + part[8:16]
@@ -443,7 +474,13 @@
     scale = lax.rsqrt(jnp.mean(pooled * pooled, axis=-1, keepdims=True) + 1e-05)
     pooled = pooled * scale
     head = head_ref[...]
-    score_ref[...] = jnp.broadcast_to(jnp.sum(pooled * head, axis=-1, keepdims=True), (8, 128))
+    score = jnp.sum(pooled * head, axis=-1, keepdims=True)
+    lane1 = lane_iota(1)
+    sent = jnp.zeros((1, 128), F32)
+    for f in range(samples):
+        sent = jnp.where(lane1 == f, score[f : f + 1], sent)
+        sent = jnp.where(lane1 == samples + f, group_ref[f].astype(F32), sent)
+    score_ref[...] = jnp.broadcast_to(sent, score_ref.shape)
     dpooled = scale * (
         head - jnp.mean(head, axis=-1, keepdims=True) - pooled * jnp.mean(pooled * head, axis=-1, keepdims=True)
     )
@@ -452,6 +489,7 @@
     datts = nt_dot(split_two(dres), outw[...])
     datts = (datts[0:8] + datts[8:16]).astype(BF16)
 
+    first_rows = sub_iota(16) % 8 == 0
     for h in range(HEADS):
         datt = datts[:, 128 * h : 128 * h + 128]
         for f in range(samples):
@@ -463,9 +501,8 @@
             dlogit = (prob * (dweight - inner) * HD ** (-0.5)).astype(BF16)
             dslots[h, span, :] = nn_dot(dlogit, slots[HEADS + h, span, :])
             dslots[HEADS + h, span, :] = tn_dot(dlogit, slots[h, span, :])
-            dslots[2 * HEADS + h, span, :] = tn_dot(
-                prob.astype(BF16), jnp.broadcast_to(row.astype(F32), (NTOK, 128)).astype(BF16)
-            )
+            pair = jnp.where(first_rows, jnp.broadcast_to(row.astype(F32), (16, 128)), 0.0).astype(BF16)
+            dslots[2 * HEADS + h, span, :] = tn_dot(both[h * samples + f], pair)
 
     parts = []
     for i in range(NT):
@@ -662,9 +699,10 @@
         functools.partial(reward_kernel, row_count, tiles, samples),
         out_shape=[
             jax.ShapeDtypeStruct((tiles, samples, 3, sent_rows, 128), BF16),
-            jax.ShapeDtypeStruct((8, 128), F32),
+            jax.ShapeDtypeStruct((tiles * parts, 128), F32),
         ],
         in_specs=[
+            smem,
             pl.BlockSpec(memory_space=pltpu.VMEM),
             pl.BlockSpec(memory_space=pltpu.VMEM),
             pl.BlockSpec(memory_space=pl.ANY),
@@ -688,33 +726,29 @@
             pltpu.VMEM((count, D), F32),
             pltpu.VMEM((2, 8, D), F32),
             pltpu.VMEM((8, HEADS * 128), F32),
+            pltpu.VMEM((HEADS * samples, 16, 128), BF16),
         ],
         compiler_params=params(),
         name="reward",
-    )(inputs, input_order, packed, head)
-
-    mine = jnp.concatenate([scores[:samples, 0], group_index.astype(F32)])
-    mine = jnp.broadcast_to(mine[None], (tiles * parts, 2 * samples))
-    everyone = lax.all_to_all(mine, TILE + ("sample",), split_axis=0, concat_axis=0, tiled=True)
-    everyone = everyone.reshape(tiles, parts, 2, samples)
+    )(group_index, inputs, input_order, packed, head)
+
+    everyone = lax.all_to_all(scores, TILE + ("sample",), split_axis=0, concat_axis=0, tiled=True)
     returned = lax.all_to_all(grads, TILE, split_axis=0, concat_axis=0, tiled=True)
     returned = returned[:SCORED]
 
-    rewards = jnp.sum(everyone[:SCORED, :, 0], axis=0).reshape(-1) / SCORED
-    groups = everyone[0, :, 1].reshape(-1)
-    here = (lax.axis_index("sample") * samples).astype(jnp.int32)
-    own_rewards = lax.dynamic_slice_in_dim(rewards, here, samples)
-    own_groups = lax.dynamic_slice_in_dim(groups, here, samples)
-    member = (own_groups[:, None] == groups[None, :]).astype(F32)
-    mean_group = jnp.sum(member * rewards[None, :], axis=1) / GROUP
-    second_group = jnp.sum(member * (rewards * rewards)[None, :], axis=1) / GROUP - mean_group * mean_group
-    advantage = (own_rewards - mean_group) * lax.rsqrt(second_group + SMOOTH)
-    cotangent = -LOSS_SCALE * advantage / SCORED
-
+    here = lax.axis_index("sample").astype(jnp.int32).reshape(1)
     result = pl.pallas_call(
-        restore_kernel,
+        functools.partial(restore_kernel, parts),
         grid=(frames,),
-        in_specs=[smem, smem, aligned_spec, aligned_spec, band_spec, sent_spec],
+        in_specs=[
+            smem,
+            smem,
+            pl.BlockSpec((tiles * parts, 128), lambda t: (0, 0)),
+            aligned_spec,
+            aligned_spec,
+            band_spec,
+            sent_spec,
+        ],
         out_specs=view_spec,
         scratch_shapes=[
             pltpu.VMEM((row_block, samples * merged // 128, 128), F32),
@@ -724,7 +758,7 @@
         out_shape=jax.ShapeDtypeStruct(view.shape, BF16),
         compiler_params=params(),
         name="restore",
-    )(frame_pick, cotangent, x_aligned, slopes, band, returned)
+    )(frame_pick, here, everyone, x_aligned, slopes, band, returned)
     result = result.reshape(frames, row_count, merged // 128, samples, 128).transpose(3, 0, 1, 2, 4)
     return with_layout_constraint(result, order).reshape(features.shape)
 

time: 155 us -> 154 us (level)
  blocking collectives: 0 us -> 23 us
  waiting for transfers between devices: 44.8 us -> 30.8 us
  starting transfers between devices: 12.2 us -> 5.17 us
  local copies, waits for them, and re-layouts: 4.32 us -> 1.5 us
    all_to_all x0 -> x2, blocking collectives: none -> 23 us  [the longest x1 12.4 us: local(): lax.all_to_all(grads, TILE, split_axis=0, concat_axis=0, tiled=True)]
    all_to_all x2 -> x0, waiting for transfers between devices: 14 us -> none  [the longest x1 7.1 us: local(): lax.all_to_all(mine, TILE + ('sample',), split_axis=0, concat_axis=0, til...]
    all_to_all x2 -> x0, starting transfers between devices: 7.05 us -> none  [the longest x1 3.6 us: local(): lax.all_to_all(mine, TILE + ('sample',), split_axis=0, concat_axis=0, til...]
  transfers between devices with their start and end apart: 4 -> 2, of which waited for: 4 -> 2; matrix products, arithmetic and copies ran while one was open for 1% -> 1% of each run, Pallas kernels for 22% -> 22%
where the time goes in v7:
time: 154 us; the launch traced here: 153 us
  Pallas kernels  79.5 us (52%)
  waiting for transfers between devices  30.8 us (20%)
  blocking collectives  23 us (15%)
  between operations  13.4 us (9%)
  starting transfers between devices  5.17 us (3%)
    pallas_call x1, Pallas kernels, local(): pl.pallas_call(functools.partial(decode_kernel, row_block), grid=(frames,...  30.8 us
    pallas_call x1, Pallas kernels, local(): pl.pallas_call(functools.partial(reward_kernel, row_count, tiles, samples...  22.4 us
    pallas_call x1, Pallas kernels, local(): pl.pallas_call(functools.partial(restore_kernel, parts), grid=(frames,),...  21.3 us
    all_gather x1, waiting for transfers between devices, packed_weights(): lax.all_gather(mine, TILE + ('sample',), axis=0, axis_index_groups=[group])  19.5 us
    all_to_all x1, blocking collectives, local(): lax.all_to_all(grads, TILE, split_axis=0, concat_axis=0, tiled=True)  12.4 us
    all_to_all x1, waiting for transfers between devices, local(): lax.all_to_all(decoded, TILE, split_axis=0, concat_axis=0, tiled=True)  11.3 us
    all_to_all x1, blocking collectives, local(): lax.all_to_all(scores, TILE + ('sample',), split_axis=0, concat_axis=0, t...  10.6 us
    all_to_all x1, starting transfers between devices, local(): lax.all_to_all(decoded, TILE, split_axis=0, concat_axis=0, tiled=True)  5.17 us
  transfers between devices with their start and end apart: 2, of which 2 were waited for; matrix products, arithmetic and copies ran while one was open for 1% of the time, Pallas kernels for 22%

profile of v7, /device:TPU:0, one launch (start us, length us, event | category | flops | bytes accessed | tf_op | source)
XLA Modules:
  0.0 153.4 jit_solution(17755850781066241515)
XLA Ops:
  6.5 0.0 copy-start.1
  6.5 0.0 all-gather.3.cloned.1.call-start
  6.5 1.9 %pack.1 = bf16[1120,128]{1,0:T(8,128)(2,1)} custom-call(s32[1]{0:T(128)} %bitcast.z_ref.here_ref, bf16[320,240]{1,0:T(8,128)(2,1)} %rows_ref.1, bf16[160,160]{1,0:T(8,128)(2,1)} %out_ref.1, bf16[32,160]{1,0:T(8,128)(2,1)} %place_ref.1, bf16[160,588]{1,0:T(8,128)(2,1)} %bitcast.22), custom_call_target="tpu_custom_call" | custom-call | tf_op jit(solution)/shard_map/pack/pallas_call | solution.py:595
  8.4 0.0 all-gather.3.cloned.1.call-update
  8.4 30.8 %decode.1 = (bf16[8,2,3,32,128]{4,3,2,1,0:T(8,128)(2,1)}, bf16[9,28,2,96,128]{4,3,2,1,0:T(8,128)(2,1)}, bf16[9,28,2,96,128]{4,3,2,1,0:T(8,128)(2,1)}, bf16[576,240]{1,0:T(8,128)(2,1)}) custom-call(s32[2,8]{1,0:T(2,128)} %pick_ref.3, bf16[9,28,168,128]{3,2,1,0:T(8,128)(2,1)} %bitcast.20, f32[1,96]{1,0:T(1,128)} %bitcast.25, bf16[3,3,3,3,96]{4,3,2,1,0:T(4,128)(2,1)} %weight_ref.1), custom_call_target="tpu_custom_call" | custom-call | tf_op jit(solution)/shard_map/decode/pallas_call | solution.py:657
  39.2 5.2 %all-to-all-start = ((bf16[8,2,3,32,128]{4,3,2,1,0:T(8,128)(2,1)}), bf16[8,2,3,32,128]{4,3,2,1,0:T(8,128)(2,1)S(1)}, u32[]{:S(2)}, u32[]{:S(2)}) async-start(bf16[8,2,3,32,128]{4,3,2,1,0:T(8,128)(2,1)} %get-tuple-element.13), calls=%async_computation | async-start | bytes 786432 | tf_op jit(solution)/shard_map/all_to_all | solution.py:683
  44.4 0.0 copy-done.1
  44.4 0.1 reshape.30
  44.5 0.1 reshape.32
  44.6 0.6 broadcast_in_dim.7.head_ref
  45.2 11.3 %all-to-all-done.part_ref = bf16[8,2,3,32,128]{4,3,2,1,0:T(8,128)(2,1)S(1)} async-done(((bf16[8,2,3,32,128]{4,3,2,1,0:T(8,128)(2,1)}), bf16[8,2,3,32,128]{4,3,2,1,0:T(8,128)(2,1)S(1)}, u32[]{:S(2)}, u32[]{:S(2)}) %all-to-all-start) | async-done | bytes 393248 | tf_op jit(solution)/shard_map/all_to_all | solution.py:683
  56.4 0.0 copy-start
  56.4 0.7 copy-done
  57.2 3.1 %patches.1 = (bf16[256,640]{1,0:T(8,128)(2,1)}, bf16[896,640]{1,0:T(8,128)(2,1)}) custom-call(bf16[8,2,3,32,128]{4,3,2,1,0:T(8,128)(2,1)} %copy-done), custom_call_target="tpu_custom_call" | custom-call | tf_op jit(solution)/shard_map/patches/pallas_call | solution.py:691
  60.3 19.5 %all-gather.3.cloned.1.call-done = bf16[35840,128]{1,0:T(8,128)(2,1)} async-done(((bf16[1120,128]{1,0:T(8,128)(2,1)}), bf16[35840,128]{1,0:T(8,128)(2,1)}) %all-gather.3.cloned.1.call-update) | async-done | bytes 9175056 | tf_op jit(solution)/shard_map/all_gather | solution.py:603
  79.9 22.4 %reward.1 = (bf16[8,2,3,32,128]{4,3,2,1,0:T(8,128)(2,1)}, f32[32,128]{1,0:T(8,128)}) custom-call(s32[2]{0:T(128)} %group_ref.1, bf16[256,640]{1,0:T(8,128)(2,1)} %get-tuple-element.14.inputs_ref, bf16[896,640]{1,0:T(8,128)(2,1)} %get-tuple-element.15.order, bf16[32,1120,128]{2,1,0:T(8,128)(2,1)} %bitcast.21, f32[1,1280]{1,0:T(1,128)} %broadcast_in_dim.7.head_ref), custom_call_target="tpu_custom_call" | custom-call | tf_op jit(solution)/shard_map/reward/pallas_call | solution.py:698
  102.2 10.6 %all_to_all.21 = f32[32,1,128]{2,1,0:T(1,128)} all-to-all(f32[32,1,128]{2,1,0:T(1,128)} %bitcast.24), channel_id=1, replica_groups=mesh['chip'=4,'core'=2,'sample'=4] {'chip','core','sample'}, dimensions={0} | all-to-all | bytes 32768 | tf_op jit(solution)/shard_map/all_to_all | solution.py:735
  112.8 12.4 %all_to_all.22.grad_ref = bf16[8,2,3,32,128]{4,3,2,1,0:T(8,128)(2,1)} all-to-all(bf16[8,2,3,32,128]{4,3,2,1,0:T(8,128)(2,1)} %get-tuple-element.20), channel_id=1, replica_groups=mesh['chip'=4,'core'=2,'sample'=4] {'chip','core'}, dimensions={0} | all-to-all | bytes 786432 | tf_op jit(solution)/shard_map/all_to_all | solution.py:736
  125.2 21.3 %restore.1 = bf16[9,28,168,128]{3,2,1,0:T(8,128)(2,1)} custom-call(s32[2,8]{1,0:T(2,128)} %pick_ref.3, s32[1]{0:T(128)} %bitcast.z_ref.here_ref, f32[32,128]{1,0:T(8,128)} %bitcast.23, bf16[9,28,2,96,128]{4,3,2,1,0:T(8,128)(2,1)} %get-tuple-element.17.x_ref, bf16[9,28,2,96,128]{4,3,2,1,0:T(8,128)(2,1)} %get-tuple-element.18.slope_ref, ...), custom_call_target="tpu_custom_call" | custom-call | tf_op jit(solution)/shard_map/restore/pallas_call | solution.py:740
  (3 shorter events, 0.0 us)
Async XLA Ops:
  6.5 37.9 %copy-start.1 = (f32[1280]{0:T(1024)S(1)}, f32[1280]{0:T(1024)}, u32[]{:S(2)}) copy-start(f32[1280]{0:T(1024)} %param.17) | copy-start | bytes 15364
  6.5 73.3 %all-gather.3.cloned.1.call-start = ((), (), s32[]{:S(2)}) async-start(), calls=%async_computation.3 | async-start | bytes 9461760 | tf_op jit(solution)/shard_map/all_gather | solution.py:603
  39.2 17.2 %all-to-all-start = ((bf16[8,2,3,32,128]{4,3,2,1,0:T(8,128)(2,1)}), bf16[8,2,3,32,128]{4,3,2,1,0:T(8,128)(2,1)S(1)}, u32[]{:S(2)}, u32[]{:S(2)}) async-start(bf16[8,2,3,32,128]{4,3,2,1,0:T(8,128)(2,1)} %get-tuple-element.13), calls=%async_computation | async-start | bytes 786432 | tf_op jit(solution)/shard_map/all_to_all | solution.py:683
  56.4 0.7 copy-start
Sparse Core Ops, SparseCore 0:
  9.0 70.8 all-gather.2

commit v8 on v7

--- a/solution.py
+++ b/solution.py
@@ -22,6 +22,7 @@
 SPANS = CH // 8
 OUT_ROWS = 27 * 16
 BACK = 6
+EARLY = 3
 BACK_ROWS = 3 * 80
 NT = 8
 NZ = 4
@@ -233,41 +234,37 @@
     return -LOSS_SCALE * ((own - mean) * lax.rsqrt(second + SMOOTH)) / SCORED
 
 
-def restore_kernel(parts, pick_ref, here_ref, everyone_ref, x_ref, slope_ref, band, grad_ref, out_ref, back, shifted, coming):
-    t = pl.program_id(0)
-    frames = pl.num_programs(0)
-    row_count = x_ref.shape[1]
+def shift_frames(pick_ref, grad_ref, shifted, row_count, begin, end, scales):
     starts = range(0, row_count, BACK)
     rows = grad_ref.shape[3]
-
-    @pl.when(t == 0)
-    def _():
-        shifted[...] = jnp.zeros(shifted.shape, BF16)
-        lane = lane_iota(rows)
-        blank = jnp.zeros((8, 128), F32)
-        scales = cotangents(parts, here_ref[0], everyone_ref[...])
-
-        def one_frame(frame, carry):
-            for s in range(2):
-                entry = entry_of(pick_ref, s, frame)
-                scale = jnp.where(entry >= 0, scales[:, s : s + 1], 0.0)
-                source = jnp.maximum(entry, 0)
-                moved = [[], [], []]
-                for o in range(3):
-                    value = grad_ref[source, s, o].astype(F32) * scale
-                    value = jnp.where(lane < COLS, value, 0.0)
-                    for e, turned in enumerate((pltpu.roll(value, 127, 1), value, pltpu.roll(value, 1, 1))):
-                        moved[e].append(turned)
-                for k, start in enumerate(starts):
-                    block = [turned[start : start + 8] for some in moved for turned in some]
-                    shifted[frame, k, :, 128 * s : 128 * s + 128] = jnp.concatenate(
-                        block + [blank], axis=0
-                    ).astype(BF16)
-            return carry
-
-        lax.fori_loop(0, frames, one_frame, 0)
-
-    for k, start in enumerate(starts):
+    shifted[...] = jnp.zeros(shifted.shape, BF16)
+    lane = lane_iota(rows)
+    blank = jnp.zeros((8, 128), F32)
+
+    def one_frame(frame, carry):
+        for s in range(2):
+            entry = entry_of(pick_ref, s, frame)
+            scale = jnp.where(entry >= 0, scales[s], 0.0)
+            source = jnp.maximum(entry, 0)
+            moved = [[], [], []]
+            for o in range(3):
+                value = grad_ref[source, s, o].astype(F32) * scale
+                value = jnp.where(lane < COLS, value, 0.0)
+                for e, turned in enumerate((pltpu.roll(value, 127, 1), value, pltpu.roll(value, 1, 1))):
+                    moved[e].append(turned)
+            for k, start in enumerate(starts):
+                block = [turned[start : start + 8] for some in moved for turned in some]
+                shifted[frame, k, :, 128 * s : 128 * s + 128] = jnp.concatenate(
+                    block + [blank], axis=0
+                ).astype(BF16)
+        return carry
+
+    lax.fori_loop(begin, end, one_frame, 0)
+
+
+def restore_frame(t, x_ref, slope_ref, band, out_ref, back, shifted, coming):
+    row_count = x_ref.shape[1]
+    for k, start in enumerate(range(0, row_count, BACK)):
         count = min(BACK, row_count - start)
         operand = jnp.concatenate([shifted[t + 2 - a, k] for a in range(3)], axis=0)
         coming[k, 0 : count * CH, :] = nn_dot(band[0 : count * CH, :], operand)
@@ -293,6 +290,40 @@
             out_ref[0, row] = back[row % back.shape[0]].astype(BF16)
 
 
+def early_kernel(pick_ref, x_ref, slope_ref, band, grad_ref, out_ref, back, shifted, coming):
+    t = pl.program_id(0)
+
+    @pl.when(t == 0)
+    def _():
+        one = jnp.ones((1, 1), F32)
+        shift_frames(pick_ref, grad_ref, shifted, x_ref.shape[1], 0, EARLY + 2, (one, one))
+
+    restore_frame(t, x_ref, slope_ref, band, out_ref, back, shifted, coming)
+
+
+def restore_kernel(parts, pick_ref, here_ref, everyone_ref, early_ref, x_ref, slope_ref, band, grad_ref, out_ref, back, shifted, coming, scaling):
+    t = pl.program_id(0)
+    row_count = x_ref.shape[1]
+
+    @pl.when(t == 0)
+    def _():
+        both = cotangents(parts, here_ref[0], everyone_ref[...])
+        scales = (both[:, 0:1], both[:, 1:2])
+        scaling[...] = jnp.where(sub_iota(8) % 2 == 0, scales[0], scales[1])
+        shift_frames(pick_ref, grad_ref, shifted, row_count, EARLY, pl.num_programs(0), scales)
+
+    @pl.when(t < EARLY)
+    def _():
+        for row in range(row_count):
+            value = early_ref[0, row].astype(F32)
+            value = value.reshape(value.shape[0] // 8, 8, 128) * scaling[...]
+            out_ref[0, row] = value.reshape(early_ref.shape[2:]).astype(BF16)
+
+    @pl.when(t >= EARLY)
+    def _():
+        restore_frame(t, x_ref, slope_ref, band, out_ref, back, shifted, coming)
+
+
 def nt_dot(one, two):
     return lax.dot_general(one, two, (((1,), (1,)), ((), ())), preferred_element_type=F32)
 
@@ -354,7 +385,7 @@
     row_count, tiles, samples,
     group_ref, inputs_ref, order, packed_ref, head_ref,
     out_ref, score_ref,
-    pack, arrived, frame, flip, embed, outw, place, patches, tokens, normed, normed16, slots, weights, dslots, dnormed, rows8, abar, both,
+    pack, arrived, frame, flip, embed, outw, place, patches, tokens, normed, normed16, slots, weights, dslots, dnormed, rows8, abar, both, dweights, dlogits,
 ):
     height = row_count * tiles
     patch_rows = height // PATCH
@@ -455,18 +486,19 @@
         for m in range(3):
             slots[3 * i + m] = jnp.where(lane_all < HD, found[m], 0.0).astype(BF16)
 
-    for h in range(HEADS):
-        for f in range(samples):
-            span = slice(f * NTOK, f * NTOK + NTOK)
-            logits = nt_dot(slots[h, span, :], slots[HEADS + h, span, :]) * HD ** (-0.5)
-            logits = jnp.exp(logits - jnp.max(logits, axis=-1, keepdims=True))
-            prob = logits / jnp.sum(logits, axis=-1, keepdims=True)
-            weights[h * samples + f] = prob
-            sums = jnp.sum(prob.astype(BF16).astype(F32), axis=0, keepdims=True)
-            sums = split_two(jnp.broadcast_to(sums, (8, 128)))
-            both[h * samples + f] = sums
-            mean = nn_dot(sums, slots[2 * HEADS + h, span, :]) * (1.0 / NTOK)
-            abar[f : f + 1, 128 * h : 128 * h + 128] = mean[0:1] + mean[8:9]
+    pairs = [(h, f, h * samples + f, slice(f * NTOK, f * NTOK + NTOK)) for h in range(HEADS) for f in range(samples)]
+    for h, f, at, span in pairs:
+        weights[at] = nt_dot(slots[h, span, :], slots[HEADS + h, span, :]) * HD ** (-0.5)
+    logits = weights[...]
+    logits = jnp.exp(logits - jnp.max(logits, axis=-1, keepdims=True))
+    prob = logits / jnp.sum(logits, axis=-1, keepdims=True)
+    weights[...] = prob
+    sums = jnp.sum(prob.astype(BF16).astype(F32), axis=1, keepdims=True)
+    for h, f, at, span in pairs:
+        two = split_two(jnp.broadcast_to(sums[at], (8, 128)))
+        both[at] = two
+        mean = nn_dot(two, slots[2 * HEADS + h, span, :]) * (1.0 / NTOK)
+        abar[f : f + 1, 128 * h : 128 * h + 128] = mean[0:1] + mean[8:9]
 
     part = nn_dot(split_two(abar[...]), outw[...])
     pooled = rows8[0] + part[0:8] + part[8:16]
@@ -490,19 +522,19 @@
     datts = (datts[0:8] + datts[8:16]).astype(BF16)
 
     first_rows = sub_iota(16) % 8 == 0
-    for h in range(HEADS):
+    for h, f, at, span in pairs:
         datt = datts[:, 128 * h : 128 * h + 128]
-        for f in range(samples):
-            span = slice(f * NTOK, f * NTOK + NTOK)
-            prob = weights[h * samples + f]
-            row = datt[f : f + 1, :]
-            dweight = nt_dot(datt, slots[2 * HEADS + h, span, :])[f : f + 1, :].astype(BF16).astype(F32)
-            inner = jnp.sum(prob * dweight, axis=-1, keepdims=True)
-            dlogit = (prob * (dweight - inner) * HD ** (-0.5)).astype(BF16)
-            dslots[h, span, :] = nn_dot(dlogit, slots[HEADS + h, span, :])
-            dslots[HEADS + h, span, :] = tn_dot(dlogit, slots[h, span, :])
-            pair = jnp.where(first_rows, jnp.broadcast_to(row.astype(F32), (16, 128)), 0.0).astype(BF16)
-            dslots[2 * HEADS + h, span, :] = tn_dot(both[h * samples + f], pair)
+        pair = jnp.where(first_rows, jnp.broadcast_to(datt[f : f + 1].astype(F32), (16, 128)), 0.0).astype(BF16)
+        dslots[2 * HEADS + h, span, :] = tn_dot(both[at], pair)
+        dweight = nt_dot(datt, slots[2 * HEADS + h, span, :])[f : f + 1, :].astype(BF16).astype(F32)
+        dweights[at] = jnp.broadcast_to(dweight, (8, 128))
+    prob = weights[...]
+    dweight = dweights[:, 0:1, :]
+    inner = jnp.sum(prob * dweight, axis=-1, keepdims=True)
+    dlogits[...] = (prob * (dweight - inner) * HD ** (-0.5)).astype(BF16)
+    for h, f, at, span in pairs:
+        dslots[h, span, :] = nn_dot(dlogits[at], slots[HEADS + h, span, :])
+        dslots[HEADS + h, span, :] = tn_dot(dlogits[at], slots[h, span, :])
 
     parts = []
     for i in range(NT):
@@ -727,16 +759,35 @@
             pltpu.VMEM((2, 8, D), F32),
             pltpu.VMEM((8, HEADS * 128), F32),
             pltpu.VMEM((HEADS * samples, 16, 128), BF16),
+            pltpu.VMEM((HEADS * samples, 8, 128), F32),
+            pltpu.VMEM((HEADS * samples, NTOK, NTOK), BF16),
         ],
         compiler_params=params(),
         name="reward",
     )(group_index, inputs, input_order, packed, head)
 
+    returned = lax.all_to_all(grads, TILE, split_axis=0, concat_axis=0, tiled=True)
+    scores, returned = lax.optimization_barrier((scores, returned))
     everyone = lax.all_to_all(scores, TILE + ("sample",), split_axis=0, concat_axis=0, tiled=True)
-    returned = lax.all_to_all(grads, TILE, split_axis=0, concat_axis=0, tiled=True)
     returned = returned[:SCORED]
-
     here = lax.axis_index("sample").astype(jnp.int32).reshape(1)
+
+    restore_scratch = [
+        pltpu.VMEM((row_block, samples * merged // 128, 128), F32),
+        pltpu.VMEM((frames + 2, -(-row_count // BACK), 80, 256), BF16),
+        pltpu.VMEM((-(-row_count // BACK), BACK * CH, 256), F32),
+    ]
+    early = pl.pallas_call(
+        early_kernel,
+        grid=(EARLY,),
+        in_specs=[smem, aligned_spec, aligned_spec, band_spec, sent_spec],
+        out_specs=view_spec,
+        scratch_shapes=restore_scratch,
+        out_shape=jax.ShapeDtypeStruct((EARLY,) + view.shape[1:], BF16),
+        compiler_params=params(),
+        name="early",
+    )(frame_pick, x_aligned, slopes, band, returned)
+    late_spec = pl.BlockSpec((1,) + aligned[1:], lambda t: (jnp.maximum(t, EARLY), 0, 0, 0, 0))
     result = pl.pallas_call(
         functools.partial(restore_kernel, parts),
         grid=(frames,),
@@ -744,21 +795,18 @@
             smem,
             smem,
             pl.BlockSpec((tiles * parts, 128), lambda t: (0, 0)),
-            aligned_spec,
-            aligned_spec,
+            pl.BlockSpec((1,) + view.shape[1:], lambda t: (jnp.minimum(t, EARLY - 1), 0, 0, 0)),
+            late_spec,
+            late_spec,
             band_spec,
             sent_spec,
         ],
         out_specs=view_spec,
-        scratch_shapes=[
-            pltpu.VMEM((row_block, samples * merged // 128, 128), F32),
-            pltpu.VMEM((frames + 2, -(-row_count // BACK), 80, 256), BF16),
-            pltpu.VMEM((-(-row_count // BACK), BACK * CH, 256), F32),
-        ],
+        scratch_shapes=restore_scratch + [pltpu.VMEM((8, 128), F32)],
         out_shape=jax.ShapeDtypeStruct(view.shape, BF16),
         compiler_params=params(),
         name="restore",
-    )(frame_pick, here, everyone, x_aligned, slopes, band, returned)
+    )(frame_pick, here, everyone, early, x_aligned, slopes, band, returned)
     result = result.reshape(frames, row_count, merged // 128, samples, 128).transpose(3, 0, 1, 2, 4)
     return with_layout_constraint(result, order).reshape(features.shape)
 

time: 154 us -> 145 us (0.942)
  blocking collectives: 23 us -> 12.4 us
  starting transfers between devices: 5.17 us -> 7.95 us
  Pallas kernels: 79.5 us -> 77.7 us
    all_to_all x1 -> x0, blocking collectives: 10.6 us -> none  [local(): lax.all_to_all(scores, TILE + ('sample',), split_axis=0, concat_axis=0, t...]
    pallas_call x0 -> x1, Pallas kernels: none -> 8.84 us  [local(): pl.pallas_call(early_kernel, grid=(EARLY,), in_specs=[smem, aligned_spec,...]
    pallas_call x1, Pallas kernels: 22.4 us -> 14.4 us  [local(): pl.pallas_call(functools.partial(reward_kernel, row_count, tiles, samples...]
    all_to_all x0 -> x1, starting transfers between devices: none -> 2.77 us  [local(): lax.all_to_all(scores, TILE + ('sample',), split_axis=0, concat_axis=0, t...]
    pallas_call x1, Pallas kernels: 21.3 us -> 18.6 us  [local(): pl.pallas_call(functools.partial(restore_kernel, parts), grid=(frames,),...]
  transfers between devices with their start and end apart: 2 -> 3, of which waited for: 2 -> 2; matrix products, arithmetic and copies ran while one was open for 1% -> 1% of each run, Pallas kernels for 22% -> 30%
where the time goes in v8:
time: 145 us; the launch traced here: 144 us
  Pallas kernels  77.7 us (54%)
  waiting for transfers between devices  30.9 us (21%)
  between operations  13.4 us (9%)
  blocking collectives  12.4 us (9%)
  starting transfers between devices  7.95 us (5%)
  local copies, waits for them, and re-layouts  2.12 us (1%)
    pallas_call x1, Pallas kernels, local(): pl.pallas_call(functools.partial(decode_kernel, row_block), grid=(frames,...  30.8 us
    all_gather x1, waiting for transfers between devices, packed_weights(): lax.all_gather(mine, TILE + ('sample',), axis=0, axis_index_groups=[group])  19.6 us
    pallas_call x1, Pallas kernels, local(): pl.pallas_call(functools.partial(restore_kernel, parts), grid=(frames,),...  18.6 us
    pallas_call x1, Pallas kernels, local(): pl.pallas_call(functools.partial(reward_kernel, row_count, tiles, samples...  14.4 us
    all_to_all x1, blocking collectives, local(): lax.all_to_all(grads, TILE, split_axis=0, concat_axis=0, tiled=True)  12.4 us
    all_to_all x1, waiting for transfers between devices, local(): lax.all_to_all(decoded, TILE, split_axis=0, concat_axis=0, tiled=True)  11.2 us
    pallas_call x1, Pallas kernels, local(): pl.pallas_call(early_kernel, grid=(EARLY,), in_specs=[smem, aligned_spec,...  8.84 us
    all_to_all x1, starting transfers between devices, local(): lax.all_to_all(decoded, TILE, split_axis=0, concat_axis=0, tiled=True)  5.17 us
  transfers between devices with their start and end apart: 3, of which 2 were waited for; matrix products, arithmetic and copies ran while one was open for 1% of the time, Pallas kernels for 30%

profile of v8, /device:TPU:0, one launch (start us, length us, event | category | flops | bytes accessed | tf_op | source)
XLA Modules:
  0.0 144.5 jit_solution(2176927069046746961)
XLA Ops:
  6.5 0.0 copy-start.2
  6.5 0.0 all-gather.3.cloned.1.call-start
  6.5 1.9 %pack.1 = bf16[1120,128]{1,0:T(8,128)(2,1)} custom-call(s32[1]{0:T(128)} %bitcast.z_ref.here_ref, bf16[320,240]{1,0:T(8,128)(2,1)} %rows_ref.1, bf16[160,160]{1,0:T(8,128)(2,1)} %out_ref.1, bf16[32,160]{1,0:T(8,128)(2,1)} %place_ref.1, bf16[160,588]{1,0:T(8,128)(2,1)} %bitcast.22), custom_call_target="tpu_custom_call" | custom-call | tf_op jit(solution)/shard_map/pack/pallas_call | solution.py:627
  8.4 0.0 all-gather.3.cloned.1.call-update
  8.4 30.8 %decode.1 = (bf16[8,2,3,32,128]{4,3,2,1,0:T(8,128)(2,1)}, bf16[9,28,2,96,128]{4,3,2,1,0:T(8,128)(2,1)}, bf16[9,28,2,96,128]{4,3,2,1,0:T(8,128)(2,1)}, bf16[576,240]{1,0:T(8,128)(2,1)}) custom-call(s32[2,8]{1,0:T(2,128)} %pick_ref.5, bf16[9,28,168,128]{3,2,1,0:T(8,128)(2,1)} %bitcast.20, f32[1,96]{1,0:T(1,128)} %bitcast.25, bf16[3,3,3,3,96]{4,3,2,1,0:T(4,128)(2,1)} %weight_ref.1), custom_call_target="tpu_custom_call" | custom-call | tf_op jit(solution)/shard_map/decode/pallas_call | solution.py:689
  39.2 5.2 %all-to-all-start = ((bf16[8,2,3,32,128]{4,3,2,1,0:T(8,128)(2,1)}), bf16[8,2,3,32,128]{4,3,2,1,0:T(8,128)(2,1)S(1)}, u32[]{:S(2)}, u32[]{:S(2)}) async-start(bf16[8,2,3,32,128]{4,3,2,1,0:T(8,128)(2,1)} %get-tuple-element.15), calls=%async_computation | async-start | bytes 786432 | tf_op jit(solution)/shard_map/all_to_all | solution.py:715
  44.4 0.0 copy-done.2
  44.4 0.1 reshape.30
  44.5 0.1 reshape.32
  44.6 0.6 broadcast_in_dim.7.head_ref
  45.2 11.2 %all-to-all-done.part_ref = bf16[8,2,3,32,128]{4,3,2,1,0:T(8,128)(2,1)S(1)} async-done(((bf16[8,2,3,32,128]{4,3,2,1,0:T(8,128)(2,1)}), bf16[8,2,3,32,128]{4,3,2,1,0:T(8,128)(2,1)S(1)}, u32[]{:S(2)}, u32[]{:S(2)}) %all-to-all-start) | async-done | bytes 393248 | tf_op jit(solution)/shard_map/all_to_all | solution.py:715
  56.4 0.0 copy-start
  56.4 0.8 copy-done
  57.1 3.1 %patches.1 = (bf16[256,640]{1,0:T(8,128)(2,1)}, bf16[896,640]{1,0:T(8,128)(2,1)}) custom-call(bf16[8,2,3,32,128]{4,3,2,1,0:T(8,128)(2,1)} %copy-done), custom_call_target="tpu_custom_call" | custom-call | tf_op jit(solution)/shard_map/patches/pallas_call | solution.py:723
  60.3 19.6 %all-gather.3.cloned.1.call-done = bf16[35840,128]{1,0:T(8,128)(2,1)} async-done(((bf16[1120,128]{1,0:T(8,128)(2,1)}), bf16[35840,128]{1,0:T(8,128)(2,1)}) %all-gather.3.cloned.1.call-update) | async-done | bytes 9175056 | tf_op jit(solution)/shard_map/all_gather | solution.py:635
  79.9 14.4 %reward.1 = (bf16[8,2,3,32,128]{4,3,2,1,0:T(8,128)(2,1)}, f32[32,128]{1,0:T(8,128)}) custom-call(s32[2]{0:T(128)} %group_ref.1, bf16[256,640]{1,0:T(8,128)(2,1)} %get-tuple-element.16.inputs_ref, bf16[896,640]{1,0:T(8,128)(2,1)} %get-tuple-element.17.order, bf16[32,1120,128]{2,1,0:T(8,128)(2,1)} %bitcast.21, f32[1,1280]{1,0:T(1,128)} %broadcast_in_dim.7.head_ref), custom_call_target="tpu_custom_call" | custom-call | tf_op jit(solution)/shard_map/reward/pallas_call | solution.py:730
  94.4 12.4 %all_to_all.21.grad_ref = bf16[8,2,3,32,128]{4,3,2,1,0:T(8,128)(2,1)} all-to-all(bf16[8,2,3,32,128]{4,3,2,1,0:T(8,128)(2,1)} %get-tuple-element.19), channel_id=1, replica_groups=mesh['chip'=4,'core'=2,'sample'=4] {'chip','core'}, dimensions={0} | all-to-all | bytes 786432 | tf_op jit(solution)/shard_map/all_to_all | solution.py:769
  106.8 2.8 %all-to-all-start.2 = ((f32[32,1,128]{2,1,0:T(1,128)}), f32[32,1,128]{2,1,0:T(1,128)S(1)}, u32[]{:S(2)}, u32[]{:S(2)}) async-start(f32[32,1,128]{2,1,0:T(1,128)} %bitcast.24), calls=%async_computation.2 | async-start | bytes 32768 | tf_op jit(solution)/shard_map/all_to_all | solution.py:771
  109.6 8.8 %early.1.early_ref = bf16[3,28,168,128]{3,2,1,0:T(8,128)(2,1)} custom-call(s32[2,8]{1,0:T(2,128)} %pick_ref.5, bf16[9,28,2,96,128]{4,3,2,1,0:T(8,128)(2,1)} %get-tuple-element.21.x_ref, bf16[9,28,2,96,128]{4,3,2,1,0:T(8,128)(2,1)} %get-tuple-element.22.slope_ref, bf16[576,240]{1,0:T(8,128)(2,1)} %get-tuple-element.23.band, ...), custom_call_target="tpu_custom_call" | custom-call | tf_op jit(solution)/shard_map/early/pallas_call | solution.py:780
  118.4 0.0 all-to-all-done.2
  118.4 0.0 copy-start.1
  118.4 0.6 copy-done.1
  119.0 18.6 %restore.1 = bf16[9,28,168,128]{3,2,1,0:T(8,128)(2,1)} custom-call(s32[2,8]{1,0:T(2,128)} %pick_ref.5, s32[1]{0:T(128)} %bitcast.z_ref.here_ref, f32[32,128]{1,0:T(8,128)} %bitcast.23, bf16[3,28,168,128]{3,2,1,0:T(8,128)(2,1)} %early.1.early_ref, bf16[9,28,2,96,128]{4,3,2,1,0:T(8,128)(2,1)} %get-tuple-element.21.x_ref, ...), custom_call_target="tpu_custom_call" | custom-call | tf_op jit(solution)/shard_map/restore/pallas_call | solution.py:791
  (3 shorter events, 0.0 us)
Async XLA Ops:
  6.5 37.9 %copy-start.2 = (f32[1280]{0:T(1024)S(1)}, f32[1280]{0:T(1024)}, u32[]{:S(2)}) copy-start(f32[1280]{0:T(1024)} %param.17) | copy-start | bytes 15364
  6.5 73.4 %all-gather.3.cloned.1.call-start = ((), (), s32[]{:S(2)}) async-start(), calls=%async_computation.3 | async-start | bytes 9461760 | tf_op jit(solution)/shard_map/all_gather | solution.py:635
  39.2 17.2 %all-to-all-start = ((bf16[8,2,3,32,128]{4,3,2,1,0:T(8,128)(2,1)}), bf16[8,2,3,32,128]{4,3,2,1,0:T(8,128)(2,1)S(1)}, u32[]{:S(2)}, u32[]{:S(2)}) async-start(bf16[8,2,3,32,128]{4,3,2,1,0:T(8,128)(2,1)} %get-tuple-element.15), calls=%async_computation | async-start | bytes 786432 | tf_op jit(solution)/shard_map/all_to_all | solution.py:715
  56.4 0.8 copy-start
  106.8 11.6 %all-to-all-start.2 = ((f32[32,1,128]{2,1,0:T(1,128)}), f32[32,1,128]{2,1,0:T(1,128)S(1)}, u32[]{:S(2)}, u32[]{:S(2)}) async-start(f32[32,1,128]{2,1,0:T(1,128)} %bitcast.24), calls=%async_computation.2 | async-start | bytes 32768 | tf_op jit(solution)/shard_map/all_to_all | solution.py:771
  118.4 0.6 copy-start.1
Sparse Core Ops, SparseCore 0:
  9.0 70.8 all-gather.2

commit v9 on v8

--- a/solution.py
+++ b/solution.py
@@ -234,7 +234,7 @@
     return -LOSS_SCALE * ((own - mean) * lax.rsqrt(second + SMOOTH)) / SCORED
 
 
-def shift_frames(pick_ref, grad_ref, shifted, row_count, begin, end, scales):
+def shift_frames(entry_ref, grad_ref, shifted, row_count, begin, end, scales):
     starts = range(0, row_count, BACK)
     rows = grad_ref.shape[3]
     shifted[...] = jnp.zeros(shifted.shape, BF16)
@@ -243,7 +243,7 @@
 
     def one_frame(frame, carry):
         for s in range(2):
-            entry = entry_of(pick_ref, s, frame)
+            entry = entry_ref[s, frame]
             scale = jnp.where(entry >= 0, scales[s], 0.0)
             source = jnp.maximum(entry, 0)
             moved = [[], [], []]
@@ -262,46 +262,54 @@
     lax.fori_loop(begin, end, one_frame, 0)
 
 
-def restore_frame(t, x_ref, slope_ref, band, out_ref, back, shifted, coming):
+def restore_frame(t, x_ref, slope_ref, band, out_ref, back, shifted, coming, factors):
     row_count = x_ref.shape[1]
     for k, start in enumerate(range(0, row_count, BACK)):
         count = min(BACK, row_count - start)
         operand = jnp.concatenate([shifted[t + 2 - a, k] for a in range(3)], axis=0)
         coming[k, 0 : count * CH, :] = nn_dot(band[0 : count * CH, :], operand)
+        places = [(local, s) for local in range(count) for s in range(2)]
+        for local, s in places:
+            totals = []
+            for m in range(SPANS // 2):
+                pair = x_ref[0, start + local, s, 16 * m : 16 * m + 16, :].astype(F32)
+                slopes = slope_ref[0, start + local, s, 16 * m : 16 * m + 16, :].astype(F32)
+                at = local * CH + 16 * m
+                out = coming[k, at : at + 16, 128 * s : 128 * s + 128] * slopes
+                coming[k, at : at + 16, 128 * s : 128 * s + 128] = out
+                out = out * pair
+                totals.append(out[0:8] + out[8:16])
+            while len(totals) > 1:
+                totals = [sum(totals[i + 1 : i + 2], totals[i]) for i in range(0, len(totals), 2)]
+            factors[k, local * 2 + s] = totals[0]
+        found = jnp.sum(factors[k], axis=1, keepdims=True) * (1.0 / CH)
+        for local, s in places:
+            row = start + local
+            for m in range(SPANS // 2):
+                pair = x_ref[0, row, s, 16 * m : 16 * m + 16, :].astype(F32)
+                at = local * CH + 16 * m
+                result = coming[k, at : at + 16, 128 * s : 128 * s + 128] - pair * found[local * 2 + s]
+                for part in range(2):
+                    g = 2 * m + part
+                    moved = tiles_of(result[8 * part : 8 * part + 8])
+                    back[row % back.shape[0], pl.ds(14 * g + s, 7, stride=2), :] = moved[0:7]
         for local in range(count):
             row = start + local
-            for s in range(2):
-                outs, units, total = [], [], None
-                for m in range(SPANS // 2):
-                    pair = x_ref[0, row, s, 16 * m : 16 * m + 16, :].astype(F32)
-                    slopes = slope_ref[0, row, s, 16 * m : 16 * m + 16, :].astype(F32)
-                    for part in range(2):
-                        g = 2 * m + part
-                        unit = pair[8 * part : 8 * part + 8]
-                        at = local * CH + 8 * g
-                        out = coming[k, at : at + 8, 128 * s : 128 * s + 128] * slopes[8 * part : 8 * part + 8]
-                        outs.append(out)
-                        units.append(unit)
-                        total = out * unit if g == 0 else total + out * unit
-                factor = jnp.sum(total, axis=0, keepdims=True) * (1.0 / CH)
-                for g in range(SPANS):
-                    result = tiles_of(outs[g] - units[g] * factor)
-                    back[row % back.shape[0], pl.ds(14 * g + s, 7, stride=2), :] = result[0:7]
             out_ref[0, row] = back[row % back.shape[0]].astype(BF16)
 
 
-def early_kernel(pick_ref, x_ref, slope_ref, band, grad_ref, out_ref, back, shifted, coming):
+def early_kernel(entry_ref, x_ref, slope_ref, band, grad_ref, out_ref, back, shifted, coming, factors):
     t = pl.program_id(0)
 
     @pl.when(t == 0)
     def _():
         one = jnp.ones((1, 1), F32)
-        shift_frames(pick_ref, grad_ref, shifted, x_ref.shape[1], 0, EARLY + 2, (one, one))
-
-    restore_frame(t, x_ref, slope_ref, band, out_ref, back, shifted, coming)
-
-
-def restore_kernel(parts, pick_ref, here_ref, everyone_ref, early_ref, x_ref, slope_ref, band, grad_ref, out_ref, back, shifted, coming, scaling):
+        shift_frames(entry_ref, grad_ref, shifted, x_ref.shape[1], 0, EARLY + 2, (one, one))
+
+    restore_frame(t, x_ref, slope_ref, band, out_ref, back, shifted, coming, factors)
+
+
+def restore_kernel(parts, entry_ref, here_ref, everyone_ref, early_ref, x_ref, slope_ref, band, grad_ref, out_ref, back, shifted, coming, factors, scaling):
     t = pl.program_id(0)
     row_count = x_ref.shape[1]
 
@@ -310,7 +318,7 @@
         both = cotangents(parts, here_ref[0], everyone_ref[...])
         scales = (both[:, 0:1], both[:, 1:2])
         scaling[...] = jnp.where(sub_iota(8) % 2 == 0, scales[0], scales[1])
-        shift_frames(pick_ref, grad_ref, shifted, row_count, EARLY, pl.num_programs(0), scales)
+        shift_frames(entry_ref, grad_ref, shifted, row_count, EARLY, pl.num_programs(0), scales)
 
     @pl.when(t < EARLY)
     def _():
@@ -321,7 +329,7 @@
 
     @pl.when(t >= EARLY)
     def _():
-        restore_frame(t, x_ref, slope_ref, band, out_ref, back, shifted, coming)
+        restore_frame(t, x_ref, slope_ref, band, out_ref, back, shifted, coming, factors)
 
 
 def nt_dot(one, two):
@@ -767,6 +775,9 @@
     )(group_index, inputs, input_order, packed, head)
 
     returned = lax.all_to_all(grads, TILE, split_axis=0, concat_axis=0, tiled=True)
+    picks, scores = lax.optimization_barrier((frame_pick, scores))
+    is_entry = picks[:, None, :] == jnp.arange(frames, dtype=jnp.int32)[None, :, None]
+    entry = jnp.max(jnp.where(is_entry, jnp.arange(SCORED, dtype=jnp.int32)[None, None, :], -1), axis=2)
     scores, returned = lax.optimization_barrier((scores, returned))
     everyone = lax.all_to_all(scores, TILE + ("sample",), split_axis=0, concat_axis=0, tiled=True)
     returned = returned[:SCORED]
@@ -776,6 +787,7 @@
         pltpu.VMEM((row_block, samples * merged // 128, 128), F32),
         pltpu.VMEM((frames + 2, -(-row_count // BACK), 80, 256), BF16),
         pltpu.VMEM((-(-row_count // BACK), BACK * CH, 256), F32),
+        pltpu.VMEM((-(-row_count // BACK), BACK * 2, 8, 128), F32),
     ]
     early = pl.pallas_call(
         early_kernel,
@@ -786,7 +798,7 @@
         out_shape=jax.ShapeDtypeStruct((EARLY,) + view.shape[1:], BF16),
         compiler_params=params(),
         name="early",
-    )(frame_pick, x_aligned, slopes, band, returned)
+    )(entry, x_aligned, slopes, band, returned)
     late_spec = pl.BlockSpec((1,) + aligned[1:], lambda t: (jnp.maximum(t, EARLY), 0, 0, 0, 0))
     result = pl.pallas_call(
         functools.partial(restore_kernel, parts),
@@ -806,7 +818,7 @@
         out_shape=jax.ShapeDtypeStruct(view.shape, BF16),
         compiler_params=params(),
         name="restore",
-    )(frame_pick, here, everyone, early, x_aligned, slopes, band, returned)
+    )(entry, here, everyone, early, x_aligned, slopes, band, returned)
     result = result.reshape(frames, row_count, merged // 128, samples, 128).transpose(3, 0, 1, 2, 4)
     return with_layout_constraint(result, order).reshape(features.shape)
 

time: 145 us -> 145 us (level)
  blocking collectives: 12.4 us -> 0 us
  waiting for transfers between devices: 30.9 us -> 39.4 us
  starting transfers between devices: 7.95 us -> 11.4 us
    all_to_all x1 -> x0, blocking collectives: 12.4 us -> none  [local(): lax.all_to_all(grads, TILE, split_axis=0, concat_axis=0, tiled=True)]
    all_to_all x0 -> x1, waiting for transfers between devices: none -> 8.27 us  [local(): lax.all_to_all(grads, TILE, split_axis=0, concat_axis=0, tiled=True)]
    all_to_all x0 -> x1, starting transfers between devices: none -> 3.46 us  [local(): lax.all_to_all(grads, TILE, split_axis=0, concat_axis=0, tiled=True)]
  transfers between devices with their start and end apart: 3 -> 4, of which waited for: 2 -> 3; matrix products, arithmetic and copies ran while one was open for 1% -> 1% of each run, Pallas kernels for 30% -> 30%
where the time goes in v9:
time: 145 us
  Pallas kernels  77.7 us (54%)
  waiting for transfers between devices  39.4 us (27%)
  between operations  13.5 us (9%)
  starting transfers between devices  11.4 us (8%)
  local copies, waits for them, and re-layouts  2.13 us (1%)
    pallas_call x1, Pallas kernels, local(): pl.pallas_call(functools.partial(decode_kernel, row_block), grid=(frames,...  30.8 us
    all_gather x1, waiting for transfers between devices, packed_weights(): lax.all_gather(mine, TILE + ('sample',), axis=0, axis_index_groups=[group])  19.8 us
    pallas_call x1, Pallas kernels, local(): pl.pallas_call(functools.partial(restore_kernel, parts), grid=(frames,),...  18.6 us
    pallas_call x1, Pallas kernels, local(): pl.pallas_call(functools.partial(reward_kernel, row_count, tiles, samples...  14.4 us
    all_to_all x1, waiting for transfers between devices, local(): lax.all_to_all(decoded, TILE, split_axis=0, concat_axis=0, tiled=True)  11.3 us
    pallas_call x1, Pallas kernels, local(): pl.pallas_call(early_kernel, grid=(EARLY,), in_specs=[smem, aligned_spec,...  8.87 us
    all_to_all x1, waiting for transfers between devices, local(): lax.all_to_all(grads, TILE, split_axis=0, concat_axis=0, tiled=True)  8.27 us
    all_to_all x1, starting transfers between devices, local(): lax.all_to_all(decoded, TILE, split_axis=0, concat_axis=0, tiled=True)  5.17 us
  transfers between devices with their start and end apart: 4, of which 3 were waited for; matrix products, arithmetic and copies ran while one was open for 1% of the time, Pallas kernels for 30%

profile of v9, /device:TPU:0, one launch (start us, length us, event | category | flops | bytes accessed | tf_op | source)
XLA Modules:
  0.0 144.8 jit_solution(15635548644867658978)
XLA Ops:
  6.5 0.0 copy-start.3
  6.5 0.0 all-gather.3.cloned.1.call-start
  6.5 1.9 %pack.1 = bf16[1120,128]{1,0:T(8,128)(2,1)} custom-call(s32[1]{0:T(128)} %bitcast.4.z_ref.here_ref, bf16[320,240]{1,0:T(8,128)(2,1)} %rows_ref.1, bf16[160,160]{1,0:T(8,128)(2,1)} %out_ref.1, bf16[32,160]{1,0:T(8,128)(2,1)} %place_ref.1, bf16[160,588]{1,0:T(8,128)(2,1)} %bitcast.22), custom_call_target="tpu_custom_call" | custom-call | tf_op jit(solution)/shard_map/pack/pallas_call | solution.py:635
  8.4 0.0 all-gather.3.cloned.1.call-update
  8.4 0.0 copy-start.4
  8.4 30.8 %decode.1 = (bf16[8,2,3,32,128]{4,3,2,1,0:T(8,128)(2,1)}, bf16[9,28,2,96,128]{4,3,2,1,0:T(8,128)(2,1)}, bf16[9,28,2,96,128]{4,3,2,1,0:T(8,128)(2,1)}, bf16[576,240]{1,0:T(8,128)(2,1)}) custom-call(s32[2,8]{1,0:T(2,128)} %pick_ref.1, bf16[9,28,168,128]{3,2,1,0:T(8,128)(2,1)} %bitcast.20, f32[1,96]{1,0:T(1,128)} %bitcast.25, bf16[3,3,3,3,96]{4,3,2,1,0:T(4,128)(2,1)} %weight_ref.1), custom_call_target="tpu_custom_call" | custom-call | tf_op jit(solution)/shard_map/decode/pallas_call | solution.py:697
  39.2 5.2 %all-to-all-start = ((bf16[8,2,3,32,128]{4,3,2,1,0:T(8,128)(2,1)}), bf16[8,2,3,32,128]{4,3,2,1,0:T(8,128)(2,1)S(1)}, u32[]{:S(2)}, u32[]{:S(2)}) async-start(bf16[8,2,3,32,128]{4,3,2,1,0:T(8,128)(2,1)} %get-tuple-element.17), calls=%async_computation | async-start | bytes 786432 | tf_op jit(solution)/shard_map/all_to_all | solution.py:723
  44.4 0.0 copy-done.3
  44.4 0.1 reshape.31
  44.5 0.1 reshape.33
  44.6 0.6 broadcast_in_dim.22.head_ref
  45.2 11.3 %all-to-all-done.part_ref = bf16[8,2,3,32,128]{4,3,2,1,0:T(8,128)(2,1)S(1)} async-done(((bf16[8,2,3,32,128]{4,3,2,1,0:T(8,128)(2,1)}), bf16[8,2,3,32,128]{4,3,2,1,0:T(8,128)(2,1)S(1)}, u32[]{:S(2)}, u32[]{:S(2)}) %all-to-all-start) | async-done | bytes 393248 | tf_op jit(solution)/shard_map/all_to_all | solution.py:723
  56.5 0.0 copy-start.1
  56.5 0.8 copy-done.1
  57.2 3.1 %patches.1 = (bf16[256,640]{1,0:T(8,128)(2,1)}, bf16[896,640]{1,0:T(8,128)(2,1)}) custom-call(bf16[8,2,3,32,128]{4,3,2,1,0:T(8,128)(2,1)} %copy-done.1), custom_call_target="tpu_custom_call" | custom-call | tf_op jit(solution)/shard_map/patches/pallas_call | solution.py:731
  60.4 19.8 %all-gather.3.cloned.1.call-done = bf16[35840,128]{1,0:T(8,128)(2,1)} async-done(((bf16[1120,128]{1,0:T(8,128)(2,1)}), bf16[35840,128]{1,0:T(8,128)(2,1)}) %all-gather.3.cloned.1.call-update) | async-done | bytes 9175056 | tf_op jit(solution)/shard_map/all_gather | solution.py:643
  80.2 14.4 %reward.1 = (bf16[8,2,3,32,128]{4,3,2,1,0:T(8,128)(2,1)}, f32[32,128]{1,0:T(8,128)}) custom-call(s32[2]{0:T(128)} %group_ref.1, bf16[256,640]{1,0:T(8,128)(2,1)} %get-tuple-element.18.inputs_ref, bf16[896,640]{1,0:T(8,128)(2,1)} %get-tuple-element.19.order, bf16[32,1120,128]{2,1,0:T(8,128)(2,1)} %bitcast.21, f32[1,1280]{1,0:T(1,128)} %broadcast_in_dim.22.head_ref), custom_call_target="tpu_custom_call" | custom-call | tf_op jit(solution)/shard_map/reward/pallas_call | solution.py:738
  94.7 3.5 %all-to-all-start.1 = ((bf16[8,2,3,32,128]{4,3,2,1,0:T(8,128)(2,1)}), bf16[8,2,3,32,128]{4,3,2,1,0:T(8,128)(2,1)S(1)}, u32[]{:S(2)}, u32[]{:S(2)}) async-start(bf16[8,2,3,32,128]{4,3,2,1,0:T(8,128)(2,1)} %get-tuple-element.23), calls=%async_computation.1 | async-start | bytes 786432 | tf_op jit(solution)/shard_map/all_to_all | solution.py:777
  98.1 8.3 %all-to-all-done.1.grad_ref = bf16[8,2,3,32,128]{4,3,2,1,0:T(8,128)(2,1)S(1)} async-done(((bf16[8,2,3,32,128]{4,3,2,1,0:T(8,128)(2,1)}), bf16[8,2,3,32,128]{4,3,2,1,0:T(8,128)(2,1)S(1)}, u32[]{:S(2)}, u32[]{:S(2)}) %all-to-all-start.1) | async-done | bytes 393248 | tf_op jit(solution)/shard_map/all_to_all | solution.py:777
  106.4 0.0 copy-start
  106.4 2.7 %all-to-all-start.2 = ((f32[32,1,128]{2,1,0:T(1,128)}), f32[32,1,128]{2,1,0:T(1,128)S(1)}, u32[]{:S(2)}, u32[]{:S(2)}) async-start(f32[32,1,128]{2,1,0:T(1,128)} %bitcast.24), calls=%async_computation.2 | async-start | bytes 32768 | tf_op jit(solution)/shard_map/all_to_all | solution.py:782
  109.2 0.0 copy-done.4
  109.2 0.7 select_reduce_fusion.entry_ref
  109.8 0.0 copy-done
  109.8 8.9 %early.1.early_ref = bf16[3,28,168,128]{3,2,1,0:T(8,128)(2,1)} custom-call(s32[2,9]{1,0:T(2,128)} %select_reduce_fusion.entry_ref, bf16[9,28,2,96,128]{4,3,2,1,0:T(8,128)(2,1)} %get-tuple-element.25.x_ref, bf16[9,28,2,96,128]{4,3,2,1,0:T(8,128)(2,1)} %get-tuple-element.26.slope_ref, bf16[576,240]{1,0:T(8,128)(2,1)} %get-tuple-element.27.band, ...), custom_call_target="tpu_custom_call" | custom-call | tf_op jit(solution)/shard_map/early/pallas_call | solution.py:792
  118.7 0.0 all-to-all-done.2
  118.7 0.0 copy-start.2
  118.7 0.6 copy-done.2
  119.3 18.6 %restore.1 = bf16[9,28,168,128]{3,2,1,0:T(8,128)(2,1)} custom-call(s32[2,9]{1,0:T(2,128)} %select_reduce_fusion.entry_ref, s32[1]{0:T(128)} %bitcast.4.z_ref.here_ref, f32[32,128]{1,0:T(8,128)} %bitcast.23, bf16[3,28,168,128]{3,2,1,0:T(8,128)(2,1)} %early.1.early_ref, bf16[9,28,2,96,128]{4,3,2,1,0:T(8,128)(2,1)} %get-tuple-element.25.x_ref, ...), custom_call_target="tpu_custom_call" | custom-call | tf_op jit(solution)/shard_map/restore/pallas_call | solution.py:803
  (3 shorter events, 0.0 us)
Async XLA Ops:
  6.5 37.9 %copy-start.3 = (f32[1280]{0:T(1024)S(1)}, f32[1280]{0:T(1024)}, u32[]{:S(2)}) copy-start(f32[1280]{0:T(1024)} %param.17) | copy-start | bytes 15364
  6.5 73.7 %all-gather.3.cloned.1.call-start = ((), (), s32[]{:S(2)}) async-start(), calls=%async_computation.3 | async-start | bytes 9461760 | tf_op jit(solution)/shard_map/all_gather | solution.py:643
  8.4 100.7 %copy-start.4 = (s32[2,8]{1,0:T(2,128)S(1)}, s32[2,8]{1,0:T(2,128)}, u32[]{:S(2)}) copy-start(s32[2,8]{1,0:T(2,128)} %pick_ref.1) | copy-start | bytes 196
  39.2 17.2 %all-to-all-start = ((bf16[8,2,3,32,128]{4,3,2,1,0:T(8,128)(2,1)}), bf16[8,2,3,32,128]{4,3,2,1,0:T(8,128)(2,1)S(1)}, u32[]{:S(2)}, u32[]{:S(2)}) async-start(bf16[8,2,3,32,128]{4,3,2,1,0:T(8,128)(2,1)} %get-tuple-element.17), calls=%async_computation | async-start | bytes 786432 | tf_op jit(solution)/shard_map/all_to_all | solution.py:723
  56.5 0.8 copy-start.1
  94.7 11.7 %all-to-all-start.1 = ((bf16[8,2,3,32,128]{4,3,2,1,0:T(8,128)(2,1)}), bf16[8,2,3,32,128]{4,3,2,1,0:T(8,128)(2,1)S(1)}, u32[]{:S(2)}, u32[]{:S(2)}) async-start(bf16[8,2,3,32,128]{4,3,2,1,0:T(8,128)(2,1)} %get-tuple-element.23), calls=%async_computation.1 | async-start | bytes 786432 | tf_op jit(solution)/shard_map/all_to_all | solution.py:777
  106.4 3.4 %copy-start = (bf16[8,2,3,32,128]{4,3,2,1,0:T(8,128)(2,1)}, bf16[8,2,3,32,128]{4,3,2,1,0:T(8,128)(2,1)S(1)}, u32[]{:S(2)}) copy-start(bf16[8,2,3,32,128]{4,3,2,1,0:T(8,128)(2,1)S(1)} %all-to-all-done.1.grad_ref) | copy-start | bytes 1179652
  106.4 12.3 %all-to-all-start.2 = ((f32[32,1,128]{2,1,0:T(1,128)}), f32[32,1,128]{2,1,0:T(1,128)S(1)}, u32[]{:S(2)}, u32[]{:S(2)}) async-start(f32[32,1,128]{2,1,0:T(1,128)} %bitcast.24), calls=%async_computation.2 | async-start | bytes 32768 | tf_op jit(solution)/shard_map/all_to_all | solution.py:782
  118.7 0.6 copy-start.2
Sparse Core Ops, SparseCore 0:
  9.0 71.2 all-gather.2

commit v10 on v9

--- a/solution.py
+++ b/solution.py
@@ -22,11 +22,11 @@
 SPANS = CH // 8
 OUT_ROWS = 27 * 16
 BACK = 6
-EARLY = 3
+EARLY = 2
 BACK_ROWS = 3 * 80
 NT = 8
 NZ = 4
-PACK = 1120
+PACK = 1088
 CYCLE = [
     (2 * chip + core, z)
     for chip, heights in ((0, (0, 1, 2, 3)), (1, (3, 2, 1, 0)), (3, (0, 1, 2, 3)), (2, (3, 2, 1, 0)))
@@ -34,7 +34,6 @@
     for core in range(2)
 ]
 PLACES = [[CYCLE.index((i, z)) for z in range(NZ)] for i in range(NT)]
-STARTS = (0, 48, 96, 112)
 KIN = 896
 D = 1280
 NTOK = 128
@@ -402,7 +401,7 @@
     count = samples * NTOK
 
     copies = []
-    for part, (begin, end) in enumerate(((880, 1120), (640, 880), (0, 640))):
+    for part, (begin, end) in enumerate(((880, 1088), (640, 880), (0, 640))):
         copies.append(
             pltpu.make_async_copy(
                 packed_ref.at[:, begin:end, :], pack.at[:, begin:end, :], arrived.at[part]
@@ -415,13 +414,14 @@
     copies[1].wait()
 
     for i in range(NT):
-        for z, (begin, height, target) in enumerate(
-            ((0, 48, 128 * i), (0, 48, 128 * i + 48), (0, 32, 128 * i + 96), (16, 32, 1024 + 32 * i))
-        ):
+        for z in range(NZ):
             source = pack.at[PLACES[i][z]]
-            for part in range(5):
-                at = 880 + 48 * part + begin
-                embed[target : target + height, 128 * part : 128 * part + 128] = source[at : at + height, :]
+            embed[128 * i : 128 * i + 128, 128 * z : 128 * z + 128] = source[880:1008, :]
+            embed[1024 + 32 * i : 1056 + 32 * i, 128 * z : 128 * z + 128] = source[1008:1040, :]
+        last = [pack[PLACES[i][z], 1040:1088, :].astype(F32)[0:40] for z in range(NZ)]
+        last = jnp.concatenate(last, axis=0).astype(BF16)
+        embed[128 * i : 128 * i + 128, 512:640] = last[0:128]
+        embed[1024 + 32 * i : 1056 + 32 * i, 512:640] = last[128:160]
     lane48 = lane_iota(48)
     for h in range(HEADS):
         outw[128 * h + HD : 128 * h + 128, :] = jnp.zeros((128 - HD, D), BF16)
@@ -600,8 +600,6 @@
     other = jnp.concatenate([out_part, place_part], axis=0)
     rest = other[:, 128:160].reshape(4, 48, 32)
     rest = jnp.concatenate([rest[q] for q in range(4)], axis=1)
-    embed_part = jnp.pad(embed_part, ((0, 0), (0, 640 - embed_part.shape[1])))
-    embed_part = embed_part.reshape(48, 5, 128).transpose(1, 0, 2).reshape(240, 128)
     return jnp.concatenate([ordered[:, 0:128], upper, other[:, 0:128], rest, embed_part], axis=0)
 
 
@@ -619,14 +617,14 @@
         [tail[0:48], tail[48:96], tail[96:144], jnp.concatenate([tail[144:160], last], axis=0)],
         axis=1,
     ).astype(BF16)
-    width = embed_ref.shape[1]
-    start = pl.multiple_of(jnp.where(z_ref[0] == NZ - 1, STARTS[-1], 48 * z_ref[0]), 16)
-    for part in range(5):
-        count = min(128, width - 128 * part)
-        value = embed_ref[pl.ds(start, 48), 128 * part : 128 * part + count]
-        if count < 128:
-            value = jnp.concatenate([value, jnp.zeros((48, 128 - count), BF16)], axis=1)
-        packed_ref[880 + 48 * part : 928 + 48 * part, :] = value
+    at = pl.multiple_of(128 * z_ref[0], 128)
+    packed_ref[880:1040, :] = embed_ref[:, pl.ds(at, 128)]
+    width = embed_ref.shape[1] - 512
+    last = jnp.concatenate([embed_ref[:, 512:].astype(F32), jnp.zeros((160, 128 - width), F32)], axis=1)
+    quarter = last[0:40]
+    for z in range(1, NZ):
+        quarter = jnp.where(z_ref[0] == z, last[40 * z : 40 * z + 40], quarter)
+    packed_ref[1040:1088, :] = jnp.concatenate([quarter, jnp.zeros((8, 128), F32)], axis=0).astype(BF16)
 
 
 def packed_weights(patch_embed, position, attend_in, attend_out):
@@ -651,7 +649,21 @@
         for value in (whole(attend_in), whole(attend_out), whole(position))
     ]
     columns = lax.all_gather(patch_embed.T, TILE, axis=0, tiled=True).reshape(NT, D // NT, -1)
-    split.append(jnp.stack([columns[:, start : start + 48] for start in STARTS], axis=1))
+    columns = jnp.pad(columns, ((0, 0), (0, 0), (0, 640 - columns.shape[2])))
+    split.append(
+        jnp.stack(
+            [
+                jnp.pad(
+                    jnp.concatenate(
+                        [columns[:, :, 128 * z : 128 * z + 128], columns[:, 40 * z : 40 * z + 40, 512:]], axis=1
+                    ),
+                    ((0, 0), (0, 8), (0, 0)),
+                )
+                for z in range(NZ)
+            ],
+            axis=1,
+        )
+    )
     packed = jax.vmap(jax.vmap(pack_part))(*split)
     return jnp.stack([packed[i, z] for i, z in CYCLE])
 

time: 145 us -> 143 us (0.986)
  Pallas kernels: 77.7 us -> 75.7 us
    pallas_call x1, Pallas kernels: 8.87 us -> 6.52 us  [local(): pl.pallas_call(early_kernel, grid=(EARLY,), in_specs=[smem, aligned_spec,...]
  transfers between devices with their start and end apart: 4 -> 4, of which waited for: 3 -> 3; matrix products, arithmetic and copies ran while one was open for 1% -> 1% of each run, Pallas kernels for 30% -> 28%
where the time goes in v10:
time: 143 us
  Pallas kernels  75.7 us (53%)
  waiting for transfers between devices  39.2 us (27%)
  between operations  13.5 us (9%)
  starting transfers between devices  11.4 us (8%)
  local copies, waits for them, and re-layouts  2.11 us (1%)
    pallas_call x1, Pallas kernels, local(): pl.pallas_call(functools.partial(decode_kernel, row_block), grid=(frames,...  30.8 us
    all_gather x1, waiting for transfers between devices, packed_weights(): lax.all_gather(mine, TILE + ('sample',), axis=0, axis_index_groups=[group])  19.7 us
    pallas_call x1, Pallas kernels, local(): pl.pallas_call(functools.partial(restore_kernel, parts), grid=(frames,),...  19.1 us
    pallas_call x1, Pallas kernels, local(): pl.pallas_call(functools.partial(reward_kernel, row_count, tiles, samples...  14.4 us
    all_to_all x1, waiting for transfers between devices, local(): lax.all_to_all(decoded, TILE, split_axis=0, concat_axis=0, tiled=True)  11.2 us
    all_to_all x1, waiting for transfers between devices, local(): lax.all_to_all(grads, TILE, split_axis=0, concat_axis=0, tiled=True)  8.27 us
    pallas_call x1, Pallas kernels, local(): pl.pallas_call(early_kernel, grid=(EARLY,), in_specs=[smem, aligned_spec,...  6.52 us
    all_to_all x1, starting transfers between devices, local(): lax.all_to_all(decoded, TILE, split_axis=0, concat_axis=0, tiled=True)  5.17 us
  transfers between devices with their start and end apart: 4, of which 3 were waited for; matrix products, arithmetic and copies ran while one was open for 1% of the time, Pallas kernels for 28%

profile of v10, /device:TPU:0, one launch (start us, length us, event | category | flops | bytes accessed | tf_op | source)
XLA Modules:
  0.0 142.5 jit_solution(6134025588923108799)
XLA Ops:
  6.5 0.0 copy-start.3
  6.5 0.0 all-gather.3.cloned.1.call-start
  6.5 1.9 %pack.1 = bf16[1088,128]{1,0:T(8,128)(2,1)} custom-call(s32[1]{0:T(128)} %bitcast.4.z_ref.here_ref, bf16[320,240]{1,0:T(8,128)(2,1)} %rows_ref.1, bf16[160,160]{1,0:T(8,128)(2,1)} %out_ref.1, bf16[32,160]{1,0:T(8,128)(2,1)} %place_ref.1, bf16[160,588]{1,0:T(8,128)(2,1)} %bitcast.22), custom_call_target="tpu_custom_call" | custom-call | tf_op jit(solution)/shard_map/pack/pallas_call | solution.py:633
  8.4 0.0 all-gather.3.cloned.1.call-update
  8.4 0.0 copy-start.4
  8.4 30.8 %decode.1 = (bf16[8,2,3,32,128]{4,3,2,1,0:T(8,128)(2,1)}, bf16[9,28,2,96,128]{4,3,2,1,0:T(8,128)(2,1)}, bf16[9,28,2,96,128]{4,3,2,1,0:T(8,128)(2,1)}, bf16[576,240]{1,0:T(8,128)(2,1)}) custom-call(s32[2,8]{1,0:T(2,128)} %pick_ref.1, bf16[9,28,168,128]{3,2,1,0:T(8,128)(2,1)} %bitcast.20, f32[1,96]{1,0:T(1,128)} %bitcast.25, bf16[3,3,3,3,96]{4,3,2,1,0:T(4,128)(2,1)} %weight_ref.1), custom_call_target="tpu_custom_call" | custom-call | tf_op jit(solution)/shard_map/decode/pallas_call | solution.py:709
  39.2 5.2 %all-to-all-start = ((bf16[8,2,3,32,128]{4,3,2,1,0:T(8,128)(2,1)}), bf16[8,2,3,32,128]{4,3,2,1,0:T(8,128)(2,1)S(1)}, u32[]{:S(2)}, u32[]{:S(2)}) async-start(bf16[8,2,3,32,128]{4,3,2,1,0:T(8,128)(2,1)} %get-tuple-element.17), calls=%async_computation | async-start | bytes 786432 | tf_op jit(solution)/shard_map/all_to_all | solution.py:735
  44.4 0.0 copy-done.3
  44.4 0.1 reshape.31
  44.5 0.1 reshape.33
  44.6 0.6 broadcast_in_dim.22.head_ref
  45.2 11.2 %all-to-all-done.part_ref = bf16[8,2,3,32,128]{4,3,2,1,0:T(8,128)(2,1)S(1)} async-done(((bf16[8,2,3,32,128]{4,3,2,1,0:T(8,128)(2,1)}), bf16[8,2,3,32,128]{4,3,2,1,0:T(8,128)(2,1)S(1)}, u32[]{:S(2)}, u32[]{:S(2)}) %all-to-all-start) | async-done | bytes 393248 | tf_op jit(solution)/shard_map/all_to_all | solution.py:735
  56.4 0.0 copy-start.1
  56.4 0.7 copy-done.1
  57.1 3.1 %patches.1 = (bf16[256,640]{1,0:T(8,128)(2,1)}, bf16[896,640]{1,0:T(8,128)(2,1)}) custom-call(bf16[8,2,3,32,128]{4,3,2,1,0:T(8,128)(2,1)} %copy-done.1), custom_call_target="tpu_custom_call" | custom-call | tf_op jit(solution)/shard_map/patches/pallas_call | solution.py:743
  60.3 19.7 %all-gather.3.cloned.1.call-done = bf16[34816,128]{1,0:T(8,128)(2,1)} async-done(((bf16[1088,128]{1,0:T(8,128)(2,1)}), bf16[34816,128]{1,0:T(8,128)(2,1)}) %all-gather.3.cloned.1.call-update) | async-done | bytes 8912912 | tf_op jit(solution)/shard_map/all_gather | solution.py:641
  79.9 14.4 %reward.1 = (bf16[8,2,3,32,128]{4,3,2,1,0:T(8,128)(2,1)}, f32[32,128]{1,0:T(8,128)}) custom-call(s32[2]{0:T(128)} %group_ref.1, bf16[256,640]{1,0:T(8,128)(2,1)} %get-tuple-element.18.inputs_ref, bf16[896,640]{1,0:T(8,128)(2,1)} %get-tuple-element.19.order, bf16[32,1088,128]{2,1,0:T(8,128)(2,1)} %bitcast.21, f32[1,1280]{1,0:T(1,128)} %broadcast_in_dim.22.head_ref), custom_call_target="tpu_custom_call" | custom-call | tf_op jit(solution)/shard_map/reward/pallas_call | solution.py:750
  94.3 3.5 %all-to-all-start.1 = ((bf16[8,2,3,32,128]{4,3,2,1,0:T(8,128)(2,1)}), bf16[8,2,3,32,128]{4,3,2,1,0:T(8,128)(2,1)S(1)}, u32[]{:S(2)}, u32[]{:S(2)}) async-start(bf16[8,2,3,32,128]{4,3,2,1,0:T(8,128)(2,1)} %get-tuple-element.23), calls=%async_computation.1 | async-start | bytes 786432 | tf_op jit(solution)/shard_map/all_to_all | solution.py:789
  97.8 8.3 %all-to-all-done.1.grad_ref = bf16[8,2,3,32,128]{4,3,2,1,0:T(8,128)(2,1)S(1)} async-done(((bf16[8,2,3,32,128]{4,3,2,1,0:T(8,128)(2,1)}), bf16[8,2,3,32,128]{4,3,2,1,0:T(8,128)(2,1)S(1)}, u32[]{:S(2)}, u32[]{:S(2)}) %all-to-all-start.1) | async-done | bytes 393248 | tf_op jit(solution)/shard_map/all_to_all | solution.py:789
  106.0 0.0 copy-start
  106.0 2.7 %all-to-all-start.2 = ((f32[32,1,128]{2,1,0:T(1,128)}), f32[32,1,128]{2,1,0:T(1,128)S(1)}, u32[]{:S(2)}, u32[]{:S(2)}) async-start(f32[32,1,128]{2,1,0:T(1,128)} %bitcast.24), calls=%async_computation.2 | async-start | bytes 32768 | tf_op jit(solution)/shard_map/all_to_all | solution.py:794
  108.8 0.0 copy-done.4
  108.8 0.7 select_reduce_fusion.entry_ref
  109.5 0.0 copy-done
  109.5 6.5 %early.1.early_ref = bf16[2,28,168,128]{3,2,1,0:T(8,128)(2,1)} custom-call(s32[2,9]{1,0:T(2,128)} %select_reduce_fusion.entry_ref, bf16[9,28,2,96,128]{4,3,2,1,0:T(8,128)(2,1)} %get-tuple-element.25.x_ref, bf16[9,28,2,96,128]{4,3,2,1,0:T(8,128)(2,1)} %get-tuple-element.26.slope_ref, bf16[576,240]{1,0:T(8,128)(2,1)} %get-tuple-element.27.band, ...), custom_call_target="tpu_custom_call" | custom-call | tf_op jit(solution)/shard_map/early/pallas_call | solution.py:804
  116.0 0.0 all-to-all-done.2
  116.0 0.0 copy-start.2
  116.0 0.6 copy-done.2
  116.6 19.1 %restore.1 = bf16[9,28,168,128]{3,2,1,0:T(8,128)(2,1)} custom-call(s32[2,9]{1,0:T(2,128)} %select_reduce_fusion.entry_ref, s32[1]{0:T(128)} %bitcast.4.z_ref.here_ref, f32[32,128]{1,0:T(8,128)} %bitcast.23, bf16[2,28,168,128]{3,2,1,0:T(8,128)(2,1)} %early.1.early_ref, bf16[9,28,2,96,128]{4,3,2,1,0:T(8,128)(2,1)} %get-tuple-element.25.x_ref, ...), custom_call_target="tpu_custom_call" | custom-call | tf_op jit(solution)/shard_map/restore/pallas_call | solution.py:815
  (3 shorter events, 0.0 us)
Async XLA Ops:
  6.5 37.9 %copy-start.3 = (f32[1280]{0:T(1024)S(1)}, f32[1280]{0:T(1024)}, u32[]{:S(2)}) copy-start(f32[1280]{0:T(1024)} %param.17) | copy-start | bytes 15364
  6.5 73.4 %all-gather.3.cloned.1.call-start = ((), (), s32[]{:S(2)}) async-start(), calls=%async_computation.3 | async-start | bytes 9191424 | tf_op jit(solution)/shard_map/all_gather | solution.py:641
  8.4 100.4 %copy-start.4 = (s32[2,8]{1,0:T(2,128)S(1)}, s32[2,8]{1,0:T(2,128)}, u32[]{:S(2)}) copy-start(s32[2,8]{1,0:T(2,128)} %pick_ref.1) | copy-start | bytes 196
  39.2 17.2 %all-to-all-start = ((bf16[8,2,3,32,128]{4,3,2,1,0:T(8,128)(2,1)}), bf16[8,2,3,32,128]{4,3,2,1,0:T(8,128)(2,1)S(1)}, u32[]{:S(2)}, u32[]{:S(2)}) async-start(bf16[8,2,3,32,128]{4,3,2,1,0:T(8,128)(2,1)} %get-tuple-element.17), calls=%async_computation | async-start | bytes 786432 | tf_op jit(solution)/shard_map/all_to_all | solution.py:735
  56.4 0.7 copy-start.1
  94.3 11.7 %all-to-all-start.1 = ((bf16[8,2,3,32,128]{4,3,2,1,0:T(8,128)(2,1)}), bf16[8,2,3,32,128]{4,3,2,1,0:T(8,128)(2,1)S(1)}, u32[]{:S(2)}, u32[]{:S(2)}) async-start(bf16[8,2,3,32,128]{4,3,2,1,0:T(8,128)(2,1)} %get-tuple-element.23), calls=%async_computation.1 | async-start | bytes 786432 | tf_op jit(solution)/shard_map/all_to_all | solution.py:789
  106.0 3.4 %copy-start = (bf16[8,2,3,32,128]{4,3,2,1,0:T(8,128)(2,1)}, bf16[8,2,3,32,128]{4,3,2,1,0:T(8,128)(2,1)S(1)}, u32[]{:S(2)}) copy-start(bf16[8,2,3,32,128]{4,3,2,1,0:T(8,128)(2,1)S(1)} %all-to-all-done.1.grad_ref) | copy-start | bytes 1179652
  106.0 9.9 %all-to-all-start.2 = ((f32[32,1,128]{2,1,0:T(1,128)}), f32[32,1,128]{2,1,0:T(1,128)S(1)}, u32[]{:S(2)}, u32[]{:S(2)}) async-start(f32[32,1,128]{2,1,0:T(1,128)} %bitcast.24), calls=%async_computation.2 | async-start | bytes 32768 | tf_op jit(solution)/shard_map/all_to_all | solution.py:794
  116.0 0.6 copy-start.2
Sparse Core Ops, SparseCore 0:
  9.0 70.9 all-gather.2
